TPU v7x, 128 devices: a whole 4x4x4 slice. The times are simulated.
128 devices in a mesh: dp: 16 (over x_hi, y, core), expert: 8 (over z, x_lo).
Axes of the slice: x: 4 (x_hi: 2, x_lo: 2; x = x_hi * 2 + x_lo), y: 4, z: 4, core: 2. Of those that a mesh axis runs over, the one named last changes fastest.
Arguments:
- expert_partials: float32 [16, 8, 1536, 2048], P('dp', 'expert'), may hold values from -5 to 5
- key_partials: float32 [16, 512, 4096], P('dp', None, 'expert'), may hold values from -5 to 5
- expert_param: float32 [8, 1536, 2048], P('expert', 'dp'), may hold values from -0.3125 to 0.3125
- expert_moment: float32 [8, 1536, 2048], P('expert', 'dp'), may hold values from -4 to 4
- expert_second: float32 [8, 1536, 2048], P('expert', 'dp'), may hold values from 0.05 to 1
- key_param: float32 [512, 4096], P('dp', 'expert'), may hold values from -0.3125 to 0.3125
- key_moment: float32 [512, 4096], P('dp', 'expert'), may hold values from -4 to 4
- key_second: float32 [512, 4096], P('dp', 'expert'), may hold values from 0.05 to 1
- expert_scales: float32 [8, 12, 16], replicated, may hold values from 0.0001 to 0.001
- key_scales: float32 [4, 32], P(None, 'expert'), may hold values from 0.0001 to 0.001
- rotary_order: int32 [128], replicated, may hold values from 0 to 127, each once
- expert_slot: int32 [8], replicated, may hold values from 0 to 7, each once
Outputs:
- new_expert_param: float32 [8, 1536, 2048], P('expert', 'dp')
- new_expert_moment: float32 [8, 1536, 2048], P('expert', 'dp')
- new_expert_second: float32 [8, 1536, 2048], P('expert', 'dp')
- new_key_param: float32 [512, 4096], P('dp', 'expert')
- new_key_moment: float32 [512, 4096], P('dp', 'expert')
- new_key_second: float32 [512, 4096], P('dp', 'expert')
- server_expert: bfloat16 [8, 2048, 1536], P(None, 'expert', 'dp')
- server_key: bfloat16 [4096, 512], P('expert')
Inputs may be any that keep to these rules, and one draw needn't show every extreme that they name: `rotary_order`: a permutation of the rows of one head. `expert_slot`: a permutation of the experts.
All inputs are finite; a program needn't handle non-finite values.
Results may differ from a plain program's by a relative error of at most 0.007.
Values may be sent and summed in bfloat16 or wider, within the bound.
No kernel may reach another device: no remote copies, remote signals or barrier semaphores. Data moves between devices by JAX's collectives and lax.ppermute only.
A program may use at most 128 MiB of HBM per device.

v0:
```python
import jax
import jax.numpy as jnp
from jax import lax
from jax.sharding import PartitionSpec as P

HD = 128
BLOCK = 128


BETA_ONE = 0.9
BETA_TWO = 0.95
LEARN = 0.01
DECAY = 0.1
EPSILON = 1e-08
LIMIT = 448.0
CORRECT_ONE = 1.0 - 0.9**10
CORRECT_TWO = 1.0 - 0.95**10


def adam_update(param, moment, second, grad):
    moment = BETA_ONE * moment + (1.0 - BETA_ONE) * grad
    second = BETA_TWO * second + (1.0 - BETA_TWO) * grad * grad
    corrected = moment / CORRECT_ONE / (jnp.sqrt(second / CORRECT_TWO) + EPSILON)
    return (param * (1.0 - LEARN * DECAY) - LEARN * corrected, moment, second)


def to_grid(weights, scales):
    return jnp.clip(weights / scales, -LIMIT, LIMIT).astype(jnp.bfloat16)


def on_device(
    expert_partials,
    key_partials,
    expert_param,
    expert_moment,
    expert_second,
    key_param,
    key_moment,
    key_second,
    expert_scales,
    key_scales,
    rotary_order,
    expert_slot,
):
    dp_index = lax.axis_index("dp")
    expert_index = lax.axis_index("expert")
    expert_grad, key_grad = (
        lax.psum_scatter(
            expert_partials.astype(jnp.bfloat16), "dp", scatter_dimension=2, tiled=True
        ).astype(jnp.float32),
        lax.psum_scatter(
            key_partials.astype(jnp.bfloat16), "dp", scatter_dimension=1, tiled=True
        ).astype(jnp.float32),
    )
    new_ep, new_em, new_es = adam_update(expert_param, expert_moment, expert_second, expert_grad[0])
    local_experts, row_count, width = new_ep.shape
    row_blocks = (dp_index * row_count + jnp.arange(row_count, dtype=jnp.int32)) // BLOCK
    row_scales = jnp.take(expert_scales, row_blocks, axis=1)
    arrived = lax.all_to_all(new_ep, "expert", split_axis=2, concat_axis=0, tiled=True)
    columns = arrived.shape[2]
    column_scales = lax.dynamic_slice_in_dim(
        row_scales, expert_index * (columns // BLOCK), columns // BLOCK, 2
    )
    grid_blocks = to_grid(arrived, jnp.repeat(column_scales, BLOCK, axis=2))
    transposed = jnp.transpose(grid_blocks, (0, 2, 1))
    server_expert = jnp.zeros_like(transposed).at[expert_slot].set(transposed)
    new_kp, new_km, new_ks = adam_update(key_param, key_moment, key_second, key_grad[0])
    column_full = jnp.repeat(key_scales, BLOCK, axis=1)
    gathered = lax.all_gather(new_kp, "dp", axis=0, tiled=True)
    key_grid = to_grid(gathered, jnp.repeat(column_full, BLOCK, axis=0))
    total_rows = key_grid.shape[0]
    all_rows = jnp.arange(total_rows, dtype=jnp.int32)
    source = all_rows // HD * HD + rotary_order[all_rows % HD]
    server_key = jnp.take(key_grid, source, axis=0).T
    return (new_ep, new_em, new_es, new_kp, new_km, new_ks, server_expert, server_key)


def solution(mesh):
    return jax.shard_map(
        on_device,
        mesh=mesh,
        in_specs=(
            P("dp", "expert", None, None),
            P("dp", None, "expert"),
            P("expert", "dp", None),
            P("expert", "dp", None),
            P("expert", "dp", None),
            P("dp", "expert"),
            P("dp", "expert"),
            P("dp", "expert"),
            P(),
            P(None, "expert"),
            P(),
            P(),
        ),
        out_specs=(
            P("expert", "dp", None),
            P("expert", "dp", None),
            P("expert", "dp", None),
            P("dp", "expert"),
            P("dp", "expert"),
            P("dp", "expert"),
            P(None, "expert", "dp"),
            P("expert", None),
        ),
        check_vma=False,
    )
```

profile of v0, /device:TPU:1, one launch (start us, length us, event | category | flops | bytes accessed | tf_op | source)
XLA Modules:
  0.0 242.4 jit_solution(14212794293018167684)
XLA Ops:
  7.2 0.0 copy-start
  7.2 0.0 reduce-scatter.5.cloned.1.call-start
  7.2 2.1 convert_element_type.15
  9.3 0.0 reduce-scatter.5.cloned.1.call-update
  9.3 0.0 reduce-scatter.7.cloned.1.call-start
  9.4 10.0 %copy.41 = bf16[1,1,1536,2048]{2,3,1,0:T(8,128)(2,1)} copy(f32[1,1,1536,2048]{3,2,1,0:T(8,128)} %param.12) | data formatting | bytes 18874368 | tf_op args[0]
  19.4 30.4 %copy.50 = bf16[1,1,1536,2048]{3,1,0,2:T(2,128)(2,1)} copy(bf16[1,1,1536,2048]{2,3,1,0:T(8,128)(2,1)} %copy.41) | data formatting | bytes 12582912
  49.8 0.0 copy-start.4
  49.8 11.3 %copy.56 = bf16[1536,1,1,2048]{3,0,1,2:T(8,128)(2,1)} copy(bf16[1536,1,1,2048]{3,2,1,0:T(2,128)(2,1)} %bitcast.53) | data formatting | bytes 12582912
  61.1 0.0 reduce-scatter.7.cloned.1.call-update
  61.1 0.0 copy-start.9
  61.1 0.0 all-gather.2.cloned.1.call-start
  61.2 0.0 copy-done
  61.2 0.7 gather_fusion
  62.0 0.3 fusion.6
  62.2 16.8 %reduce-scatter.5.cloned.1.call-done = bf16[1,32,512]{2,1,0:T(8,128)(2,1)} async-done(((bf16[1,512,512]{2,1,0:T(8,128)(2,1)}), bf16[1,32,512]{2,1,0:T(8,128)(2,1)}) %reduce-scatter.5.cloned.1.call-update) | async-done | bytes 32784 | tf_op jit(solution)/shard_map/reduce_scatter | solution.py:51
  79.0 0.0 copy-done.5
  79.0 0.0 copy-done.6
  79.0 1.5 multiply_subtract_fusion.1
  80.5 0.0 all-gather.2.cloned.1.call-update
  80.5 0.1 broadcast_bitcast_fusion
  80.6 0.1 copy.45
  80.7 1.0 broadcast_in_dim.40
  81.6 1.5 reshape.212
  83.2 0.0 copy-done.4
  83.2 0.3 copy.39
  83.5 1.5 copy.40
  85.0 2.5 %copy.42 = f32[1,96,2048]{1,2,0:T(8,128)} copy(f32[1,96,2048]{2,1,0:T(8,128)} %param.16) | data formatting | bytes 1572864 | tf_op args[4]
  87.5 3.3 %gather_fusion.1 = s32[512]{0:T(512)S(1)} fusion(s32[128]{0:T(128)S(1)} %copy-done.1, s32[1024]{0:T(1024)S(1)} %pad_clamp_fusion.1), kind=kCustom, calls=%fused_computation.1 | custom fusion | bytes 6144 | tf_op jit(solution)/shard_map/gather | solution.py:73
  90.9 82.3 %reduce-scatter.7.cloned.1.call-done = bf16[96,2048]{1,0:T(8,128)(2,1)} async-done(((bf16[1536,2048]{1,0:T(8,128)(2,1)}), bf16[96,2048]{1,0:T(8,128)(2,1)}) %reduce-scatter.7.cloned.1.call-update) | async-done | bytes 393232
  173.1 1.5 reshape_bitcast_fusion
  174.6 1.8 copy.51
  176.4 3.5 %multiply_subtract_fusion = (f32[1,96,2048]{1,2,0:T(8,128)}, f32[1,96,2048]{1,2,0:T(8,128)}, f32[1,96,2048]{1,2,0:T(8,128)S(1)}) fusion(f32[1,96,2048]{1,2,0:T(8,128)S(1)} %copy.39, bf16[1,1,96,2048]{2,3,1,0:T(8,128)(2,1)} %copy.51, f32[1,96,2048]{1,2,0:T(8,128)S(1)} %copy.40, f32[1,96,2048]{1,2,0:T(8,128)} %copy.42), kind=kLoop, calls=%fused_computation.13 | loop fusion | flops 2949120 | bytes 5111808 | tf_op jit(solution)/shard_map/sub | solution.py:24
  179.9 4.3 %all-to-all-start = ((f32[1,96,2048]{1,0,2:T(1,128)}), f32[1,96,2048]{1,0,2:T(1,128)S(1)}, u32[]{:S(2)}, u32[]{:S(2)}) async-start(f32[1,96,2048]{1,0,2:T(1,128)} %bitcast.7), calls=%async_computation.1 | async-start | bytes 2097152 | tf_op jit(solution)/shard_map/all_to_all | solution.py:59
  184.2 37.2 %all-gather.2.cloned.1.call-done = f32[512,512]{1,0:T(8,128)} async-done(((f32[32,512]{1,0:T(8,128)}), f32[512,512]{1,0:T(8,128)}) %all-gather.2.cloned.1.call-update) | async-done | bytes 1048592 | tf_op jit(solution)/shard_map/all_gather | solution.py:69
  221.5 1.3 fusion.3
  222.8 2.6 %gather_fusion.2 = bf16[512,512]{1,0:T(8,128)(2,1)} fusion(bf16[512,512]{1,0:T(8,128)(2,1)S(1)} %fusion.3, s32[1024]{0:T(1024)S(1)} %pad_clamp_fusion), kind=kCustom, calls=%fused_computation.2 | custom fusion | bytes 1050624 | tf_op jit(solution)/shard_map/jit(_take)/gather | solution.py:74
  225.4 1.2 select_bitcast_fusion
  226.6 1.0 copy.49
  227.6 2.4 %copy.46 = f32[1,96,2048]{2,1,0:T(8,128)} copy(f32[1,96,2048]{1,2,0:T(8,128)} %get-tuple-element.43) | data formatting | bytes 1572864
  230.0 2.4 %copy.47 = f32[1,96,2048]{2,1,0:T(8,128)} copy(f32[1,96,2048]{1,2,0:T(8,128)} %get-tuple-element.44) | data formatting | bytes 1572864
  232.5 1.2 copy.48
  233.7 0.0 all-to-all-done
  233.7 0.3 copy.44
  234.0 0.1 fusion.7
  234.2 0.9 scatter_fusion
  235.1 0.0 copy-start.3
  235.1 0.7 copy-done.3
  (22 shorter events, 0.1 us)
Async XLA Ops:
  7.2 54.1 %copy-start = (f32[8,12,16]{2,0,1:T(8,128)S(1)}, f32[8,12,16]{2,0,1:T(8,128)}, u32[]{:S(2)}) copy-start(f32[8,12,16]{2,0,1:T(8,128)} %param.20) | copy-start | bytes 18436
  7.2 71.8 %reduce-scatter.5.cloned.1.call-start = ((), (), s32[]{:S(2)}) async-start(), calls=%async_computation.3 | async-start | bytes 557056 | tf_op jit(solution)/shard_map/reduce_scatter | solution.py:51
  9.3 163.8 %reduce-scatter.7.cloned.1.call-start = ((), (), s32[]{:S(2)}) async-start(), calls=%async_computation.5 | async-start | bytes 6684672
  49.8 29.2 %copy-start.5 = (f32[32,512]{1,0:T(8,128)S(1)}, f32[32,512]{1,0:T(8,128)}, u32[]{:S(2)}) copy-start(f32[32,512]{1,0:T(8,128)} %param.17) | copy-start | bytes 196612
  49.8 29.2 %copy-start.6 = (f32[32,512]{1,0:T(8,128)S(1)}, f32[32,512]{1,0:T(8,128)}, u32[]{:S(2)}) copy-start(f32[32,512]{1,0:T(8,128)} %param.18) | copy-start | bytes 196612
  49.8 29.2 %copy-start.7 = (f32[32,512]{1,0:T(8,128)S(1)}, f32[32,512]{1,0:T(8,128)}, u32[]{:S(2)}) copy-start(f32[32,512]{1,0:T(8,128)} %param.19) | copy-start | bytes 196612
  49.8 30.7 %copy-start.8 = (f32[4,4]{1,0:T(4,128)S(1)}, f32[4,4]{1,0:T(4,128)}, u32[]{:S(2)}) copy-start(f32[4,4]{1,0:T(4,128)} %param.21) | copy-start | bytes 196
  49.8 33.4 %copy-start.4 = (f32[1,96,2048]{2,1,0:T(8,128)S(1)}, f32[1,96,2048]{2,1,0:T(8,128)}, u32[]{:S(2)}) copy-start(f32[1,96,2048]{2,1,0:T(8,128)} %param.14) | copy-start | bytes 2359300
  61.1 26.4 %copy-start.1 = (s32[128]{0:T(128)S(1)}, s32[128]{0:T(128)}, u32[]{:S(2)}) copy-start(s32[128]{0:T(128)} %param.22) | copy-start | bytes 1540
  61.1 123.1 %copy-start.9 = (s32[8]{0:T(128)S(1)}, s32[8]{0:T(128)}, u32[]{:S(2)}) copy-start(s32[8]{0:T(128)} %param.23) | copy-start | bytes 100
  61.1 160.3 %all-gather.2.cloned.1.call-start = ((), (), s32[]{:S(2)}) async-start(), calls=%async_computation.4 | async-start | bytes 1114112 | tf_op jit(solution)/shard_map/all_gather | solution.py:69
  179.9 54.1 %copy-start.2 = (f32[8,96,256]{2,1,0:T(8,128)S(1)}, f32[8,96,256]{2,1,0:T(8,128)}, u32[]{:S(2)}) copy-start(f32[8,96,256]{2,1,0:T(8,128)} %reshape.212) | copy-start | bytes 2359300
  179.9 53.8 %all-to-all-start = ((f32[1,96,2048]{1,0,2:T(1,128)}), f32[1,96,2048]{1,0,2:T(1,128)S(1)}, u32[]{:S(2)}, u32[]{:S(2)}) async-start(f32[1,96,2048]{1,0,2:T(1,128)} %bitcast.7), calls=%async_computation.1 | async-start | bytes 2097152 | tf_op jit(solution)/shard_map/all_to_all | solution.py:59
  235.1 0.7 copy-start.3
Sparse Core Ops, SparseCore 0:
  12.3 66.6 reduce-scatter.4
  83.8 89.3 reduce-scatter.6
  176.2 45.2 all-gather.1
where the time goes:
time: 244 us; the launch traced here: 242 us
  waiting for transfers between devices  136 us (56%)
  local copies, waits for them, and re-layouts  77.7 us (32%)
  between operations  14 us (6%)
  other arithmetic  10 us (4%)
  starting transfers between devices  4.41 us (2%)
    unnamed x4, waiting for transfers between devices  82.3 us
    unnamed x34, local copies, waits for them, and re-layouts  67.1 us
    all_gather x1, waiting for transfers between devices, on_device(): gathered = lax.all_gather(new_kp, 'dp', axis=0, tiled=True)  37.2 us
    reduce_scatter x1, waiting for transfers between devices, on_device(): lax.psum_scatter(key_partials.astype(jnp.bfloat16), 'dp', scatter_dimensi...  16.8 us
    sub x2, other arithmetic, adam_update(): return (param * (1.0 - LEARN * DECAY) - LEARN * corrected, moment, second)  4.93 us
  transfers between devices with their start and end apart: 4, of which 3 were waited for; matrix products, arithmetic and copies ran while one was open for 34% of the time, Pallas kernels for 0%

commit v1 on v0

v1 whole, which is shorter than its diff:
```python
import functools

import jax
import jax.numpy as jnp
from jax import lax
from jax.experimental import pallas as pl
from jax.experimental.pallas import tpu as pltpu
from jax.sharding import PartitionSpec as P

HD = 128
BLOCK = 128

BETA_ONE = 0.9
BETA_TWO = 0.95
LEARN = 0.01
DECAY = 0.1
EPSILON = 1e-08
LIMIT = 448.0
CORRECT_ONE = 1.0 - 0.9**10
CORRECT_TWO = 1.0 - 0.95**10

ROWS = 96
KROWS = 32
HALF = 1024
KCOLS = 512
PROWS = 112

BF = jnp.bfloat16
F32 = jnp.float32
VMEM_BYTES = 40 * 1024 * 1024


def dp_of(x, y, c):
    return ((x % 2) * 4 + (y % 4)) * 2 + c % 2


def dp_perm(dx, dy, dc):
    return [
        (dp_of(x, y, c), dp_of(x + dx, y + dy, c + dc))
        for x in range(2)
        for y in range(4)
        for c in range(2)
    ]


def send(value, dx, dy, dc):
    return lax.ppermute(value, "dp", dp_perm(dx, dy, dc))


def adam_update(param, moment, second, grad):
    moment = BETA_ONE * moment + (1.0 - BETA_ONE) * grad
    second = BETA_TWO * second + (1.0 - BETA_TWO) * grad * grad
    corrected = moment / CORRECT_ONE / (jnp.sqrt(second / CORRECT_TWO) + EPSILON)
    return (param * (1.0 - LEARN * DECAY) - LEARN * corrected, moment, second)


def to_grid(weights, scales):
    return jnp.clip(weights / scales, -LIMIT, LIMIT).astype(BF)


def stage_kernel(pieces, received_at, written_at, n_received, ids, ep, kp, *refs):
    received = refs[:n_received]
    n_out = 1 + max(place[0] for place in written_at)
    outs = refs[n_received : n_received + n_out]
    ebuf, kbuf, esem, ksem = refs[n_received + n_out :]
    copies = []
    kslot = 0
    for slot, (kind, _, _) in enumerate(pieces):
        half = 0 if kind == "P" else 1
        block = ids[slot]
        one = pltpu.make_async_copy(
            ep.at[block, :, pl.ds(half * HALF, HALF)], ebuf.at[slot], esem.at[slot]
        )
        one.start()
        two = None
        if kind == "P":
            two = pltpu.make_async_copy(kp.at[block], kbuf.at[kslot], ksem.at[kslot])
            two.start()
        copies.append((one, two, kslot))
        kslot += kind == "P"
    for slot, (kind, _, _) in enumerate(pieces):
        one, two, kslot = copies[slot]
        out, place = outs[written_at[slot][0]], written_at[slot][1]
        one.wait()
        value = ebuf[slot]
        if n_received:
            group, index = received_at[slot]
            value = value + received[group][index, 0:ROWS].astype(F32)
        out[place, 0:ROWS] = value.astype(BF)
        if two is not None:
            two.wait()
            for part in range(2):
                value = kbuf[kslot, part * 16 : part * 16 + 16]
                if n_received:
                    value = value + received[group][
                        index, ROWS:PROWS, part * KCOLS : (part + 1) * KCOLS
                    ].astype(F32)
                out[place, ROWS:PROWS, part * KCOLS : (part + 1) * KCOLS] = value.astype(BF)


def stage(ids, ep, kp, groups, received=(), received_at=None):
    pieces, written_at, shapes = [], [], []
    for number, group in enumerate(groups):
        for place, piece in enumerate(group):
            pieces.append(piece)
            written_at.append((number, place))
        rows = PROWS if group[0][0] == "P" else ROWS
        shapes.append(pltpu.VMEM((len(group), rows, HALF), BF))
    n_key = max(1, sum(piece[0] == "P" for piece in pieces))
    x, y, c = ids
    blocks = jnp.stack([dp_of(x + dx, y + dy, c) for _, dx, dy in pieces]).astype(jnp.int32)
    vmem = pl.BlockSpec(memory_space=pltpu.VMEM)
    hbm = pl.BlockSpec(memory_space=pl.ANY)
    return pl.pallas_call(
        functools.partial(stage_kernel, pieces, received_at, written_at, len(received)),
        out_shape=shapes,
        in_specs=[pl.BlockSpec(memory_space=pltpu.SMEM), hbm, hbm] + [vmem] * len(received),
        out_specs=[vmem] * len(shapes),
        scratch_shapes=[
            pltpu.VMEM((len(pieces), ROWS, HALF), F32),
            pltpu.VMEM((n_key, KROWS, KCOLS), F32),
            pltpu.SemaphoreType.DMA((len(pieces),)),
            pltpu.SemaphoreType.DMA((n_key,)),
        ],
        compiler_params=pltpu.CompilerParams(vmem_limit_bytes=VMEM_BYTES),
        cost_estimate=pl.CostEstimate(
            flops=len(pieces) * ROWS * HALF,
            bytes_accessed=len(pieces) * ROWS * HALF * 6,
            transcendentals=0,
        ),
    )(blocks, ep, kp, *received)


def plus(*values):
    total = values[0].astype(F32)
    for value in values[1:]:
        total = total + value.astype(F32)
    return total


def turn_kernel(slot, arrived, out):
    del slot
    out[0] = arrived[0].T


def turned(arrived, expert_slot):
    experts, rows, columns = arrived.shape
    return pl.pallas_call(
        turn_kernel,
        out_shape=jax.ShapeDtypeStruct((experts, columns, rows), BF),
        grid_spec=pltpu.PrefetchScalarGridSpec(
            num_scalar_prefetch=1,
            grid=(experts,),
            in_specs=[pl.BlockSpec((1, rows, columns), lambda e, slot: (e, 0, 0))],
            out_specs=pl.BlockSpec((1, columns, rows), lambda e, slot: (slot[e], 0, 0)),
        ),
    )(expert_slot, arrived)


def on_device(
    expert_partials,
    key_partials,
    expert_param,
    expert_moment,
    expert_second,
    key_param,
    key_moment,
    key_second,
    expert_scales,
    key_scales,
    rotary_order,
    expert_slot,
):
    dp_index = lax.axis_index("dp")
    expert_index = lax.axis_index("expert")
    x, y, c = dp_index // 8, dp_index // 2 % 4, dp_index % 2
    ep = expert_partials.reshape(16, ROWS, 2 * HALF)
    kp = key_partials.reshape(16, KROWS, KCOLS)
    mine, other = (x, y, c), (x, y, c + 1)

    group_a = [("P", 0, 2), ("P", 1, 2)]
    group_b = [("Q", 1, 2), ("Q", 1, 1), ("Q", 1, 3), ("Q", 1, 0)]
    group_c = [("P", 0, 1), ("P", 1, 1), ("P", 0, 3), ("P", 1, 3)]
    group_d = [("P", 0, 0), ("P", 1, 0)]
    group_e = [("Q", 0, 2), ("Q", 0, 1), ("Q", 0, 3), ("Q", 0, 0)]
    cast_a, cast_b = stage(other, ep, kp, [group_a, group_b])
    core_a, core_b = send(cast_a, 0, 0, 1), send(cast_b, 0, 0, 1)
    cast_c, cast_d, cast_e = stage(other, ep, kp, [group_c, group_d, group_e])
    core_c, core_d, core_e = (send(v, 0, 0, 1) for v in (cast_c, cast_d, cast_e))
    a0, a1 = stage(mine, ep, kp, [group_a[:1], group_a[1:]], (core_a,), [(0, 0), (0, 1)])
    up = send(a0, 0, 1, 0)
    down = send(a1, 0, -1, 0)
    b_far, b_rest = stage(
        mine, ep, kp, [group_b[:1], group_b[1:]], (core_b,), [(0, i) for i in range(4)]
    )
    x_far = send(b_far, 1, 0, 0)
    x_rest = send(b_rest, 1, 0, 0)
    c01, c11, c03, c13 = stage(
        mine, ep, kp, [[piece] for piece in group_c], (core_c,), [(0, i) for i in range(4)]
    )
    up_plain = send(c11, 0, 1, 0)
    down_plain = send(c03, 0, -1, 0)
    d0, d1, e2, e1, e3, e0 = stage(
        mine,
        ep,
        kp,
        [[piece] for piece in group_d + group_e],
        (core_d, core_e),
        [(0, 0), (0, 1)] + [(1, i) for i in range(4)],
    )
    up_sum = send(plus(c01, up).astype(BF), 0, 1, 0)
    down_sum = send(plus(c13, down).astype(BF), 0, -1, 0)
    q2 = plus(e2, x_far).astype(BF)
    q_up = send(q2[:, :48], 0, 1, 0)
    q_down = send(q2[:, 48:], 0, -1, 0)
    q1 = plus(e1, x_rest[0:1])
    q3 = plus(e3, x_rest[1:2])
    q0 = plus(e0, x_rest[2:3])
    q1 = jnp.concatenate([q1[:, :48] + q_up.astype(F32), q1[:, 48:]], axis=1).astype(BF)
    q3 = jnp.concatenate([q3[:, :48], q3[:, 48:] + q_down.astype(F32)], axis=1).astype(BF)
    x_last = send(plus(d1, up_plain, down_sum).astype(BF), 1, 0, 0)
    q_up_sum = send(q1, 0, 1, 0)
    q_down_sum = send(q3, 0, -1, 0)
    first = plus(d0, up_sum, down_plain, x_last)[0]
    second = (q0 + q_up_sum.astype(F32) + q_down_sum.astype(F32))[0]

    key_grad = jnp.concatenate([first[ROWS:, :KCOLS], first[ROWS:, KCOLS:]], axis=0)
    new_kp, new_km, new_ks = adam_update(key_param, key_moment, key_second, key_grad)
    key_row = lax.dynamic_slice_in_dim(key_scales, dp_index // 4, 1, 0)
    key_grid = to_grid(new_kp, jnp.repeat(key_row, BLOCK, axis=1))
    chip_x = send(key_grid, 1, 0, 0)
    column = jnp.stack([key_grid, chip_x])
    all_y = jnp.stack([column, send(column, 0, -1, 0), send(column, 0, -2, 0), send(column, 0, -3, 0)])
    everything = jnp.stack([all_y, send(all_y, 0, 0, 1)]).reshape(16 * KROWS, KCOLS)
    order = jnp.arange(16 * KROWS, dtype=jnp.int32)
    piece, row = order // KROWS, order % KROWS
    held = dp_of(x + piece % 2, y + piece // 2 % 4, c + piece // 8) * KROWS + row
    source = order // HD * HD + rotary_order[order % HD]
    pick = (held[:, None] == source[None, :]).astype(BF)
    server_key = lax.dot_general(
        everything, pick, (((0,), (0,)), ((), ())), preferred_element_type=F32
    ).astype(BF)

    expert_grad = jnp.concatenate([first[:ROWS], second], axis=1)
    new_ep, new_em, new_es = adam_update(expert_param, expert_moment, expert_second, expert_grad[None])
    row_blocks = (dp_index * ROWS + jnp.arange(ROWS, dtype=jnp.int32)) // BLOCK
    my_scales = lax.dynamic_index_in_dim(expert_scales, expert_index, 0, keepdims=False)
    row_scales = jnp.take(my_scales, row_blocks, axis=0)
    grid = to_grid(new_ep[0], jnp.repeat(row_scales, BLOCK, axis=1))
    blocks = jnp.transpose(grid.reshape(ROWS, 8, 256), (1, 0, 2))
    arrived = lax.all_to_all(blocks, "expert", split_axis=0, concat_axis=0, tiled=True)
    server_expert = turned(arrived, expert_slot)
    return (new_ep, new_em, new_es, new_kp, new_km, new_ks, server_expert, server_key)


def solution(mesh):
    return jax.shard_map(
        on_device,
        mesh=mesh,
        in_specs=(
            P("dp", "expert", None, None),
            P("dp", None, "expert"),
            P("expert", "dp", None),
            P("expert", "dp", None),
            P("expert", "dp", None),
            P("dp", "expert"),
            P("dp", "expert"),
            P("dp", "expert"),
            P(),
            P(None, "expert"),
            P(),
            P(),
        ),
        out_specs=(
            P("expert", "dp", None),
            P("expert", "dp", None),
            P("expert", "dp", None),
            P("dp", "expert"),
            P("dp", "expert"),
            P("dp", "expert"),
            P(None, "expert", "dp"),
            P("expert", None),
        ),
        check_vma=False,
    )
```

time: 244 us -> 111 us (0.45)
  waiting for transfers between devices: 136 us -> 17.4 us
  local copies, waits for them, and re-layouts: 77.7 us -> 15.7 us
  starting transfers between devices: 4.41 us -> 42.6 us
  Pallas kernels: 0 us -> 21.9 us
  between operations: 14 us -> 1.19 us
    unnamed x4 -> x0, waiting for transfers between devices: 82.3 us -> none
    unnamed x34 -> x29, local copies, waits for them, and re-layouts: 67.1 us -> 10.2 us
    all_gather x1 -> x0, waiting for transfers between devices: 37.2 us -> none  [on_device(): gathered = lax.all_gather(new_kp, 'dp', axis=0, tiled=True)]
    ppermute x0 -> x23, starting transfers between devices: none -> 36.6 us  [send(): return lax.ppermute(value, 'dp', dp_perm(dx, dy, dc))]
    pallas_call x0 -> x7, Pallas kernels: none -> 21.9 us  [the longest x6 16.5 us: stage(): pl.pallas_call(functools.partial(stage_kernel, pieces, received_at, writt...]
    reduce_scatter x1 -> x0, waiting for transfers between devices: 16.8 us -> none  [on_device(): lax.psum_scatter(key_partials.astype(jnp.bfloat16), 'dp', scatter_dimensi...]
    ppermute x0 -> x23, waiting for transfers between devices: none -> 10.6 us  [send(): return lax.ppermute(value, 'dp', dp_perm(dx, dy, dc))]
    all_to_all x1, waiting for transfers between devices: 0.01 us -> 6.8 us  [on_device(): lax.all_to_all(blocks, 'expert', split_axis=0, concat_axis=0, tiled=True)]
  transfers between devices with their start and end apart: 4 -> 24, of which waited for: 3 -> 7; matrix products, arithmetic and copies ran while one was open for 34% -> 15% of each run, Pallas kernels for 0% -> 11%
where the time goes in v1:
time: 111 us; the launch traced here: 110 us
  starting transfers between devices  42.6 us (38%)
  Pallas kernels  21.9 us (20%)
  waiting for transfers between devices  17.4 us (16%)
  local copies, waits for them, and re-layouts  15.7 us (14%)
  other arithmetic  9.68 us (9%)
  matrix products  1.35 us (1%)
  between operations  1.19 us (1%)
    ppermute x23, starting transfers between devices, send(): return lax.ppermute(value, 'dp', dp_perm(dx, dy, dc))  36.6 us
    pallas_call x6, Pallas kernels, stage(): pl.pallas_call(functools.partial(stage_kernel, pieces, received_at, writt...  16.5 us
    ppermute x23, waiting for transfers between devices, send(): return lax.ppermute(value, 'dp', dp_perm(dx, dy, dc))  10.6 us
    unnamed x29, local copies, waits for them, and re-layouts  10.2 us
    all_to_all x1, waiting for transfers between devices, on_device(): lax.all_to_all(blocks, 'expert', split_axis=0, concat_axis=0, tiled=True)  6.8 us
    all_to_all x1, starting transfers between devices, on_device(): lax.all_to_all(blocks, 'expert', split_axis=0, concat_axis=0, tiled=True)  5.96 us
    pallas_call x1, Pallas kernels, turned(): pl.pallas_call(turn_kernel, out_shape=jax.ShapeDtypeStruct((experts, colu...  5.48 us
    gather x1, local copies, waits for them, and re-layouts, on_device(): source = order // HD * HD + rotary_order[order % HD]  3.35 us
  transfers between devices with their start and end apart: 24, of which 7 were waited for; matrix products, arithmetic and copies ran while one was open for 15% of the time, Pallas kernels for 11%

profile of v1, /device:TPU:1, one launch (start us, length us, event | category | flops | bytes accessed | tf_op | source)
XLA Modules:
  0.0 109.8 jit_solution(2989012360687771305)
XLA Ops:
  0.9 1.2 %copy-done.2 = f32[1,512,512]{2,1,0:T(8,128)S(1)} copy-done((f32[1,512,512]{2,1,0:T(8,128)S(1)}, f32[1,512,512]{2,1,0:T(8,128)}, u32[]{:S(2)}) %copy-start.2) | copy-done | bytes 1048600
  2.1 4.2 %shard_map.179 = (bf16[4,112,1024]{2,1,0:T(8,128)(2,1)}, bf16[2,112,1024]{2,1,0:T(8,128)(2,1)}, bf16[4,96,1024]{2,1,0:T(8,128)(2,1)}) custom-call(s32[10]{0:T(128)S(1)} %stack.128.ids, f32[16,96,2048]{2,1,0:T(8,128)} %bitcast.46, f32[16,32,512]{2,1,0:T(8,128)S(1)} %bitcast.52), custom_call_target="tpu_custom_call" | custom-call | flops 983040 | bytes 5898240 | tf_op jit(solution)/shard_map/pallas_call | solution.py:114
  6.3 1.5 %collective-permute-start = (bf16[2,112,1024]{2,1,0:T(8,128)(2,1)}, bf16[2,112,1024]{2,1,0:T(8,128)(2,1)S(1)}, u32[]{:S(2)}, u32[]{:S(2)}) collective-permute-start(bf16[2,112,1024]{2,1,0:T(8,128)(2,1)} %get-tuple-element.27), channel_id=1, source_target_pairs={{0,8},{8,0},{16,24},{24,16},{32,40},{40,32},{48,56},{56,48},{64,72... | collective-permute-start | bytes 1376264 | tf_op jit(solution)/shard_map/ppermute | solution.py:47
  8.0 3.3 %shard_map.182 = (bf16[2,112,1024]{2,1,0:T(8,128)(2,1)}, bf16[4,96,1024]{2,1,0:T(8,128)(2,1)}) custom-call(s32[6]{0:T(128)S(1)} %stack.135.ids, f32[16,96,2048]{2,1,0:T(8,128)} %bitcast.47, f32[16,32,512]{2,1,0:T(8,128)S(1)} %bitcast.53), custom_call_target="tpu_custom_call" | custom-call | flops 589824 | bytes 3538944 | tf_op jit(solution)/shard_map/pallas_call | solution.py:114
  11.3 0.5 collective-permute-start.11
  11.9 0.4 collective-permute-start.2
  12.5 0.7 dynamic-slice_bitcast_fusion
  13.3 2.0 %collective-permute-done.3.refs_0_ = bf16[2,112,1024]{2,1,0:T(8,128)(2,1)} collective-permute-done((bf16[2,112,1024]{2,1,0:T(8,128)(2,1)}, bf16[2,112,1024]{2,1,0:T(8,128)(2,1)}, u32[]{:S(2)}, u32[]{:S(2)}) %collective-permute-start.3) | collective-permute-done | bytes 458784 | tf_op jit(solution)/shard_map/ppermute | solution.py:47
  15.4 4.6 %copy-done.1 = f32[1,1,1536,2048]{3,2,1,0:T(8,128)S(1)} copy-done((f32[1,1,1536,2048]{3,2,1,0:T(8,128)S(1)}, f32[1,1,1536,2048]{3,2,1,0:T(8,128)}, u32[]{:S(2)}) %copy-start.1) | copy-done | bytes 12582936
  19.9 2.1 %shard_map.183 = (bf16[1,112,1024]{2,1,0:T(8,128)(2,1)S(1)}, bf16[1,112,1024]{2,1,0:T(8,128)(2,1)}) custom-call(s32[2]{0:T(128)S(1)} %pad_add_fusion.1.ids, f32[16,96,2048]{2,1,0:T(8,128)S(1)} %bitcast.51, f32[16,32,512]{2,1,0:T(8,128)S(1)} %bitcast.54, bf16[2,112,1024]{2,1,0:T(8,128)(2,1)} %collective-permute-done.3.refs_0_), custom_call_target="tpu_custom_call" | custom-call | flops 196608 | bytes 1179648 | tf_op jit(solution)/shard_map/pallas_call | solution.py:114
  22.0 0.7 copy-done.4
  22.7 2.8 %collective-permute-start.8 = (bf16[1,112,1024]{2,1,0:T(8,128)(2,1)}, bf16[1,112,1024]{2,1,0:T(8,128)(2,1)}, u32[]{:S(2)}, u32[]{:S(2)}) collective-permute-start(bf16[1,112,1024]{2,1,0:T(8,128)(2,1)} %get-tuple-element.38), channel_id=1, source_target_pairs={{0,48},{8,56},{16,0},{24,8},{32,16},{40,24},{48,32},{56,40},{64,11... | collective-permute-start | bytes 688136 | tf_op jit(solution)/shard_map/ppermute | solution.py:47
  25.7 0.6 gather_fusion
  26.3 3.3 %gather_fusion.1 = s32[512]{0:T(512)S(1)} fusion(s32[128]{0:T(128)S(1)} %copy-done.5, s32[1024]{0:T(1024)S(1)} %pad_clamp_fusion), kind=kCustom, calls=%fused_computation.1 | custom fusion | bytes 6144 | tf_op jit(solution)/shard_map/gather | solution.py:238
  29.9 2.6 %shard_map.184 = (bf16[1,96,1024]{2,1,0:T(8,128)(2,1)S(1)}, bf16[3,96,1024]{2,1,0:T(8,128)(2,1)S(1)}) custom-call(s32[4]{0:T(128)S(1)} %pad_add_fusion.2.ids, f32[16,96,2048]{2,1,0:T(8,128)} %bitcast.48, f32[16,32,512]{2,1,0:T(8,128)S(1)} %bitcast.55, bf16[4,96,1024]{2,1,0:T(8,128)(2,1)} %collective-permute-done.11.refs_0_), custom_call_target="tpu_custom_call" | custom-call | flops 393216 | bytes 2359296 | tf_op jit(solution)/shard_map/pallas_call | solution.py:114
  32.4 2.8 %collective-permute-start.12 = (bf16[3,96,1024]{2,1,0:T(8,128)(2,1)S(1)}, bf16[3,96,1024]{2,1,0:T(8,128)(2,1)S(1)}, u32[]{:S(2)}, u32[]{:S(2)}) collective-permute-start(bf16[3,96,1024]{2,1,0:T(8,128)(2,1)S(1)} %get-tuple-element.41), channel_id=1, source_target_pairs={{0,64},{8,72},{16,80},{24,88},{32,96},{40,104},{48,112},{56,120},{... | collective-permute-start | bytes 1769480 | tf_op jit(solution)/shard_map/ppermute | solution.py:47
  35.5 2.3 %shard_map.180 = (bf16[1,112,1024]{2,1,0:T(8,128)(2,1)S(1)}, bf16[1,112,1024]{2,1,0:T(8,128)(2,1)S(1)}, bf16[1,96,1024]{2,1,0:T(8,128)(2,1)S(1)}, bf16[1,96,1024...) custom-call(s32[6]{0:T(128)S(1)} %stack.120.ids, f32[16,96,2048]{2,1,0:T(8,128)} %bitcast.49, ...), custom_call_target="tpu_custom_call" | custom-call | flops 589824 | bytes 3538944 | tf_op jit(solution)/shard_map/pallas_call | solution.py:114
  37.8 2.1 %shard_map.181 = (bf16[1,112,1024]{2,1,0:T(8,128)(2,1)S(1)}, bf16[1,112,1024]{2,1,0:T(8,128)(2,1)S(1)}, bf16[1,112,1024]{2,1,0:T(8,128)(2,1)S(1)}, bf16[1,112,1024]{2,1,0:T(8,128)(2,1)S(1)}) custom-call(s32[4]{0:T(128)S(1)} %pad_add_fusion.ids, f32[16,96,2048]{2,1,0:T(8,128)} %bitcast.50, f32[16,32,512]{2,1,0:T(8,128)S(1)} %bitcast.57, ...), custom_call_target="tpu_custom_call" | custom-call | flops 393216 | bytes 2359296 | tf_op jit(solution)/shard_map/pallas_call | solution.py:114
  39.9 1.0 add_convert_fusion.1
  40.9 2.7 %collective-permute-start.9 = (bf16[1,112,1024]{2,1,0:T(8,128)(2,1)S(1)}, bf16[1,112,1024]{2,1,0:T(8,128)(2,1)S(1)}, u32[]{:S(2)}, u32[]{:S(2)}) collective-permute-start(bf16[1,112,1024]{2,1,0:T(8,128)(2,1)S(1)} %add_convert_fusion.1), channel_id=1, source_target_pairs={{0,48},{8,56},{16,0},{24,8},{32,16},{40,24},{48,32},{56,40},{64,11... | collective-permute-start | bytes 688136 | tf_op jit(solution)/shard_map/ppermute | solution.py:47
  43.7 2.7 %collective-permute-start.6 = (bf16[1,112,1024]{2,1,0:T(8,128)(2,1)S(1)}, bf16[1,112,1024]{2,1,0:T(8,128)(2,1)S(1)}, u32[]{:S(2)}, u32[]{:S(2)}) collective-permute-start(bf16[1,112,1024]{2,1,0:T(8,128)(2,1)S(1)} %get-tuple-element.34), channel_id=1, source_target_pairs={{0,48},{8,56},{16,0},{24,8},{32,16},{40,24},{48,32},{56,40},{64,11... | collective-permute-start | bytes 688136 | tf_op jit(solution)/shard_map/ppermute | solution.py:47
  46.4 6.1 %collective-permute-done.13 = bf16[1,96,1024]{2,1,0:T(8,128)(2,1)S(1)} collective-permute-done((bf16[1,96,1024]{2,1,0:T(8,128)(2,1)S(1)}, bf16[1,96,1024]{2,1,0:T(8,128)(2,1)S(1)}, u32[]{:S(2)}, u32[]{:S(2)}) %collective-permute-start.13) | collective-permute-done | bytes 196640 | tf_op jit(solution)/shard_map/ppermute | solution.py:47
  52.6 2.7 %collective-permute-start.16 = (bf16[1,48,1024]{2,1,0:T(8,128)(2,1)S(1)}, bf16[1,48,1024]{2,1,0:T(8,128)(2,1)S(1)}, u32[]{:S(2)}, u32[]{:S(2)}) collective-permute-start(bf16[1,48,1024]{2,1,0:T(8,128)(2,1)S(1)} %get-tuple-element.76), channel_id=1, source_target_pairs={{0,48},{8,56},{16,0},{24,8},{32,16},{40,24},{48,32},{56,40},{64,11... | collective-permute-start | bytes 294920 | tf_op jit(solution)/shard_map/ppermute | solution.py:47
  55.4 2.8 %collective-permute-start.10 = (bf16[1,112,1024]{2,1,0:T(8,128)(2,1)S(1)}, bf16[1,112,1024]{2,1,0:T(8,128)(2,1)S(1)}, u32[]{:S(2)}, u32[]{:S(2)}) collective-permute-start(bf16[1,112,1024]{2,1,0:T(8,128)(2,1)S(1)} %add_convert_fusion), channel_id=1, source_target_pairs={{0,64},{8,72},{16,80},{24,88},{32,96},{40,104},{48,112},{56,120},{... | collective-permute-start | bytes 688136 | tf_op jit(solution)/shard_map/ppermute | solution.py:47
  58.4 0.7 pad_maximum_fusion.4
  59.1 2.7 %collective-permute-start.17 = (bf16[1,96,1024]{2,1,0:T(8,128)(2,1)}, bf16[1,96,1024]{2,1,0:T(8,128)(2,1)S(1)}, u32[]{:S(2)}, u32[]{:S(2)}) collective-permute-start(bf16[1,96,1024]{2,1,0:T(8,128)(2,1)} %pad_maximum_fusion.4), channel_id=1, source_target_pairs={{0,48},{8,56},{16,0},{24,8},{32,16},{40,24},{48,32},{56,40},{64,11... | collective-permute-start | bytes 589832 | tf_op jit(solution)/shard_map/ppermute | solution.py:47
  62.1 0.7 clamp_convert_fusion
  62.8 3.1 %collective-permute-start.18 = (bf16[32,512]{1,0:T(8,128)(2,1)S(1)}, bf16[32,512]{1,0:T(8,128)(2,1)S(1)}, u32[]{:S(2)}, u32[]{:S(2)}) collective-permute-start(bf16[32,512]{1,0:T(8,128)(2,1)S(1)} %get-tuple-element.62), channel_id=1, source_target_pairs={{0,64},{8,72},{16,80},{24,88},{32,96},{40,104},{48,112},{56,120},{... | collective-permute-start | bytes 98312 | tf_op jit(solution)/shard_map/ppermute | solution.py:47
  65.9 0.7 pad_maximum_fusion.3
  66.6 0.3 collective-permute-start.15
  66.9 0.3 collective-permute-done.18
  67.2 1.2 %collective-permute-start.21 = (bf16[2,32,512]{2,1,0:T(8,128)(2,1)S(1)}, bf16[2,32,512]{2,1,0:T(8,128)(2,1)S(1)}, u32[]{:S(2)}, u32[]{:S(2)}) collective-permute-start(bf16[2,32,512]{2,1,0:T(8,128)(2,1)S(1)} %get-tuple-element.78), channel_id=1, source_target_pairs={{0,16},{8,24},{16,32},{24,40},{32,48},{40,56},{48,0},{56,8},{64,80... | collective-permute-start | bytes 196616 | tf_op jit(solution)/shard_map/ppermute | solution.py:47
  68.4 2.7 %collective-permute-start.20 = (bf16[2,32,512]{2,1,0:T(8,128)(2,1)S(1)}, bf16[2,32,512]{2,1,0:T(8,128)(2,1)S(1)}, u32[]{:S(2)}, u32[]{:S(2)}) collective-permute-start(bf16[2,32,512]{2,1,0:T(8,128)(2,1)S(1)} %get-tuple-element.78), channel_id=1, source_target_pairs={{0,32},{8,40},{16,48},{24,56},{32,0},{40,8},{48,16},{56,24},{64,96... | collective-permute-start | bytes 196616 | tf_op jit(solution)/shard_map/ppermute | solution.py:47
  71.1 1.3 %collective-permute-start.19 = (bf16[2,32,512]{2,1,0:T(8,128)(2,1)S(1)}, bf16[2,32,512]{2,1,0:T(8,128)(2,1)S(1)}, u32[]{:S(2)}, u32[]{:S(2)}) collective-permute-start(bf16[2,32,512]{2,1,0:T(8,128)(2,1)S(1)} %get-tuple-element.78), channel_id=1, source_target_pairs={{0,48},{8,56},{16,0},{24,8},{32,16},{40,24},{48,32},{56,40},{64,11... | collective-permute-start | bytes 196616 | tf_op jit(solution)/shard_map/ppermute | solution.py:47
  72.4 0.3 broadcast_in_dim.24
  72.9 0.4 collective-permute-done.21
  73.3 1.7 %collective-permute-done.20 = bf16[2,32,512]{2,1,0:T(8,128)(2,1)S(1)} collective-permute-done((bf16[2,32,512]{2,1,0:T(8,128)(2,1)S(1)}, bf16[2,32,512]{2,1,0:T(8,128)(2,1)S(1)}, u32[]{:S(2)}, u32[]{:S(2)}) %collective-permute-start.20) | collective-permute-done | bytes 65568 | tf_op jit(solution)/shard_map/ppermute | solution.py:47
  75.0 5.9 %collective-permute-start.22 = (bf16[4,2,32,512]{3,2,1,0:T(8,128)(2,1)S(1)}, bf16[4,2,32,512]{3,2,1,0:T(8,128)(2,1)S(1)}, u32[]{:S(2)}, u32[]{:S(2)}) collective-permute-start(bf16[4,2,32,512]{3,2,1,0:T(8,128)(2,1)S(1)} %get-tuple-element.74), channel_id=1, source_target_pairs={{0,8},{8,0},{16,24},{24,16},{32,40},{40,32},{48,56},{56,48},{64,72... | collective-permute-start | bytes 786440 | tf_op jit(solution)/shard_map/ppermute | solution.py:47
  80.9 0.7 copy-done.9
  81.6 1.1 %convert_add_fusion.1 = f32[1,96,1024]{2,1,0:T(8,128)S(1)} fusion(bf16[1,96,1024]{2,1,0:T(8,128)(2,1)} %copy-done.9, bf16[1,96,1024]{2,1,0:T(8,128)(2,1)S(1)} %collective-permute-done.15, bf16[1,96,1024]{2,1,0:T(8,128)(2,1)S(1)} %get-tuple-element.39, bf16[3,96,1024]{2,1,0:T(8,128)(2,1)} %copy-done.8), kind=kLoop, calls=%fused_computation.19 | loop fusion | flops 688128 | bytes 1179648 | tf_op jit(solution)/shard_map/add | solution.py:225
  82.7 3.3 %multiply_subtract_fusion = (f32[1,96,2048]{2,1,0:T(8,128)S(1)}, f32[1,96,2048]{2,1,0:T(8,128)}, f32[1,96,2048]{2,1,0:T(8,128)}) fusion(f32[1,96,2048]{2,1,0:T(8,128)} %param.14, f32[1,96,1024]{2,1,0:T(8,128)S(1)} %convert_add_fusion.1, f32[1,96,1024]{2,1,0:T(8,128)S(1)} %slice.55, f32[1,96,2048]{2,1,0:T(8,128)} %param.15, f32[1,96,2048]{2,1,0:T(8,128)} %param.16), kind=kLoop, calls=%fused_computation.10 | loop fusion | flops 2949120 | bytes 5505024 | tf_op jit(solution)/shard_map/sub | solution.py:54
  86.2 1.2 %fusion.6 = bf16[8,96,256]{2,1,0:T(8,128)(2,1)} fusion(f32[96,8,256]{2,1,0:T(8,128)S(1)} %reshape.392, f32[96,8,256]{2,1,0:T(8,128)S(1)} %bitcast.59), kind=kLoop, calls=%fused_computation.23 | loop fusion | flops 589824 | bytes 1966080 | tf_op jit(solution)/shard_map/transpose | solution.py:250
  87.4 6.0 %all-to-all-start = ((bf16[8,96,256]{2,1,0:T(8,128)(2,1)}), bf16[8,96,256]{2,1,0:T(8,128)(2,1)S(1)}, u32[]{:S(2)}, u32[]{:S(2)}) async-start(bf16[8,96,256]{2,1,0:T(8,128)(2,1)} %fusion.6), calls=%async_computation | async-start | bytes 786432 | tf_op jit(solution)/shard_map/all_to_all | solution.py:251
  93.5 1.3 %convolution_convert_fusion = bf16[512,512]{1,0:T(8,128)(2,1)} fusion(bf16[512,512]{1,0:T(8,128)(2,1)S(1)} %bitcast.62, s32[512]{0:T(512)S(1)} %get-tuple-element.80, s32[512]{0:T(512)S(1)} %get-tuple-element.79), kind=kOutput, calls=%fused_computation.2 | convolution fusion | flops 268959744 | bytes 1052672 | tf_op jit(solution)/shard_map/dot_general | solution.py:240
  94.8 6.8 %all-to-all-done.arrived = bf16[8,96,256]{2,1,0:T(8,128)(2,1)S(1)} async-done(((bf16[8,96,256]{2,1,0:T(8,128)(2,1)}), bf16[8,96,256]{2,1,0:T(8,128)(2,1)S(1)}, u32[]{:S(2)}, u32[]{:S(2)}) %all-to-all-start) | async-done | bytes 393248 | tf_op jit(solution)/shard_map/all_to_all | solution.py:251
  101.6 0.7 copy-done.7
  102.4 5.5 %shard_map.185 = bf16[8,256,96]{2,1,0:T(8,128)(2,1)} custom-call(s32[8]{0:T(128)} %slot.1, bf16[8,96,256]{2,1,0:T(8,128)(2,1)} %copy-done.7), custom_call_target="tpu_custom_call" | custom-call | tf_op jit(solution)/shard_map/pallas_call | solution.py:148
  107.8 2.0 %copy.24 = bf16[8,256,96]{1,2,0:T(8,128)(2,1)} copy(bf16[8,256,96]{2,1,0:T(8,128)(2,1)} %shard_map.185) | data formatting | bytes 786432
  (79 shorter events, 2.5 us)
Async XLA Ops:
  0.6 12.7 %copy-start = (f32[8,12,16]{2,0,1:T(8,128)S(1)}, f32[8,12,16]{2,0,1:T(8,128)}, u32[]{:S(2)}) copy-start(f32[8,12,16]{2,0,1:T(8,128)} %param.20) | copy-start | bytes 18436
  0.9 1.2 %copy-start.2 = (f32[1,512,512]{2,1,0:T(8,128)S(1)}, f32[1,512,512]{2,1,0:T(8,128)}, u32[]{:S(2)}) copy-start(f32[1,512,512]{2,1,0:T(8,128)} %param.13) | copy-start | bytes 3145732
  2.1 5.9 %copy-start.3 = (f32[1,512,512]{2,1,0:T(8,128)S(1)}, f32[1,512,512]{2,1,0:T(8,128)}, u32[]{:S(2)}) copy-start(f32[1,512,512]{2,1,0:T(8,128)} %param.13) | copy-start | bytes 3145732
  6.3 26.1 %collective-permute-start = (bf16[2,112,1024]{2,1,0:T(8,128)(2,1)}, bf16[2,112,1024]{2,1,0:T(8,128)(2,1)S(1)}, u32[]{:S(2)}, u32[]{:S(2)}) collective-permute-start(bf16[2,112,1024]{2,1,0:T(8,128)(2,1)} %get-tuple-element.27), channel_id=1, source_target_pairs={{0,8},{8,0},{16,24},{24,16},{32,40},{40,32},{48,56},{56,48},{64,72... | collective-permute-start | bytes 1376264 | tf_op jit(solution)/shard_map/ppermute | solution.py:47
  7.8 27.4 %collective-permute-start.1 = (bf16[4,96,1024]{2,1,0:T(8,128)(2,1)}, bf16[4,96,1024]{2,1,0:T(8,128)(2,1)S(1)}, u32[]{:S(2)}, u32[]{:S(2)}) collective-permute-start(bf16[4,96,1024]{2,1,0:T(8,128)(2,1)} %get-tuple-element.28), channel_id=1, source_target_pairs={{0,8},{8,0},{16,24},{24,16},{32,40},{40,32},{48,56},{56,48},{64,72... | collective-permute-start | bytes 2359304 | tf_op jit(solution)/shard_map/ppermute | solution.py:47
  8.0 18.3 %copy-start.5 = (s32[128]{0:T(128)S(1)}, s32[128]{0:T(128)}, u32[]{:S(2)}) copy-start(s32[128]{0:T(128)} %param.22) | copy-start | bytes 1540
  11.3 18.5 %collective-permute-start.11 = (bf16[4,96,1024]{2,1,0:T(8,128)(2,1)}, bf16[4,96,1024]{2,1,0:T(8,128)(2,1)}, u32[]{:S(2)}, u32[]{:S(2)}) collective-permute-start(bf16[4,96,1024]{2,1,0:T(8,128)(2,1)} %get-tuple-element.40), channel_id=1, source_target_pairs={{0,8},{8,0},{16,24},{24,16},{32,40},{40,32},{48,56},{56,48},{64,72... | collective-permute-start | bytes 2359304 | tf_op jit(solution)/shard_map/ppermute | solution.py:47
  11.8 3.6 %collective-permute-start.3 = (bf16[2,112,1024]{2,1,0:T(8,128)(2,1)}, bf16[2,112,1024]{2,1,0:T(8,128)(2,1)}, u32[]{:S(2)}, u32[]{:S(2)}) collective-permute-start(bf16[2,112,1024]{2,1,0:T(8,128)(2,1)} %get-tuple-element.32), channel_id=1, source_target_pairs={{0,8},{8,0},{16,24},{24,16},{32,40},{40,32},{48,56},{56,48},{64,72... | collective-permute-start | bytes 1376264 | tf_op jit(solution)/shard_map/ppermute | solution.py:47
  11.9 25.9 %collective-permute-start.2 = (bf16[4,112,1024]{2,1,0:T(8,128)(2,1)}, bf16[4,112,1024]{2,1,0:T(8,128)(2,1)S(1)}, u32[]{:S(2)}, u32[]{:S(2)}) collective-permute-start(bf16[4,112,1024]{2,1,0:T(8,128)(2,1)} %get-tuple-element.30), channel_id=1, source_target_pairs={{0,8},{8,0},{16,24},{24,16},{32,40},{40,32},{48,56},{56,48},{64,72... | collective-permute-start | bytes 2752520 | tf_op jit(solution)/shard_map/ppermute | solution.py:47
  15.4 4.6 %copy-start.1 = (f32[1,1,1536,2048]{3,2,1,0:T(8,128)S(1)}, f32[1,1,1536,2048]{3,2,1,0:T(8,128)}, u32[]{:S(2)}) copy-start(f32[1,1,1536,2048]{3,2,1,0:T(8,128)} %param.12) | copy-start | bytes 37748740
  22.0 0.7 copy-start.4
  22.7 17.2 %collective-permute-start.8 = (bf16[1,112,1024]{2,1,0:T(8,128)(2,1)}, bf16[1,112,1024]{2,1,0:T(8,128)(2,1)}, u32[]{:S(2)}, u32[]{:S(2)}) collective-permute-start(bf16[1,112,1024]{2,1,0:T(8,128)(2,1)} %get-tuple-element.38), channel_id=1, source_target_pairs={{0,48},{8,56},{16,0},{24,8},{32,16},{40,24},{48,32},{56,40},{64,11... | collective-permute-start | bytes 688136 | tf_op jit(solution)/shard_map/ppermute | solution.py:47
  29.8 13.9 %collective-permute-start.4 = (bf16[1,112,1024]{2,1,0:T(8,128)(2,1)}, bf16[1,112,1024]{2,1,0:T(8,128)(2,1)S(1)}, u32[]{:S(2)}, u32[]{:S(2)}) collective-permute-start(bf16[1,112,1024]{2,1,0:T(8,128)(2,1)} %copy-done.4), channel_id=1, source_target_pairs={{0,16},{8,24},{16,32},{24,40},{32,48},{40,56},{48,0},{56,8},{64,80... | collective-permute-start | bytes 688136 | tf_op jit(solution)/shard_map/ppermute | solution.py:47
  32.4 23.0 %collective-permute-start.12 = (bf16[3,96,1024]{2,1,0:T(8,128)(2,1)S(1)}, bf16[3,96,1024]{2,1,0:T(8,128)(2,1)S(1)}, u32[]{:S(2)}, u32[]{:S(2)}) collective-permute-start(bf16[3,96,1024]{2,1,0:T(8,128)(2,1)S(1)} %get-tuple-element.41), channel_id=1, source_target_pairs={{0,64},{8,72},{16,80},{24,88},{32,96},{40,104},{48,112},{56,120},{... | collective-permute-start | bytes 1769480 | tf_op jit(solution)/shard_map/ppermute | solution.py:47
  35.3 17.2 %collective-permute-start.13 = (bf16[1,96,1024]{2,1,0:T(8,128)(2,1)S(1)}, bf16[1,96,1024]{2,1,0:T(8,128)(2,1)S(1)}, u32[]{:S(2)}, u32[]{:S(2)}) collective-permute-start(bf16[1,96,1024]{2,1,0:T(8,128)(2,1)S(1)} %get-tuple-element.44), channel_id=1, source_target_pairs={{0,64},{8,72},{16,80},{24,88},{32,96},{40,104},{48,112},{56,120},{... | collective-permute-start | bytes 589832 | tf_op jit(solution)/shard_map/ppermute | solution.py:47
  37.8 24.3 %copy-start.10 = (f32[32,512]{1,0:T(8,128)S(1)}, f32[32,512]{1,0:T(8,128)}, u32[]{:S(2)}) copy-start(f32[32,512]{1,0:T(8,128)} %param.17) | copy-start | bytes 196612
  37.8 24.3 %copy-start.11 = (f32[32,512]{1,0:T(8,128)S(1)}, f32[32,512]{1,0:T(8,128)}, u32[]{:S(2)}) copy-start(f32[32,512]{1,0:T(8,128)} %param.18) | copy-start | bytes 196612
  37.8 24.3 %copy-start.12 = (f32[32,512]{1,0:T(8,128)S(1)}, f32[32,512]{1,0:T(8,128)}, u32[]{:S(2)}) copy-start(f32[32,512]{1,0:T(8,128)} %param.19) | copy-start | bytes 196612
  40.9 11.6 %collective-permute-start.9 = (bf16[1,112,1024]{2,1,0:T(8,128)(2,1)S(1)}, bf16[1,112,1024]{2,1,0:T(8,128)(2,1)S(1)}, u32[]{:S(2)}, u32[]{:S(2)}) collective-permute-start(bf16[1,112,1024]{2,1,0:T(8,128)(2,1)S(1)} %add_convert_fusion.1), channel_id=1, source_target_pairs={{0,48},{8,56},{16,0},{24,8},{32,16},{40,24},{48,32},{56,40},{64,11... | collective-permute-start | bytes 688136 | tf_op jit(solution)/shard_map/ppermute | solution.py:47
  43.6 11.7 %collective-permute-start.7 = (bf16[1,112,1024]{2,1,0:T(8,128)(2,1)S(1)}, bf16[1,112,1024]{2,1,0:T(8,128)(2,1)S(1)}, u32[]{:S(2)}, u32[]{:S(2)}) collective-permute-start(bf16[1,112,1024]{2,1,0:T(8,128)(2,1)S(1)} %get-tuple-element.36), channel_id=1, source_target_pairs={{0,16},{8,24},{16,32},{24,40},{32,48},{40,56},{48,0},{56,8},{64,80... | collective-permute-start | bytes 688136 | tf_op jit(solution)/shard_map/ppermute | solution.py:47
  43.7 18.1 %collective-permute-start.6 = (bf16[1,112,1024]{2,1,0:T(8,128)(2,1)S(1)}, bf16[1,112,1024]{2,1,0:T(8,128)(2,1)S(1)}, u32[]{:S(2)}, u32[]{:S(2)}) collective-permute-start(bf16[1,112,1024]{2,1,0:T(8,128)(2,1)S(1)} %get-tuple-element.34), channel_id=1, source_target_pairs={{0,48},{8,56},{16,0},{24,8},{32,16},{40,24},{48,32},{56,40},{64,11... | collective-permute-start | bytes 688136 | tf_op jit(solution)/shard_map/ppermute | solution.py:47
  52.5 9.3 %collective-permute-start.5 = (bf16[1,112,1024]{2,1,0:T(8,128)(2,1)S(1)}, bf16[1,112,1024]{2,1,0:T(8,128)(2,1)S(1)}, u32[]{:S(2)}, u32[]{:S(2)}) collective-permute-start(bf16[1,112,1024]{2,1,0:T(8,128)(2,1)S(1)} %add_convert_fusion.2), channel_id=1, source_target_pairs={{0,16},{8,24},{16,32},{24,40},{32,48},{40,56},{48,0},{56,8},{64,80... | collective-permute-start | bytes 688136 | tf_op jit(solution)/shard_map/ppermute | solution.py:47
  52.6 5.8 %collective-permute-start.16 = (bf16[1,48,1024]{2,1,0:T(8,128)(2,1)S(1)}, bf16[1,48,1024]{2,1,0:T(8,128)(2,1)S(1)}, u32[]{:S(2)}, u32[]{:S(2)}) collective-permute-start(bf16[1,48,1024]{2,1,0:T(8,128)(2,1)S(1)} %get-tuple-element.76), channel_id=1, source_target_pairs={{0,48},{8,56},{16,0},{24,8},{32,16},{40,24},{48,32},{56,40},{64,11... | collective-permute-start | bytes 294920 | tf_op jit(solution)/shard_map/ppermute | solution.py:47
  55.3 10.6 %collective-permute-start.14 = (bf16[1,48,1024]{2,1,0:T(8,128)(2,1)S(1)}, bf16[1,48,1024]{2,1,0:T(8,128)(2,1)S(1)}, u32[]{:S(2)}, u32[]{:S(2)}) collective-permute-start(bf16[1,48,1024]{2,1,0:T(8,128)(2,1)S(1)} %get-tuple-element.75), channel_id=1, source_target_pairs={{0,16},{8,24},{16,32},{24,40},{32,48},{40,56},{48,0},{56,8},{64,80... | collective-permute-start | bytes 294920 | tf_op jit(solution)/shard_map/ppermute | solution.py:47
  55.4 17.0 %copy-start.8 = (bf16[3,96,1024]{2,1,0:T(8,128)(2,1)}, bf16[3,96,1024]{2,1,0:T(8,128)(2,1)S(1)}, u32[]{:S(2)}) copy-start(bf16[3,96,1024]{2,1,0:T(8,128)(2,1)S(1)} %collective-permute-done.12) | copy-start | bytes 1769476
  55.4 6.5 %collective-permute-start.10 = (bf16[1,112,1024]{2,1,0:T(8,128)(2,1)S(1)}, bf16[1,112,1024]{2,1,0:T(8,128)(2,1)S(1)}, u32[]{:S(2)}, u32[]{:S(2)}) collective-permute-start(bf16[1,112,1024]{2,1,0:T(8,128)(2,1)S(1)} %add_convert_fusion), channel_id=1, source_target_pairs={{0,64},{8,72},{16,80},{24,88},{32,96},{40,104},{48,112},{56,120},{... | collective-permute-start | bytes 688136 | tf_op jit(solution)/shard_map/ppermute | solution.py:47
  59.1 21.8 %collective-permute-start.17 = (bf16[1,96,1024]{2,1,0:T(8,128)(2,1)}, bf16[1,96,1024]{2,1,0:T(8,128)(2,1)S(1)}, u32[]{:S(2)}, u32[]{:S(2)}) collective-permute-start(bf16[1,96,1024]{2,1,0:T(8,128)(2,1)} %pad_maximum_fusion.4), channel_id=1, source_target_pairs={{0,48},{8,56},{16,0},{24,8},{32,16},{40,24},{48,32},{56,40},{64,11... | collective-permute-start | bytes 589832 | tf_op jit(solution)/shard_map/ppermute | solution.py:47
  62.8 4.4 %collective-permute-start.18 = (bf16[32,512]{1,0:T(8,128)(2,1)S(1)}, bf16[32,512]{1,0:T(8,128)(2,1)S(1)}, u32[]{:S(2)}, u32[]{:S(2)}) collective-permute-start(bf16[32,512]{1,0:T(8,128)(2,1)S(1)} %get-tuple-element.62), channel_id=1, source_target_pairs={{0,64},{8,72},{16,80},{24,88},{32,96},{40,104},{48,112},{56,120},{... | collective-permute-start | bytes 98312 | tf_op jit(solution)/shard_map/ppermute | solution.py:47
  66.6 14.3 %collective-permute-start.15 = (bf16[1,96,1024]{2,1,0:T(8,128)(2,1)}, bf16[1,96,1024]{2,1,0:T(8,128)(2,1)S(1)}, u32[]{:S(2)}, u32[]{:S(2)}) collective-permute-start(bf16[1,96,1024]{2,1,0:T(8,128)(2,1)} %pad_maximum_fusion.3), channel_id=1, source_target_pairs={{0,16},{8,24},{16,32},{24,40},{32,48},{40,56},{48,0},{56,8},{64,80... | collective-permute-start | bytes 589832 | tf_op jit(solution)/shard_map/ppermute | solution.py:47
  67.2 6.0 %collective-permute-start.21 = (bf16[2,32,512]{2,1,0:T(8,128)(2,1)S(1)}, bf16[2,32,512]{2,1,0:T(8,128)(2,1)S(1)}, u32[]{:S(2)}, u32[]{:S(2)}) collective-permute-start(bf16[2,32,512]{2,1,0:T(8,128)(2,1)S(1)} %get-tuple-element.78), channel_id=1, source_target_pairs={{0,16},{8,24},{16,32},{24,40},{32,48},{40,56},{48,0},{56,8},{64,80... | collective-permute-start | bytes 196616 | tf_op jit(solution)/shard_map/ppermute | solution.py:47
  68.4 6.6 %collective-permute-start.20 = (bf16[2,32,512]{2,1,0:T(8,128)(2,1)S(1)}, bf16[2,32,512]{2,1,0:T(8,128)(2,1)S(1)}, u32[]{:S(2)}, u32[]{:S(2)}) collective-permute-start(bf16[2,32,512]{2,1,0:T(8,128)(2,1)S(1)} %get-tuple-element.78), channel_id=1, source_target_pairs={{0,32},{8,40},{16,48},{24,56},{32,0},{40,8},{48,16},{56,24},{64,96... | collective-permute-start | bytes 196616 | tf_op jit(solution)/shard_map/ppermute | solution.py:47
  71.1 3.9 %collective-permute-start.19 = (bf16[2,32,512]{2,1,0:T(8,128)(2,1)S(1)}, bf16[2,32,512]{2,1,0:T(8,128)(2,1)S(1)}, u32[]{:S(2)}, u32[]{:S(2)}) collective-permute-start(bf16[2,32,512]{2,1,0:T(8,128)(2,1)S(1)} %get-tuple-element.78), channel_id=1, source_target_pairs={{0,48},{8,56},{16,0},{24,8},{32,16},{40,24},{48,32},{56,40},{64,11... | collective-permute-start | bytes 196616 | tf_op jit(solution)/shard_map/ppermute | solution.py:47
  75.0 18.4 %collective-permute-start.22 = (bf16[4,2,32,512]{3,2,1,0:T(8,128)(2,1)S(1)}, bf16[4,2,32,512]{3,2,1,0:T(8,128)(2,1)S(1)}, u32[]{:S(2)}, u32[]{:S(2)}) collective-permute-start(bf16[4,2,32,512]{3,2,1,0:T(8,128)(2,1)S(1)} %get-tuple-element.74), channel_id=1, source_target_pairs={{0,8},{8,0},{16,24},{24,16},{32,40},{40,32},{48,56},{56,48},{64,72... | collective-permute-start | bytes 786440 | tf_op jit(solution)/shard_map/ppermute | solution.py:47
  80.9 0.7 copy-start.9
  86.0 23.8 %copy-start.6 = (f32[1,96,2048]{2,1,0:T(8,128)}, f32[1,96,2048]{2,1,0:T(8,128)S(1)}, u32[]{:S(2)}) copy-start(f32[1,96,2048]{2,1,0:T(8,128)S(1)} %get-tuple-element.66) | copy-start | bytes 2359300
  87.4 14.2 %all-to-all-start = ((bf16[8,96,256]{2,1,0:T(8,128)(2,1)}), bf16[8,96,256]{2,1,0:T(8,128)(2,1)S(1)}, u32[]{:S(2)}, u32[]{:S(2)}) async-start(bf16[8,96,256]{2,1,0:T(8,128)(2,1)} %fusion.6), calls=%async_computation | async-start | bytes 786432 | tf_op jit(solution)/shard_map/all_to_all | solution.py:251
  101.6 0.7 copy-start.7

commit v2 on v0

v2 whole, which is shorter than its diff:
```python
import functools

import jax
import jax.numpy as jnp
from jax import lax
from jax.experimental import pallas as pl
from jax.experimental.pallas import tpu as pltpu
from jax.sharding import PartitionSpec as P

HD = 128
BLOCK = 128

BETA_ONE = 0.9
BETA_TWO = 0.95
LEARN = 0.01
DECAY = 0.1
EPSILON = 1e-08
LIMIT = 448.0
CORRECT_ONE = 1.0 - 0.9**10
CORRECT_TWO = 1.0 - 0.95**10

ROWS = 96
KROWS = 32
HALF = 1024
KCOLS = 512
PROWS = 112

BF = jnp.bfloat16
F32 = jnp.float32
VMEM_BYTES = 12 * 1024 * 1024


def dp_of(x, y, c):
    return ((x % 2) * 4 + (y % 4)) * 2 + c % 2


def dp_perm(dx, dy, dc):
    return [
        (dp_of(x, y, c), dp_of(x + dx, y + dy, c + dc))
        for x in range(2)
        for y in range(4)
        for c in range(2)
    ]


def send(value, dx, dy, dc):
    return lax.ppermute(value, "dp", dp_perm(dx, dy, dc))


def ring(value):
    pairs = [
        (dp_of(x, y, c), dp_of(x, y + 1 - 2 * c, c))
        for x in range(2)
        for y in range(4)
        for c in range(2)
    ]
    return lax.ppermute(value, "dp", pairs)


def after(value, *earlier):
    return lax.optimization_barrier((value, *earlier))[0]


def adam_update(param, moment, second, grad):
    moment = BETA_ONE * moment + (1.0 - BETA_ONE) * grad
    second = BETA_TWO * second + (1.0 - BETA_TWO) * grad * grad
    corrected = moment / CORRECT_ONE / (jnp.sqrt(second / CORRECT_TWO) + EPSILON)
    return (param * (1.0 - LEARN * DECAY) - LEARN * corrected, moment, second)


def to_grid(weights, scales):
    return jnp.clip(weights / scales, -LIMIT, LIMIT).astype(BF)


def owner(piece, x, y, c):
    _, dx, role = piece
    step = {"far": 2, "near": 1 - 2 * c, "plain": 1 - 2 * c, "own": 0}[role]
    return dp_of(x + dx, y + 4 + step, 1 - c if role == "plain" else c)


def parts_of(piece, block, ep, kp, out):
    if piece[0] == "Q":
        return [(ep.at[block, :, pl.ds(HALF, HALF)], out)]
    return [
        (ep.at[block, :, pl.ds(0, HALF)], out.at[pl.ds(0, ROWS)]),
        (kp.at[block, pl.ds(0, 16)], out.at[pl.ds(ROWS, 16), pl.ds(0, KCOLS)]),
        (kp.at[block, pl.ds(16, 16)], out.at[pl.ds(ROWS, 16), pl.ds(KCOLS, KCOLS)]),
    ]


def rows_of(kind):
    return PROWS if kind == "P" else ROWS


def load_kernel(groups, n_late, ep, kp, *refs):
    refs = refs[n_late:]
    n = len(groups)
    casts, keeps, buffers, sems = refs[:n], refs[n : 2 * n], refs[2 * n : 3 * n], refs[3 * n]
    dp_index = lax.axis_index("dp")
    x, y, c = dp_index // 8, dp_index // 2 % 4, dp_index % 2
    used = 0
    waits = []
    for group, buffer in zip(groups, buffers):
        for place, piece in enumerate(group):
            block = owner(piece, x, y, 1 - c)
            copies = []
            for source, target in parts_of(piece, block, ep, kp, buffer.at[place]):
                copies.append(pltpu.make_async_copy(source, target, sems.at[used]))
                used += 1
            for copy in copies:
                copy.start()
            waits.append(copies)
    kept = []
    for group, keep in zip(groups, keeps):
        for place, piece in enumerate(group):
            block = owner(piece, x, y, c)
            for source, target in parts_of(piece, block, ep, kp, keep.at[place]):
                copy = pltpu.make_async_copy(source, target, sems.at[used])
                used += 1
                copy.start()
                kept.append(copy)
    at = 0
    for group, buffer, cast in zip(groups, buffers, casts):
        for place, piece in enumerate(group):
            for copy in waits[at]:
                copy.wait()
            at += 1

            def rows(step, carry):
                some = pl.ds(pl.multiple_of(step * 16, 16), 16)
                cast[place, some] = buffer[place, some].astype(BF)
                return carry

            lax.fori_loop(0, rows_of(piece[0]) // 16, rows, 0)
    for copy in kept:
        copy.wait()


def load(ep, kp, groups, late=()):
    shapes = [(len(group), rows_of(group[0][0]), HALF) for group in groups]
    n_copies = 2 * sum(3 if piece[0] == "P" else 1 for group in groups for piece in group)
    vmem = pl.BlockSpec(memory_space=pltpu.VMEM)
    hbm = pl.BlockSpec(memory_space=pltpu.HBM)
    anywhere = pl.BlockSpec(memory_space=pl.ANY)
    out = pl.pallas_call(
        functools.partial(load_kernel, groups, len(late)),
        out_shape=[pltpu.VMEM(shape, BF) for shape in shapes]
        + [pltpu.VMEM(shape, F32) for shape in shapes],
        in_specs=[hbm, hbm] + [anywhere] * len(late),
        out_specs=[vmem] * (2 * len(shapes)),
        scratch_shapes=[pltpu.VMEM(shape, F32) for shape in shapes]
        + [pltpu.SemaphoreType.DMA((n_copies,))],
        compiler_params=pltpu.CompilerParams(vmem_limit_bytes=VMEM_BYTES),
        cost_estimate=pl.CostEstimate(flops=1000, bytes_accessed=1000, transcendentals=0),
    )(ep, kp, *late)
    return out[: len(shapes)], out[len(shapes) :]


def plus(*values):
    total = values[0].astype(F32)
    for value in values[1:]:
        total = total + value.astype(F32)
    return total


def update_kernel(first, second, param, moment, variance, scales, new_param, new_moment, new_variance, grid):
    for j in range(8):
        for h in range(2):
            k = 2 * j + h
            columns = pl.ds(k * BLOCK, BLOCK)
            source = first if k < 8 else second
            grad = source[:ROWS, pl.ds(k % 8 * BLOCK, BLOCK)]
            p, m, v = adam_update(param[0, :, columns], moment[0, :, columns], variance[0, :, columns], grad)
            new_param[0, :, columns] = p
            new_moment[0, :, columns] = m
            new_variance[0, :, columns] = v
            grid[j, :, pl.ds(h * BLOCK, BLOCK)] = to_grid(p, scales[:, k : k + 1])


def update(first, second, param, moment, variance, scales):
    vmem = pl.BlockSpec(memory_space=pltpu.VMEM)
    near = lambda v: pltpu.with_memory_space_constraint(v, pltpu.VMEM)
    return pl.pallas_call(
        update_kernel,
        out_shape=[pltpu.VMEM(param.shape, F32)] * 3 + [pltpu.VMEM((8, ROWS, 256), BF)],
        in_specs=[vmem] * 6,
        out_specs=[vmem] * 4,
        compiler_params=pltpu.CompilerParams(vmem_limit_bytes=VMEM_BYTES),
        cost_estimate=pl.CostEstimate(flops=1000, bytes_accessed=1000, transcendentals=0),
    )(near(first), near(second), near(param), near(moment), near(variance), scales)


def on_device(
    expert_partials,
    key_partials,
    expert_param,
    expert_moment,
    expert_second,
    key_param,
    key_moment,
    key_second,
    expert_scales,
    key_scales,
    rotary_order,
    expert_slot,
):
    dp_index = lax.axis_index("dp")
    expert_index = lax.axis_index("expert")
    x, y, c = dp_index // 8, dp_index // 2 % 4, dp_index % 2
    ep = pltpu.with_memory_space_constraint(expert_partials.reshape(16, ROWS, 2 * HALF), pltpu.HBM)
    kp = pltpu.with_memory_space_constraint(key_partials.reshape(16, KROWS, KCOLS), pltpu.HBM)

    q1_groups = [[("Q", 1, "far")], [("Q", 1, "plain"), ("Q", 1, "near"), ("Q", 1, "own")]]
    far_groups = [[("P", 0, "far"), ("P", 1, "far")]]
    plain_groups = [
        [("P", 0, "plain"), ("P", 1, "plain")],
        [("P", 0, "near"), ("P", 1, "near")],
    ]
    own_groups = [
        [("Q", 0, "far"), ("Q", 0, "plain"), ("Q", 0, "near"), ("Q", 0, "own")],
        [("P", 0, "own"), ("P", 1, "own")],
    ]

    casts_1, keeps_1 = load(ep, kp, q1_groups)
    got_1 = [send(v, 0, 0, 1) for v in casts_1]
    casts_2, keeps_2 = load(ep, kp, far_groups, late=(casts_1[0],))
    got_2 = [send(v, 0, 0, 1) for v in casts_2]
    q1_far = plus(keeps_1[0], got_1[0]).astype(BF)
    x_far = send(q1_far, 1, 0, 0)
    p_far = plus(keeps_2[0], got_2[0]).astype(BF)
    ring_far = ring(p_far)
    q1_rest = plus(keeps_1[1], got_1[1]).astype(BF)
    x_rest = send(q1_rest, 1, 0, 0)
    casts_3, keeps_3 = load(ep, kp, plain_groups, late=(p_far,))
    got_3 = [send(v, 0, 0, 1) for v in casts_3]
    casts_4, keeps_4 = load(ep, kp, own_groups, late=(casts_3[0], q1_rest))
    got_4 = [send(v, 0, 0, 1) for v in casts_4]
    ring_plain = ring(plus(keeps_3[0], got_3[0]).astype(BF))
    ring_near = ring(plus(keeps_3[1], got_3[1], ring_far).astype(BF))
    stay = keeps_4[0], got_4[0]
    ring_q_far = ring(plus(stay[0][:1], stay[1][:1], x_far).astype(BF))
    cross_plain = send(ring_plain, 0, 0, 1)
    p_own = plus(keeps_4[1], got_4[1])
    ring_q_plain = ring(plus(stay[0][1:2], stay[1][1:2], x_rest[0:1]).astype(BF))
    ring_q_near = ring(plus(stay[0][2:3], stay[1][2:3], x_rest[1:2], ring_q_far).astype(BF))
    x_last = send(plus(p_own[1:], ring_near[1:], cross_plain[1:]).astype(BF), 1, 0, 0)
    cross_q_plain = send(ring_q_plain, 0, 0, 1)
    first = plus(p_own[:1], ring_near[:1], cross_plain[:1], x_last)[0]
    second = plus(stay[0][3:], stay[1][3:], x_rest[2:3], cross_q_plain, ring_q_near)[0]

    low = dp_index * ROWS // BLOCK
    my_scales = lax.dynamic_slice(expert_scales, (expert_index, low, 0), (1, 1, 16))[0]
    next_scales = lax.dynamic_slice(
        expert_scales, (expert_index, jnp.minimum(low + 1, 11), 0), (1, 1, 16)
    )[0]
    row_blocks = (dp_index * ROWS + jnp.arange(ROWS, dtype=jnp.int32)) // BLOCK
    row_scales = jnp.where((row_blocks == low)[:, None], my_scales, next_scales)
    new_ep, new_em, new_es, blocks = update(
        first, second, expert_param, expert_moment, expert_second, row_scales
    )
    arrived = lax.all_to_all(blocks, "expert", split_axis=0, concat_axis=0, tiled=True)
    placed = jnp.zeros_like(arrived).at[expert_slot].set(arrived)
    server_expert = jnp.transpose(placed, (0, 2, 1))

    key_grad = jnp.concatenate([first[ROWS:, :KCOLS], first[ROWS:, KCOLS:]], axis=0)
    new_kp, new_km, new_ks = adam_update(key_param, key_moment, key_second, key_grad)
    key_row = lax.dynamic_slice_in_dim(key_scales, dp_index // 4, 1, 0)
    key_grid = to_grid(new_kp, jnp.repeat(key_row, BLOCK, axis=1))
    chip_x = send(key_grid, 1, 0, 0)
    column = jnp.stack([key_grid, chip_x])
    all_y = jnp.stack([column, send(column, 0, -1, 0), send(column, 0, -2, 0), send(column, 0, -3, 0)])
    everything = jnp.stack([all_y, send(all_y, 0, 0, 1)]).reshape(16 * KROWS, KCOLS)
    order = jnp.arange(16 * KROWS, dtype=jnp.int32)
    piece, row = order // KROWS, order % KROWS
    held = dp_of(x + piece % 2, y + piece // 2 % 4, c + piece // 8) * KROWS + row
    head = jnp.arange(HD, dtype=jnp.int32)
    goes = jnp.sum(jnp.where(rotary_order[:, None] == head[None, :], head[:, None], 0), axis=0)
    target = held // HD * HD + jnp.sum(
        jnp.where((held % HD)[:, None] == head[None, :], goes[None, :], 0), axis=1
    )
    pick = (target[:, None] == order[None, :]).astype(BF)
    server_key = lax.dot_general(
        everything, pick, (((0,), (0,)), ((), ())), preferred_element_type=F32
    ).astype(BF)
    return (new_ep, new_em, new_es, new_kp, new_km, new_ks, server_expert, server_key)


def solution(mesh):
    return jax.shard_map(
        on_device,
        mesh=mesh,
        in_specs=(
            P("dp", "expert", None, None),
            P("dp", None, "expert"),
            P("expert", "dp", None),
            P("expert", "dp", None),
            P("expert", "dp", None),
            P("dp", "expert"),
            P("dp", "expert"),
            P("dp", "expert"),
            P(),
            P(None, "expert"),
            P(),
            P(),
        ),
        out_specs=(
            P("expert", "dp", None),
            P("expert", "dp", None),
            P("expert", "dp", None),
            P("dp", "expert"),
            P("dp", "expert"),
            P("dp", "expert"),
            P(None, "expert", "dp"),
            P("expert", None),
        ),
        check_vma=False,
    )
```

time: 244 us -> 78.1 us (0.32)
  the two profiles are of different devices: /device:TPU:1 before, /device:TPU:0 now
where the time goes in v2:
time: 78.1 us; the launch traced here: 77.7 us
  starting transfers between devices  29.3 us (38%)
  waiting for transfers between devices  26.2 us (34%)
  Pallas kernels  10.5 us (13%)
  other arithmetic  4.77 us (6%)
  local copies, waits for them, and re-layouts  4.46 us (6%)
  matrix products  1.35 us (2%)
  between operations  1.08 us (1%)
    ppermute x17, starting transfers between devices, send(): return lax.ppermute(value, 'dp', dp_perm(dx, dy, dc))  16.8 us
    ppermute x6, waiting for transfers between devices, ring(): return lax.ppermute(value, 'dp', pairs)  13.2 us
    pallas_call x4, Pallas kernels, load(): pl.pallas_call(functools.partial(load_kernel, groups, len(late)), out_sha...  9.1 us
    ppermute x17, waiting for transfers between devices, send(): return lax.ppermute(value, 'dp', dp_perm(dx, dy, dc))  8.11 us
    all_to_all x1, starting transfers between devices, on_device(): lax.all_to_all(blocks, 'expert', split_axis=0, concat_axis=0, tiled=True)  6.36 us
    ppermute x6, starting transfers between devices, ring(): return lax.ppermute(value, 'dp', pairs)  6.11 us
    all_to_all x1, waiting for transfers between devices, on_device(): lax.all_to_all(blocks, 'expert', split_axis=0, concat_axis=0, tiled=True)  4.9 us
    unnamed x23, local copies, waits for them, and re-layouts  2.71 us
  transfers between devices with their start and end apart: 24, of which 9 were waited for; matrix products, arithmetic and copies ran while one was open for 12% of the time, Pallas kernels for 10%

profile of v2, /device:TPU:0, one launch (start us, length us, event | category | flops | bytes accessed | tf_op | source)
XLA Modules:
  0.0 77.7 jit_solution(306953172621373235)
XLA Ops:
  0.6 2.7 %shard_map.179 = (bf16[1,96,1024]{2,1,0:T(8,128)(2,1)S(1)}, bf16[3,96,1024]{2,1,0:T(8,128)(2,1)}, f32[1,96,1024]{2,1,0:T(8,128)S(1)}, f32[3,96,1024]{2,1,0:T(8,128)S(1)}) custom-call(f32[16,96,2048]{2,1,0:T(8,128)} %bitcast.28, f32[16,32,512]{2,1,0:T(8,128)} %bitcast.32), custom_call_target="tpu_custom_call" | custom-call | flops 1000 | bytes 1000 | tf_op jit(solution)/shard_map/pallas_call | solution.py:145
  3.5 0.5 collective-permute-start.1
  4.0 1.6 %shard_map.180 = (bf16[2,112,1024]{2,1,0:T(8,128)(2,1)S(1)}, f32[2,112,1024]{2,1,0:T(8,128)S(1)}) custom-call(f32[16,96,2048]{2,1,0:T(8,128)} %bitcast.29, f32[16,32,512]{2,1,0:T(8,128)} %bitcast.33, bf16[1,96,1024]{2,1,0:T(8,128)(2,1)S(1)} %get-tuple-element.26.refs_0_), custom_call_target="tpu_custom_call" | custom-call | flops 1000 | bytes 1000 | tf_op jit(solution)/shard_map/pallas_call | solution.py:145
  5.6 0.2 collective-permute-start
  5.7 0.7 fusion.35
  6.7 0.8 %collective-permute-done = bf16[2,112,1024]{2,1,0:T(8,128)(2,1)} collective-permute-done((bf16[2,112,1024]{2,1,0:T(8,128)(2,1)S(1)}, bf16[2,112,1024]{2,1,0:T(8,128)(2,1)}, u32[]{:S(2)}, u32[]{:S(2)}) %collective-permute-start) | collective-permute-done | bytes 458784 | tf_op jit(solution)/shard_map/ppermute | solution.py:47
  7.6 1.1 %add_convert_fusion.3.refs_0_ = bf16[2,112,1024]{2,1,0:T(8,128)(2,1)S(1)} fusion(f32[2,112,1024]{2,1,0:T(8,128)S(1)} %get-tuple-element.27, bf16[2,112,1024]{2,1,0:T(8,128)(2,1)} %collective-permute-done), kind=kLoop, calls=%fused_computation.7 | loop fusion | flops 688128 | bytes 1835008 | tf_op jit(solution)/shard_map/convert_element_type | solution.py:230
  8.7 2.3 %shard_map.181 = (bf16[2,112,1024]{2,1,0:T(8,128)(2,1)S(1)}, bf16[2,112,1024]{2,1,0:T(8,128)(2,1)S(1)}, f32[2,112,1024]{2,1,0:T(8,128)S(1)}, f32[2,112,1024]{2,1,0:T(8,128)S(1)}) custom-call(f32[16,96,2048]{2,1,0:T(8,128)} %bitcast.30, f32[16,32,512]{2,1,0:T(8,128)} %bitcast.34, bf16[2,112,1024]{2,1,0:T(8,128)(2,1)S(1)} %add_convert_fusion.3.refs_0_), custom_call_target="tpu_custom_call" | custom-call | flops 1000 | bytes 1000 | tf_op jit(solution)/shard_map/pallas_call | solution.py:145
  11.0 0.2 collective-permute-start.6
  11.3 1.7 %collective-permute-start.4 = (bf16[2,112,1024]{2,1,0:T(8,128)(2,1)S(1)}, bf16[2,112,1024]{2,1,0:T(8,128)(2,1)S(1)}, u32[]{:S(2)}, u32[]{:S(2)}) collective-permute-start(bf16[2,112,1024]{2,1,0:T(8,128)(2,1)S(1)} %add_convert_fusion.3.refs_0_), channel_id=1, source_target_pairs={{0,16},{8,56},{16,32},{24,8},{32,48},{40,24},{48,0},{56,40},{64,80... | collective-permute-start | bytes 1376264 | tf_op jit(solution)/shard_map/ppermute | solution.py:57
  13.0 1.3 %add_convert_fusion.refs_1_ = bf16[3,96,1024]{2,1,0:T(8,128)(2,1)S(1)} fusion(f32[3,96,1024]{2,1,0:T(8,128)S(1)} %get-tuple-element.30, bf16[3,96,1024]{2,1,0:T(8,128)(2,1)} %collective-permute-done.1), kind=kLoop, calls=%fused_computation.2 | loop fusion | flops 884736 | bytes 2359296 | tf_op jit(solution)/shard_map/convert_element_type | solution.py:232
  14.2 1.6 %collective-permute-start.3 = (bf16[2,112,1024]{2,1,0:T(8,128)(2,1)S(1)}, bf16[2,112,1024]{2,1,0:T(8,128)(2,1)S(1)}, u32[]{:S(2)}, u32[]{:S(2)}) collective-permute-start(bf16[2,112,1024]{2,1,0:T(8,128)(2,1)S(1)} %get-tuple-element.35), channel_id=1, source_target_pairs={{0,8},{8,0},{16,24},{24,16},{32,40},{40,32},{48,56},{56,48},{64,72... | collective-permute-start | bytes 1376264 | tf_op jit(solution)/shard_map/ppermute | solution.py:47
  15.8 2.5 %shard_map.182 = (bf16[4,96,1024]{2,1,0:T(8,128)(2,1)S(1)}, bf16[2,112,1024]{2,1,0:T(8,128)(2,1)S(1)}, f32[4,96,1024]{2,1,0:T(8,128)S(1)}, f32[2,112,1024]{2,1,0:T(8,128)S(1)}) custom-call(f32[16,96,2048]{2,1,0:T(8,128)} %bitcast.31, f32[16,32,512]{2,1,0:T(8,128)} %bitcast.35, bf16[2,112,1024]{2,1,0:T(8,128)(2,1)S(1)} %get-tuple-element.29.refs_0_, ...), custom_call_target="tpu_custom_call" | custom-call | flops 1000 | bytes 1000 | tf_op jit(solution)/shard_map/pallas_call | solution.py:145
  18.4 0.1 collective-permute-start.2
  18.5 0.5 collective-permute-start.10
  19.1 0.2 collective-permute-start.7
  19.4 1.6 %collective-permute-done.4 = bf16[2,112,1024]{2,1,0:T(8,128)(2,1)S(1)} collective-permute-done((bf16[2,112,1024]{2,1,0:T(8,128)(2,1)S(1)}, bf16[2,112,1024]{2,1,0:T(8,128)(2,1)S(1)}, u32[]{:S(2)}, u32[]{:S(2)}) %collective-permute-start.4) | collective-permute-done | bytes 458784 | tf_op jit(solution)/shard_map/ppermute | solution.py:57
  21.0 3.1 %collective-permute-start.15 = (bf16[1,96,1024]{2,1,0:T(8,128)(2,1)S(1)}, bf16[1,96,1024]{2,1,0:T(8,128)(2,1)S(1)}, u32[]{:S(2)}, u32[]{:S(2)}) collective-permute-start(bf16[1,96,1024]{2,1,0:T(8,128)(2,1)S(1)} %add_convert_fusion.6), channel_id=1, source_target_pairs={{0,64},{8,72},{16,80},{24,88},{32,96},{40,104},{48,112},{56,120},{... | collective-permute-start | bytes 589832 | tf_op jit(solution)/shard_map/ppermute | solution.py:47
  24.1 0.4 collective-permute-start.11
  24.5 0.2 add_convert_fusion.2
  24.7 0.5 collective-permute-start.5
  25.2 3.6 %collective-permute-done.7 = bf16[2,112,1024]{2,1,0:T(8,128)(2,1)S(1)} collective-permute-done((bf16[2,112,1024]{2,1,0:T(8,128)(2,1)S(1)}, bf16[2,112,1024]{2,1,0:T(8,128)(2,1)S(1)}, u32[]{:S(2)}, u32[]{:S(2)}) %collective-permute-start.7) | collective-permute-done | bytes 458784 | tf_op jit(solution)/shard_map/ppermute | solution.py:57
  29.0 0.7 collective-permute-done.15
  29.8 1.1 %collective-permute-start.16 = (bf16[1,96,1024]{2,1,0:T(8,128)(2,1)S(1)}, bf16[1,96,1024]{2,1,0:T(8,128)(2,1)S(1)}, u32[]{:S(2)}, u32[]{:S(2)}) collective-permute-start(bf16[1,96,1024]{2,1,0:T(8,128)(2,1)S(1)} %add_convert_fusion.5), channel_id=1, source_target_pairs={{0,16},{8,56},{16,32},{24,8},{32,48},{40,24},{48,0},{56,40},{64,80... | collective-permute-start | bytes 589832 | tf_op jit(solution)/shard_map/ppermute | solution.py:57
  30.9 3.6 %collective-permute-done.5 = bf16[2,112,1024]{2,1,0:T(8,128)(2,1)S(1)} collective-permute-done((bf16[2,112,1024]{2,1,0:T(8,128)(2,1)S(1)}, bf16[2,112,1024]{2,1,0:T(8,128)(2,1)S(1)}, u32[]{:S(2)}, u32[]{:S(2)}) %collective-permute-start.5) | collective-permute-done | bytes 458784 | tf_op jit(solution)/shard_map/ppermute | solution.py:57
  34.6 3.2 %collective-permute-start.9 = (bf16[1,112,1024]{2,1,0:T(8,128)(2,1)S(1)}, bf16[1,112,1024]{2,1,0:T(8,128)(2,1)S(1)}, u32[]{:S(2)}, u32[]{:S(2)}) collective-permute-start(bf16[1,112,1024]{2,1,0:T(8,128)(2,1)S(1)} %fusion.2), channel_id=1, source_target_pairs={{0,64},{8,72},{16,80},{24,88},{32,96},{40,104},{48,112},{56,120},{... | collective-permute-start | bytes 688136 | tf_op jit(solution)/shard_map/ppermute | solution.py:47
  37.8 4.5 %collective-permute-done.11 = bf16[3,96,1024]{2,1,0:T(8,128)(2,1)S(1)} collective-permute-done((bf16[3,96,1024]{2,1,0:T(8,128)(2,1)S(1)}, bf16[3,96,1024]{2,1,0:T(8,128)(2,1)S(1)}, u32[]{:S(2)}, u32[]{:S(2)}) %collective-permute-start.11) | collective-permute-done | bytes 589856 | tf_op jit(solution)/shard_map/ppermute | solution.py:47
  42.3 0.2 add_convert_fusion.7
  42.5 1.1 %collective-permute-start.12 = (bf16[1,96,1024]{2,1,0:T(8,128)(2,1)S(1)}, bf16[1,96,1024]{2,1,0:T(8,128)(2,1)S(1)}, u32[]{:S(2)}, u32[]{:S(2)}) collective-permute-start(bf16[1,96,1024]{2,1,0:T(8,128)(2,1)S(1)} %get-tuple-element.48), channel_id=1, source_target_pairs={{0,16},{8,56},{16,32},{24,8},{32,48},{40,24},{48,0},{56,40},{64,80... | collective-permute-start | bytes 589832 | tf_op jit(solution)/shard_map/ppermute | solution.py:57
  43.7 1.5 %collective-permute-start.17 = (bf16[1,96,1024]{2,1,0:T(8,128)(2,1)S(1)}, bf16[1,96,1024]{2,1,0:T(8,128)(2,1)S(1)}, u32[]{:S(2)}, u32[]{:S(2)}) collective-permute-start(bf16[1,96,1024]{2,1,0:T(8,128)(2,1)S(1)} %get-tuple-element.49), channel_id=1, source_target_pairs={{0,16},{8,56},{16,32},{24,8},{32,48},{40,24},{48,0},{56,40},{64,80... | collective-permute-start | bytes 589832 | tf_op jit(solution)/shard_map/ppermute | solution.py:57
  45.2 4.3 %collective-permute-done.12 = bf16[1,96,1024]{2,1,0:T(8,128)(2,1)S(1)} collective-permute-done((bf16[1,96,1024]{2,1,0:T(8,128)(2,1)S(1)}, bf16[1,96,1024]{2,1,0:T(8,128)(2,1)S(1)}, u32[]{:S(2)}, u32[]{:S(2)}) %collective-permute-start.12) | collective-permute-done | bytes 196640 | tf_op jit(solution)/shard_map/ppermute | solution.py:57
  49.5 0.1 fusion.5.first
  49.7 0.7 clamp_convert_fusion
  50.4 3.8 %collective-permute-start.18 = (bf16[32,512]{1,0:T(8,128)(2,1)S(1)}, bf16[32,512]{1,0:T(8,128)(2,1)S(1)}, u32[]{:S(2)}, u32[]{:S(2)}) collective-permute-start(bf16[32,512]{1,0:T(8,128)(2,1)S(1)} %get-tuple-element.44), channel_id=1, source_target_pairs={{0,64},{8,72},{16,80},{24,88},{32,96},{40,104},{48,112},{56,120},{... | collective-permute-start | bytes 98312 | tf_op jit(solution)/shard_map/ppermute | solution.py:47
  54.2 2.0 %collective-permute-done.18 = bf16[32,512]{1,0:T(8,128)(2,1)S(1)} collective-permute-done((bf16[32,512]{1,0:T(8,128)(2,1)S(1)}, bf16[32,512]{1,0:T(8,128)(2,1)S(1)}, u32[]{:S(2)}, u32[]{:S(2)}) %collective-permute-start.18) | collective-permute-done | bytes 32800 | tf_op jit(solution)/shard_map/ppermute | solution.py:47
  56.2 1.0 %collective-permute-start.20 = (bf16[2,32,512]{2,1,0:T(8,128)(2,1)S(1)}, bf16[2,32,512]{2,1,0:T(8,128)(2,1)S(1)}, u32[]{:S(2)}, u32[]{:S(2)}) collective-permute-start(bf16[2,32,512]{2,1,0:T(8,128)(2,1)S(1)} %get-tuple-element.55), channel_id=1, source_target_pairs={{0,32},{8,40},{16,48},{24,56},{32,0},{40,8},{48,16},{56,24},{64,96... | collective-permute-start | bytes 196616 | tf_op jit(solution)/shard_map/ppermute | solution.py:47
  57.3 1.1 %collective-permute-start.19 = (bf16[2,32,512]{2,1,0:T(8,128)(2,1)S(1)}, bf16[2,32,512]{2,1,0:T(8,128)(2,1)S(1)}, u32[]{:S(2)}, u32[]{:S(2)}) collective-permute-start(bf16[2,32,512]{2,1,0:T(8,128)(2,1)S(1)} %get-tuple-element.55), channel_id=1, source_target_pairs={{0,48},{8,56},{16,0},{24,8},{32,16},{40,24},{48,32},{56,40},{64,11... | collective-permute-start | bytes 196616 | tf_op jit(solution)/shard_map/ppermute | solution.py:47
  58.4 0.9 %collective-permute-start.21 = (bf16[2,32,512]{2,1,0:T(8,128)(2,1)S(1)}, bf16[2,32,512]{2,1,0:T(8,128)(2,1)S(1)}, u32[]{:S(2)}, u32[]{:S(2)}) collective-permute-start(bf16[2,32,512]{2,1,0:T(8,128)(2,1)S(1)} %get-tuple-element.55), channel_id=1, source_target_pairs={{0,16},{8,24},{16,32},{24,40},{32,48},{40,56},{48,0},{56,8},{64,80... | collective-permute-start | bytes 196616 | tf_op jit(solution)/shard_map/ppermute | solution.py:47
  59.3 0.1 add_bitcast_fusion.second
  59.5 1.4 %shard_map.183 = (f32[1,96,2048]{2,1,0:T(8,128)S(1)}, f32[1,96,2048]{2,1,0:T(8,128)S(1)}, f32[1,96,2048]{2,1,0:T(8,128)S(1)}, bf16[8,96,256]{2,1,0:T(8,128)(2,1)}) custom-call(f32[112,1024]{1,0:T(8,128)S(1)} %fusion.5.first, f32[96,1024]{1,0:T(8,128)S(1)} %add_bitcast_fusion.second, f32[1,96,2048]{2,1,0:T(8,128)S(1)} %copy-done.1, ...), custom_call_target="tpu_custom_call" | custom-call | flops 1000 | bytes 1000 | tf_op jit(solution)/shard_map/pallas_call | solution.py:183
  60.9 6.4 %all-to-all-start = ((bf16[8,96,256]{2,1,0:T(8,128)(2,1)}), bf16[8,96,256]{2,1,0:T(8,128)(2,1)S(1)}, u32[]{:S(2)}, u32[]{:S(2)}) async-start(bf16[8,96,256]{2,1,0:T(8,128)(2,1)} %get-tuple-element.43), calls=%async_computation | async-start | bytes 786432 | tf_op jit(solution)/shard_map/all_to_all | solution.py:261
  67.5 0.2 select_reduce_fusion
  67.7 0.9 %copy.21 = f32[1,96,2048]{2,1,0:T(8,128)} copy(f32[1,96,2048]{2,1,0:T(8,128)S(1)} %get-tuple-element.58) | data formatting | bytes 1572864
  68.6 0.9 %copy.22 = f32[1,96,2048]{2,1,0:T(8,128)} copy(f32[1,96,2048]{2,1,0:T(8,128)S(1)} %get-tuple-element.59) | data formatting | bytes 1572864
  69.5 0.9 %copy.23 = f32[1,96,2048]{2,1,0:T(8,128)} copy(f32[1,96,2048]{2,1,0:T(8,128)S(1)} %get-tuple-element.60) | data formatting | bytes 1572864
  70.4 4.9 %all-to-all-done = bf16[8,96,256]{2,1,0:T(8,128)(2,1)S(1)} async-done(((bf16[8,96,256]{2,1,0:T(8,128)(2,1)}), bf16[8,96,256]{2,1,0:T(8,128)(2,1)S(1)}, u32[]{:S(2)}, u32[]{:S(2)}) %all-to-all-start) | async-done | bytes 393248 | tf_op jit(solution)/shard_map/all_to_all | solution.py:261
  75.3 0.9 %scatter_fusion = bf16[8,96,256]{2,1,0:T(8,128)(2,1)S(1)} fusion(bf16[8,96,256]{2,1,0:T(8,128)(2,1)S(1)} %broadcast_in_dim.77, s32[8]{0:T(128)S(1)} %compare_select_fusion, bf16[8,96,256]{2,1,0:T(8,128)(2,1)S(1)} %all-to-all-done), kind=kCustom, calls=%fused_computation | custom fusion | bytes 1179680 | tf_op jit(solution)/shard_map/scatter | solution.py:262
  76.3 1.4 %convolution_convert_fusion = bf16[512,512]{1,0:T(8,128)(2,1)} fusion(bf16[512,512]{1,0:T(8,128)(2,1)S(1)} %bitcast.37, s32[512]{0:T(512)S(1)} %fusion.26), kind=kOutput, calls=%fused_computation.1 | convolution fusion | flops 268959744 | bytes 1050624 | tf_op jit(solution)/shard_map/dot_general | solution.py:282
  (57 shorter events, 1.2 us)
Async XLA Ops:
  0.6 6.1 %copy-start = (f32[4,4]{1,0:T(4,128)S(1)}, f32[4,4]{1,0:T(4,128)}, u32[]{:S(2)}) copy-start(f32[4,4]{1,0:T(4,128)} %param.22) | copy-start | bytes 196
  3.4 15.7 %collective-permute-start.14 = (bf16[1,96,1024]{2,1,0:T(8,128)(2,1)S(1)}, bf16[1,96,1024]{2,1,0:T(8,128)(2,1)S(1)}, u32[]{:S(2)}, u32[]{:S(2)}) collective-permute-start(bf16[1,96,1024]{2,1,0:T(8,128)(2,1)S(1)} %get-tuple-element.26.refs_0_), channel_id=1, source_target_pairs={{0,8},{8,0},{16,24},{24,16},{32,40},{40,32},{48,56},{56,48},{64,72... | collective-permute-start | bytes 589832 | tf_op jit(solution)/shard_map/ppermute | solution.py:47
  3.5 3.0 %copy-start.8 = (s32[128]{0:T(128)S(1)}, s32[128]{0:T(128)}, u32[]{:S(2)}) copy-start(s32[128]{0:T(128)} %param.23) | copy-start | bytes 1540
  3.5 9.4 %collective-permute-start.1 = (bf16[3,96,1024]{2,1,0:T(8,128)(2,1)}, bf16[3,96,1024]{2,1,0:T(8,128)(2,1)}, u32[]{:S(2)}, u32[]{:S(2)}) collective-permute-start(bf16[3,96,1024]{2,1,0:T(8,128)(2,1)} %get-tuple-element.31), channel_id=1, source_target_pairs={{0,8},{8,0},{16,24},{24,16},{32,40},{40,32},{48,56},{56,48},{64,72... | collective-permute-start | bytes 1769480 | tf_op jit(solution)/shard_map/ppermute | solution.py:47
  5.6 2.0 %collective-permute-start = (bf16[2,112,1024]{2,1,0:T(8,128)(2,1)S(1)}, bf16[2,112,1024]{2,1,0:T(8,128)(2,1)}, u32[]{:S(2)}, u32[]{:S(2)}) collective-permute-start(bf16[2,112,1024]{2,1,0:T(8,128)(2,1)S(1)} %get-tuple-element.28), channel_id=1, source_target_pairs={{0,8},{8,0},{16,24},{24,16},{32,40},{40,32},{48,56},{56,48},{64,72... | collective-permute-start | bytes 1376264 | tf_op jit(solution)/shard_map/ppermute | solution.py:47
  11.0 7.5 %collective-permute-start.6 = (bf16[2,112,1024]{2,1,0:T(8,128)(2,1)S(1)}, bf16[2,112,1024]{2,1,0:T(8,128)(2,1)S(1)}, u32[]{:S(2)}, u32[]{:S(2)}) collective-permute-start(bf16[2,112,1024]{2,1,0:T(8,128)(2,1)S(1)} %get-tuple-element.29.refs_0_), channel_id=1, source_target_pairs={{0,8},{8,0},{16,24},{24,16},{32,40},{40,32},{48,56},{56,48},{64,72... | collective-permute-start | bytes 1376264 | tf_op jit(solution)/shard_map/ppermute | solution.py:47
  11.3 9.7 %collective-permute-start.4 = (bf16[2,112,1024]{2,1,0:T(8,128)(2,1)S(1)}, bf16[2,112,1024]{2,1,0:T(8,128)(2,1)S(1)}, u32[]{:S(2)}, u32[]{:S(2)}) collective-permute-start(bf16[2,112,1024]{2,1,0:T(8,128)(2,1)S(1)} %add_convert_fusion.3.refs_0_), channel_id=1, source_target_pairs={{0,16},{8,56},{16,32},{24,8},{32,48},{40,24},{48,0},{56,40},{64,80... | collective-permute-start | bytes 1376264 | tf_op jit(solution)/shard_map/ppermute | solution.py:57
  14.2 9.9 %collective-permute-start.3 = (bf16[2,112,1024]{2,1,0:T(8,128)(2,1)S(1)}, bf16[2,112,1024]{2,1,0:T(8,128)(2,1)S(1)}, u32[]{:S(2)}, u32[]{:S(2)}) collective-permute-start(bf16[2,112,1024]{2,1,0:T(8,128)(2,1)S(1)} %get-tuple-element.35), channel_id=1, source_target_pairs={{0,8},{8,0},{16,24},{24,16},{32,40},{40,32},{48,56},{56,48},{64,72... | collective-permute-start | bytes 1376264 | tf_op jit(solution)/shard_map/ppermute | solution.py:47
  18.4 6.3 %collective-permute-start.2 = (bf16[2,112,1024]{2,1,0:T(8,128)(2,1)S(1)}, bf16[2,112,1024]{2,1,0:T(8,128)(2,1)S(1)}, u32[]{:S(2)}, u32[]{:S(2)}) collective-permute-start(bf16[2,112,1024]{2,1,0:T(8,128)(2,1)S(1)} %get-tuple-element.33), channel_id=1, source_target_pairs={{0,8},{8,0},{16,24},{24,16},{32,40},{40,32},{48,56},{56,48},{64,72... | collective-permute-start | bytes 1376264 | tf_op jit(solution)/shard_map/ppermute | solution.py:47
  18.5 11.2 %collective-permute-start.10 = (bf16[4,96,1024]{2,1,0:T(8,128)(2,1)S(1)}, bf16[4,96,1024]{2,1,0:T(8,128)(2,1)S(1)}, u32[]{:S(2)}, u32[]{:S(2)}) collective-permute-start(bf16[4,96,1024]{2,1,0:T(8,128)(2,1)S(1)} %get-tuple-element.38), channel_id=1, source_target_pairs={{0,8},{8,0},{16,24},{24,16},{32,40},{40,32},{48,56},{56,48},{64,72... | collective-permute-start | bytes 2359304 | tf_op jit(solution)/shard_map/ppermute | solution.py:47
  19.1 9.8 %collective-permute-start.7 = (bf16[2,112,1024]{2,1,0:T(8,128)(2,1)S(1)}, bf16[2,112,1024]{2,1,0:T(8,128)(2,1)S(1)}, u32[]{:S(2)}, u32[]{:S(2)}) collective-permute-start(bf16[2,112,1024]{2,1,0:T(8,128)(2,1)S(1)} %add_convert_fusion.1), channel_id=1, source_target_pairs={{0,16},{8,56},{16,32},{24,8},{32,48},{40,24},{48,0},{56,40},{64,80... | collective-permute-start | bytes 1376264 | tf_op jit(solution)/shard_map/ppermute | solution.py:57
  21.0 8.7 %collective-permute-start.15 = (bf16[1,96,1024]{2,1,0:T(8,128)(2,1)S(1)}, bf16[1,96,1024]{2,1,0:T(8,128)(2,1)S(1)}, u32[]{:S(2)}, u32[]{:S(2)}) collective-permute-start(bf16[1,96,1024]{2,1,0:T(8,128)(2,1)S(1)} %add_convert_fusion.6), channel_id=1, source_target_pairs={{0,64},{8,72},{16,80},{24,88},{32,96},{40,104},{48,112},{56,120},{... | collective-permute-start | bytes 589832 | tf_op jit(solution)/shard_map/ppermute | solution.py:47
  24.1 18.2 %collective-permute-start.11 = (bf16[3,96,1024]{2,1,0:T(8,128)(2,1)S(1)}, bf16[3,96,1024]{2,1,0:T(8,128)(2,1)S(1)}, u32[]{:S(2)}, u32[]{:S(2)}) collective-permute-start(bf16[3,96,1024]{2,1,0:T(8,128)(2,1)S(1)} %add_convert_fusion.refs_1_), channel_id=1, source_target_pairs={{0,64},{8,72},{16,80},{24,88},{32,96},{40,104},{48,112},{56,120},{... | collective-permute-start | bytes 1769480 | tf_op jit(solution)/shard_map/ppermute | solution.py:47
  24.7 9.8 %collective-permute-start.5 = (bf16[2,112,1024]{2,1,0:T(8,128)(2,1)S(1)}, bf16[2,112,1024]{2,1,0:T(8,128)(2,1)S(1)}, u32[]{:S(2)}, u32[]{:S(2)}) collective-permute-start(bf16[2,112,1024]{2,1,0:T(8,128)(2,1)S(1)} %add_convert_fusion.2), channel_id=1, source_target_pairs={{0,16},{8,56},{16,32},{24,8},{32,48},{40,24},{48,0},{56,40},{64,80... | collective-permute-start | bytes 1376264 | tf_op jit(solution)/shard_map/ppermute | solution.py:57
  28.9 5.6 %collective-permute-start.8 = (bf16[2,112,1024]{2,1,0:T(8,128)(2,1)S(1)}, bf16[2,112,1024]{2,1,0:T(8,128)(2,1)S(1)}, u32[]{:S(2)}, u32[]{:S(2)}) collective-permute-start(bf16[2,112,1024]{2,1,0:T(8,128)(2,1)S(1)} %collective-permute-done.7), channel_id=1, source_target_pairs={{0,8},{8,0},{16,24},{24,16},{32,40},{40,32},{48,56},{56,48},{64,72... | collective-permute-start | bytes 1376264 | tf_op jit(solution)/shard_map/ppermute | solution.py:47
  29.8 13.9 %copy-start.9 = (s32[8]{0:T(128)S(1)}, s32[8]{0:T(128)}, u32[]{:S(2)}) copy-start(s32[8]{0:T(128)} %param.24) | copy-start | bytes 100
  29.8 12.6 %collective-permute-start.16 = (bf16[1,96,1024]{2,1,0:T(8,128)(2,1)S(1)}, bf16[1,96,1024]{2,1,0:T(8,128)(2,1)S(1)}, u32[]{:S(2)}, u32[]{:S(2)}) collective-permute-start(bf16[1,96,1024]{2,1,0:T(8,128)(2,1)S(1)} %add_convert_fusion.5), channel_id=1, source_target_pairs={{0,16},{8,56},{16,32},{24,8},{32,48},{40,24},{48,0},{56,40},{64,80... | collective-permute-start | bytes 589832 | tf_op jit(solution)/shard_map/ppermute | solution.py:57
  34.6 15.1 %copy-start.5 = (f32[32,512]{1,0:T(8,128)S(1)}, f32[32,512]{1,0:T(8,128)}, u32[]{:S(2)}) copy-start(f32[32,512]{1,0:T(8,128)} %param.18) | copy-start | bytes 196612
  34.6 15.1 %copy-start.6 = (f32[32,512]{1,0:T(8,128)S(1)}, f32[32,512]{1,0:T(8,128)}, u32[]{:S(2)}) copy-start(f32[32,512]{1,0:T(8,128)} %param.19) | copy-start | bytes 196612
  34.6 15.1 %copy-start.7 = (f32[32,512]{1,0:T(8,128)S(1)}, f32[32,512]{1,0:T(8,128)}, u32[]{:S(2)}) copy-start(f32[32,512]{1,0:T(8,128)} %param.20) | copy-start | bytes 196612
  34.6 14.9 %collective-permute-start.9 = (bf16[1,112,1024]{2,1,0:T(8,128)(2,1)S(1)}, bf16[1,112,1024]{2,1,0:T(8,128)(2,1)S(1)}, u32[]{:S(2)}, u32[]{:S(2)}) collective-permute-start(bf16[1,112,1024]{2,1,0:T(8,128)(2,1)S(1)} %fusion.2), channel_id=1, source_target_pairs={{0,64},{8,72},{16,80},{24,88},{32,96},{40,104},{48,112},{56,120},{... | collective-permute-start | bytes 688136 | tf_op jit(solution)/shard_map/ppermute | solution.py:47
  42.5 6.9 %collective-permute-start.12 = (bf16[1,96,1024]{2,1,0:T(8,128)(2,1)S(1)}, bf16[1,96,1024]{2,1,0:T(8,128)(2,1)S(1)}, u32[]{:S(2)}, u32[]{:S(2)}) collective-permute-start(bf16[1,96,1024]{2,1,0:T(8,128)(2,1)S(1)} %get-tuple-element.48), channel_id=1, source_target_pairs={{0,16},{8,56},{16,32},{24,8},{32,48},{40,24},{48,0},{56,40},{64,80... | collective-permute-start | bytes 589832 | tf_op jit(solution)/shard_map/ppermute | solution.py:57
  43.7 15.7 %collective-permute-start.17 = (bf16[1,96,1024]{2,1,0:T(8,128)(2,1)S(1)}, bf16[1,96,1024]{2,1,0:T(8,128)(2,1)S(1)}, u32[]{:S(2)}, u32[]{:S(2)}) collective-permute-start(bf16[1,96,1024]{2,1,0:T(8,128)(2,1)S(1)} %get-tuple-element.49), channel_id=1, source_target_pairs={{0,16},{8,56},{16,32},{24,8},{32,48},{40,24},{48,0},{56,40},{64,80... | collective-permute-start | bytes 589832 | tf_op jit(solution)/shard_map/ppermute | solution.py:57
  49.5 9.8 %collective-permute-start.13 = (bf16[1,96,1024]{2,1,0:T(8,128)(2,1)S(1)}, bf16[1,96,1024]{2,1,0:T(8,128)(2,1)S(1)}, u32[]{:S(2)}, u32[]{:S(2)}) collective-permute-start(bf16[1,96,1024]{2,1,0:T(8,128)(2,1)S(1)} %collective-permute-done.12), channel_id=1, source_target_pairs={{0,8},{8,0},{16,24},{24,16},{32,40},{40,32},{48,56},{56,48},{64,72... | collective-permute-start | bytes 589832 | tf_op jit(solution)/shard_map/ppermute | solution.py:47
  49.6 9.8 %copy-start.1 = (f32[1,96,2048]{2,1,0:T(8,128)S(1)}, f32[1,96,2048]{2,1,0:T(8,128)}, u32[]{:S(2)}) copy-start(f32[1,96,2048]{2,1,0:T(8,128)} %param.25) | copy-start | bytes 2359300
  49.6 9.8 %copy-start.2 = (f32[1,96,2048]{2,1,0:T(8,128)S(1)}, f32[1,96,2048]{2,1,0:T(8,128)}, u32[]{:S(2)}) copy-start(f32[1,96,2048]{2,1,0:T(8,128)} %moment.1) | copy-start | bytes 2359300
  49.7 9.8 %copy-start.3 = (f32[1,96,2048]{2,1,0:T(8,128)S(1)}, f32[1,96,2048]{2,1,0:T(8,128)}, u32[]{:S(2)}) copy-start(f32[1,96,2048]{2,1,0:T(8,128)} %variance.1) | copy-start | bytes 2359300
  50.4 5.8 %collective-permute-start.18 = (bf16[32,512]{1,0:T(8,128)(2,1)S(1)}, bf16[32,512]{1,0:T(8,128)(2,1)S(1)}, u32[]{:S(2)}, u32[]{:S(2)}) collective-permute-start(bf16[32,512]{1,0:T(8,128)(2,1)S(1)} %get-tuple-element.44), channel_id=1, source_target_pairs={{0,64},{8,72},{16,80},{24,88},{32,96},{40,104},{48,112},{56,120},{... | collective-permute-start | bytes 98312 | tf_op jit(solution)/shard_map/ppermute | solution.py:47
  56.2 11.1 %collective-permute-start.20 = (bf16[2,32,512]{2,1,0:T(8,128)(2,1)S(1)}, bf16[2,32,512]{2,1,0:T(8,128)(2,1)S(1)}, u32[]{:S(2)}, u32[]{:S(2)}) collective-permute-start(bf16[2,32,512]{2,1,0:T(8,128)(2,1)S(1)} %get-tuple-element.55), channel_id=1, source_target_pairs={{0,32},{8,40},{16,48},{24,56},{32,0},{40,8},{48,16},{56,24},{64,96... | collective-permute-start | bytes 196616 | tf_op jit(solution)/shard_map/ppermute | solution.py:47
  57.3 10.0 %collective-permute-start.19 = (bf16[2,32,512]{2,1,0:T(8,128)(2,1)S(1)}, bf16[2,32,512]{2,1,0:T(8,128)(2,1)S(1)}, u32[]{:S(2)}, u32[]{:S(2)}) collective-permute-start(bf16[2,32,512]{2,1,0:T(8,128)(2,1)S(1)} %get-tuple-element.55), channel_id=1, source_target_pairs={{0,48},{8,56},{16,0},{24,8},{32,16},{40,24},{48,32},{56,40},{64,11... | collective-permute-start | bytes 196616 | tf_op jit(solution)/shard_map/ppermute | solution.py:47
  58.4 8.9 %collective-permute-start.21 = (bf16[2,32,512]{2,1,0:T(8,128)(2,1)S(1)}, bf16[2,32,512]{2,1,0:T(8,128)(2,1)S(1)}, u32[]{:S(2)}, u32[]{:S(2)}) collective-permute-start(bf16[2,32,512]{2,1,0:T(8,128)(2,1)S(1)} %get-tuple-element.55), channel_id=1, source_target_pairs={{0,16},{8,24},{16,32},{24,40},{32,48},{40,56},{48,0},{56,8},{64,80... | collective-permute-start | bytes 196616 | tf_op jit(solution)/shard_map/ppermute | solution.py:47
  60.9 14.3 %all-to-all-start = ((bf16[8,96,256]{2,1,0:T(8,128)(2,1)}), bf16[8,96,256]{2,1,0:T(8,128)(2,1)S(1)}, u32[]{:S(2)}, u32[]{:S(2)}) async-start(bf16[8,96,256]{2,1,0:T(8,128)(2,1)} %get-tuple-element.43), calls=%async_computation | async-start | bytes 786432 | tf_op jit(solution)/shard_map/all_to_all | solution.py:261
  67.4 8.9 %collective-permute-start.22 = (bf16[4,2,32,512]{3,2,1,0:T(8,128)(2,1)S(1)}, bf16[4,2,32,512]{3,2,1,0:T(8,128)(2,1)S(1)}, u32[]{:S(2)}, u32[]{:S(2)}) collective-permute-start(bf16[4,2,32,512]{3,2,1,0:T(8,128)(2,1)S(1)} %get-tuple-element.53), channel_id=1, source_target_pairs={{0,8},{8,0},{16,24},{24,16},{32,40},{40,32},{48,56},{56,48},{64,72... | collective-permute-start | bytes 786440 | tf_op jit(solution)/shard_map/ppermute | solution.py:47
  76.2 1.4 %copy-start.4 = (bf16[8,96,256]{2,1,0:T(8,128)(2,1)}, bf16[8,96,256]{2,1,0:T(8,128)(2,1)S(1)}, u32[]{:S(2)}) copy-start(bf16[8,96,256]{2,1,0:T(8,128)(2,1)S(1)} %scatter_fusion) | copy-start | bytes 1179652

commit v3 on v0

v3 whole, which is shorter than its diff:
```python
import functools

import jax
import jax.numpy as jnp
from jax import lax
from jax.experimental import pallas as pl
from jax.experimental.pallas import tpu as pltpu
from jax.sharding import PartitionSpec as P

HD = 128
BLOCK = 128

BETA_ONE = 0.9
BETA_TWO = 0.95
LEARN = 0.01
DECAY = 0.1
EPSILON = 1e-08
LIMIT = 448.0
CORRECT_ONE = 1.0 - 0.9**10
CORRECT_TWO = 1.0 - 0.95**10

ROWS = 96
KROWS = 32
HALF = 1024
KCOLS = 512
FOLD = 2 * ROWS
KFOLD = 16

BF = jnp.bfloat16
F32 = jnp.float32
VMEM_BYTES = 7 * 1024 * 1024
SLOTS = 6


def dp_of(x, y, c):
    return ((x % 2) * 4 + (y % 4)) * 2 + c % 2


def dp_perm(dx, dy, dc):
    return [
        (dp_of(x, y, c), dp_of(x + dx, y + dy, c + dc))
        for x in range(2)
        for y in range(4)
        for c in range(2)
    ]


def send(value, dx, dy, dc):
    return lax.ppermute(value, "dp", dp_perm(dx, dy, dc))


def ring(value):
    pairs = [
        (dp_of(x, y, c), dp_of(x, y + 1 - 2 * c, c))
        for x in range(2)
        for y in range(4)
        for c in range(2)
    ]
    return lax.ppermute(value, "dp", pairs)


def after(value, *earlier):
    return lax.optimization_barrier((value, *earlier))[0]


def adam_update(param, moment, second, grad):
    moment = BETA_ONE * moment + (1.0 - BETA_ONE) * grad
    second = BETA_TWO * second + (1.0 - BETA_TWO) * grad * grad
    corrected = moment / CORRECT_ONE / (jnp.sqrt(second / CORRECT_TWO) + EPSILON)
    return (param * (1.0 - LEARN * DECAY) - LEARN * corrected, moment, second)


def to_grid(weights, scales):
    return jnp.clip(weights / scales, -LIMIT, LIMIT).astype(BF)


def owner(role, dx, x, y, c):
    step = {"far": 2, "near": 1 - 2 * c, "plain": 1 - 2 * c, "own": 0}[role]
    return dp_of(x + dx, y + 4 + step, 1 - c if role == "plain" else c)


def parts_of(batch, role, x, y, c, ep, kp, out):
    block = owner(role, 1 if batch == "turn" else 0, x, y, c)
    parts = [
        (ep.at[block, :, pl.ds(half * HALF, HALF)], out.at[pl.ds(half * ROWS, ROWS)])
        for half in range(2)
    ]
    if batch == "turn":
        for place, dx in enumerate((1, 0)):
            block = owner(role, dx, x, y, c)
            target = out.at[pl.ds(FOLD + place * KFOLD, KFOLD)]
            parts += [
                (kp.at[block, pl.ds(part * KFOLD, KFOLD)], target.at[:, pl.ds(part * KCOLS, KCOLS)])
                for part in range(2)
            ]
    return parts


def rows_of(batch):
    return FOLD + 2 * KFOLD if batch == "turn" else FOLD


def load_kernel(batch, roles, n_late, ep, kp, *refs):
    refs = refs[n_late:]
    n = len(roles)
    casts, keeps, buffer, sems = refs[:n], refs[n : 2 * n], refs[2 * n], refs[2 * n + 1]
    dp_index = lax.axis_index("dp")
    x, y, c = dp_index // 8, dp_index // 2 % 4, dp_index % 2
    work = [(role, 1 - c, out) for role, out in zip(roles, casts)]
    work += [(role, c, out) for role, out in zip(roles, keeps)]

    def start(index):
        role, core, _ = work[index]
        slot = index % SLOTS
        copies = [
            pltpu.make_async_copy(source, target, sems.at[slot, number])
            for number, (source, target) in enumerate(
                parts_of(batch, role, x, y, core, ep, kp, buffer.at[slot])
            )
        ]
        for copy in copies:
            copy.start()
        return copies

    flying = [start(index) for index in range(min(SLOTS, len(work)))]
    for index, (_, _, out) in enumerate(work):
        for copy in flying[index]:
            copy.wait()
        slot = index % SLOTS

        def rows(step, carry):
            some = pl.ds(pl.multiple_of(step * 16, 16), 16)
            out[0, some] = buffer[slot, some].astype(BF)
            return carry

        lax.fori_loop(0, rows_of(batch) // 16, rows, 0)
        if index + SLOTS < len(work):
            flying.append(start(index + SLOTS))


def load(ep, kp, batch, roles, late=()):
    shape = (1, rows_of(batch), HALF)
    vmem = pl.BlockSpec(memory_space=pltpu.VMEM)
    hbm = pl.BlockSpec(memory_space=pltpu.HBM)
    anywhere = pl.BlockSpec(memory_space=pl.ANY)
    out = pl.pallas_call(
        functools.partial(load_kernel, batch, roles, len(late)),
        out_shape=[jax.ShapeDtypeStruct(shape, BF)] * (2 * len(roles)),
        in_specs=[hbm, hbm] + [anywhere] * len(late),
        out_specs=[vmem] * (2 * len(roles)),
        scratch_shapes=[
            pltpu.VMEM((SLOTS,) + shape[1:], F32),
            pltpu.SemaphoreType.DMA((SLOTS, 6)),
        ],
        compiler_params=pltpu.CompilerParams(vmem_limit_bytes=VMEM_BYTES),
        cost_estimate=pl.CostEstimate(flops=1000, bytes_accessed=1000, transcendentals=0),
    )(ep, kp, *late)
    return out[: len(roles)], out[len(roles) :]


def plus(*values):
    total = values[0].astype(F32)
    for value in values[1:]:
        total = total + value.astype(F32)
    return total


def update_kernel(*refs):
    terms, (param, moment, variance, scales), results, grid = refs[:4], refs[4:8], refs[8:11], refs[11]
    start = lax.axis_index("dp") * ROWS
    low = start // BLOCK
    expert = lax.axis_index("expert")
    row = lax.broadcasted_iota(jnp.int32, (ROWS, 16), 0) + start
    row_scales = jnp.where(
        row < (low + 1) * BLOCK,
        scales[expert, pl.ds(low, 1), :],
        scales[expert, pl.ds(jnp.minimum(low + 1, 11), 1), :],
    )
    for j in range(8):
        for h in range(2):
            k = 2 * j + h
            columns = pl.ds(k * BLOCK, BLOCK)
            held = pl.ds(k % 8 * BLOCK, BLOCK)
            rows = pl.ds(k // 8 * ROWS, ROWS)
            grad = terms[0][0, rows, held].astype(F32)
            for term in terms[1:]:
                grad = grad + term[0, rows, held].astype(F32)
            new = adam_update(param[0, :, columns], moment[0, :, columns], variance[0, :, columns], grad)
            for result, value in zip(results, new):
                result[0, :, columns] = value
            grid[j, :, pl.ds(h * BLOCK, BLOCK)] = to_grid(new[0], row_scales[:, k : k + 1])


def key_kernel(own, arrived, param, moment, variance, scales, *results):
    quarter = lax.axis_index("dp") * KROWS // BLOCK
    row_scales = scales[pl.ds(quarter, 1), :]
    for part in range(2):
        rows = pl.ds(part * KFOLD, KFOLD)
        for k in range(KCOLS // BLOCK):
            columns = pl.ds(k * BLOCK, BLOCK)
            held = pl.ds(part * KCOLS + k * BLOCK, BLOCK)
            grad = own[0, FOLD + KFOLD :, held] + arrived[0, FOLD:, held].astype(F32)
            new = adam_update(param[rows, columns], moment[rows, columns], variance[rows, columns], grad)
            for result, value in zip(results, new):
                result[rows, columns] = value
            results[3][rows, columns] = to_grid(new[0], row_scales[:, k : k + 1])


def update(kernel, terms, param, moment, variance, scales, grid_shape):
    vmem = pl.BlockSpec(memory_space=pltpu.VMEM)
    near = lambda v: pltpu.with_memory_space_constraint(v, pltpu.VMEM)
    return pl.pallas_call(
        kernel,
        out_shape=[pltpu.VMEM(param.shape, F32)] * 3 + [jax.ShapeDtypeStruct(grid_shape, BF)],
        in_specs=[vmem] * (len(terms) + 4),
        out_specs=[vmem] * 4,
        compiler_params=pltpu.CompilerParams(vmem_limit_bytes=VMEM_BYTES),
        cost_estimate=pl.CostEstimate(flops=1000, bytes_accessed=1000, transcendentals=0),
    )(*terms, near(param), near(moment), near(variance), scales)


def on_device(
    expert_partials,
    key_partials,
    expert_param,
    expert_moment,
    expert_second,
    key_param,
    key_moment,
    key_second,
    expert_scales,
    key_scales,
    rotary_order,
    expert_slot,
):
    dp_index = lax.axis_index("dp")
    x, y, c = dp_index // 8, dp_index // 2 % 4, dp_index % 2
    expert_partials, x, y, c = lax.optimization_barrier((expert_partials, x, y, c))
    ep = pltpu.with_memory_space_constraint(expert_partials.reshape(16, ROWS, 2 * HALF), pltpu.HBM)
    kp = pltpu.with_memory_space_constraint(key_partials.reshape(16, KROWS, KCOLS), pltpu.HBM)

    across = lambda values: [send(value, 0, 0, 1) for value in values]
    casts, keeps = load(ep, kp, "turn", ["far", "plain"])
    got = across(casts)
    casts_b, keeps_b = load(ep, kp, "turn", ["near", "own"], late=(casts[0],))
    got_b = across(casts_b)
    casts_c, keeps_c = load(ep, kp, "stay", ["far", "plain", "near", "own"], late=(casts_b[0],))
    got_c = across(casts_c)
    far = ring(plus(keeps[0], got[0]).astype(BF))
    plain = ring(plus(keeps[1], got[1]).astype(BF))
    near = ring(plus(keeps_b[0], got_b[0], far).astype(BF))
    cross = send(plain, 0, 0, 1)
    far_c = ring(plus(keeps_c[0], got_c[0]).astype(BF))
    plain_c = ring(plus(keeps_c[1], got_c[1]).astype(BF))
    turned = plus(keeps_b[1], got_b[1], cross, near)
    x_last = send(turned[:, : FOLD + KFOLD].astype(BF), 1, 0, 0)
    near_c = ring(plus(keeps_c[2], got_c[2], far_c).astype(BF))
    cross_c = send(plain_c, 0, 0, 1)
    stayed = plus(keeps_c[3], got_c[3]).astype(BF)
    new_ep, new_em, new_es, blocks = update(
        update_kernel,
        (stayed, cross_c, near_c, x_last),
        expert_param,
        expert_moment,
        expert_second,
        expert_scales,
        (8, ROWS, 256),
    )
    arrived = lax.all_to_all(blocks, "expert", split_axis=0, concat_axis=0, tiled=True)
    placed = jnp.zeros_like(arrived).at[expert_slot].set(arrived)
    server_expert = jnp.transpose(placed, (0, 2, 1))

    new_kp, new_km, new_ks, key_grid = update(
        key_kernel,
        (turned, x_last),
        key_param,
        key_moment,
        key_second,
        key_scales,
        (KROWS, KCOLS),
    )
    chip_x = send(after(key_grid, far_c), 1, 0, 0)
    column = after(jnp.stack([key_grid, chip_x]), near_c)
    all_y = jnp.stack([column, send(column, 0, -1, 0), send(column, 0, -2, 0), send(column, 0, -3, 0)])
    everything = jnp.stack([all_y, send(all_y, 0, 0, 1)]).reshape(16 * KROWS, KCOLS)
    order = jnp.arange(16 * KROWS, dtype=jnp.int32)
    piece, row = order // KROWS, order % KROWS
    held = dp_of(x + piece % 2, y + piece // 2 % 4, c + piece // 8) * KROWS + row
    head = jnp.arange(HD, dtype=jnp.int32)
    goes = jnp.sum(jnp.where(rotary_order[:, None] == head[None, :], head[:, None], 0), axis=0)
    target = held // HD * HD + jnp.sum(
        jnp.where((held % HD)[:, None] == head[None, :], goes[None, :], 0), axis=1
    )
    pick = (target[:, None] == order[None, :]).astype(BF)
    server_key = lax.dot_general(
        everything, pick, (((0,), (0,)), ((), ())), preferred_element_type=F32
    ).astype(BF)
    return (new_ep, new_em, new_es, new_kp, new_km, new_ks, server_expert, server_key)


def solution(mesh):
    return jax.shard_map(
        on_device,
        mesh=mesh,
        in_specs=(
            P("dp", "expert", None, None),
            P("dp", None, "expert"),
            P("expert", "dp", None),
            P("expert", "dp", None),
            P("expert", "dp", None),
            P("dp", "expert"),
            P("dp", "expert"),
            P("dp", "expert"),
            P(),
            P(None, "expert"),
            P(),
            P(),
        ),
        out_specs=(
            P("expert", "dp", None),
            P("expert", "dp", None),
            P("expert", "dp", None),
            P("dp", "expert"),
            P("dp", "expert"),
            P("dp", "expert"),
            P(None, "expert", "dp"),
            P("expert", None),
        ),
        check_vma=False,
    )
```

time: 244 us -> 69.6 us (0.29)
  waiting for transfers between devices: 136 us -> 10.6 us
  local copies, waits for them, and re-layouts: 77.7 us -> 6.25 us
  starting transfers between devices: 4.41 us -> 35 us
  between operations: 14 us -> 1.08 us
  Pallas kernels: 0 us -> 10.1 us
  other arithmetic: 10 us -> 3.94 us
    unnamed x4 -> x0, waiting for transfers between devices: 82.3 us -> none
    unnamed x34 -> x35, local copies, waits for them, and re-layouts: 67.1 us -> 5.24 us
    all_gather x1 -> x0, waiting for transfers between devices: 37.2 us -> none  [on_device(): gathered = lax.all_gather(new_kp, 'dp', axis=0, tiled=True)]
    ppermute x0 -> x22, starting transfers between devices: none -> 29 us  [the longest x16 18.1 us: send(): return lax.ppermute(value, 'dp', dp_perm(dx, dy, dc))]
    reduce_scatter x1 -> x0, waiting for transfers between devices: 16.8 us -> none  [on_device(): lax.psum_scatter(key_partials.astype(jnp.bfloat16), 'dp', scatter_dimensi...]
    ppermute x0 -> x22, waiting for transfers between devices: none -> 10.6 us  [the longest x16 6.69 us: send(): return lax.ppermute(value, 'dp', dp_perm(dx, dy, dc))]
    pallas_call x0 -> x5, Pallas kernels: none -> 10.1 us  [the longest x3 8.32 us: load(): pl.pallas_call(functools.partial(load_kernel, batch, roles, len(late)), o...]
    gather x3 -> x0, local copies, waits for them, and re-layouts: 6.67 us -> none  [the longest x1 3.35 us: on_device(): source = all_rows // HD * HD + rotary_order[all_rows % HD]]
  transfers between devices with their start and end apart: 4 -> 23, of which waited for: 3 -> 6; matrix products, arithmetic and copies ran while one was open for 34% -> 12% of each run, Pallas kernels for 0% -> 11%
where the time goes in v3:
time: 69.6 us; the launch traced here: 68.3 us
  starting transfers between devices  35 us (50%)
  waiting for transfers between devices  10.6 us (15%)
  Pallas kernels  10.1 us (15%)
  local copies, waits for them, and re-layouts  6.25 us (9%)
  other arithmetic  3.94 us (6%)
  matrix products  1.35 us (2%)
  between operations  1.08 us (2%)
    ppermute x16, starting transfers between devices, send(): return lax.ppermute(value, 'dp', dp_perm(dx, dy, dc))  18.1 us
    ppermute x6, starting transfers between devices, ring(): return lax.ppermute(value, 'dp', pairs)  11 us
    pallas_call x3, Pallas kernels, load(): pl.pallas_call(functools.partial(load_kernel, batch, roles, len(late)), o...  8.32 us
    ppermute x16, waiting for transfers between devices, send(): return lax.ppermute(value, 'dp', dp_perm(dx, dy, dc))  6.69 us
    all_to_all x1, starting transfers between devices, on_device(): lax.all_to_all(blocks, 'expert', split_axis=0, concat_axis=0, tiled=True)  5.96 us
    unnamed x35, local copies, waits for them, and re-layouts  5.24 us
    ppermute x6, waiting for transfers between devices, ring(): return lax.ppermute(value, 'dp', pairs)  3.92 us
    another operation x2, other arithmetic, on_device(): jnp.stack([all_y, send(all_y, 0, 0, 1)]).reshape(16 * KROWS, KCOLS)  2.09 us
  transfers between devices with their start and end apart: 23, of which 6 were waited for; matrix products, arithmetic and copies ran while one was open for 12% of the time, Pallas kernels for 11%

profile of v3, /device:TPU:1, one launch (start us, length us, event | category | flops | bytes accessed | tf_op | source)
XLA Modules:
  0.0 68.3 jit_solution(13078445596189129513)
XLA Ops:
  0.7 2.4 %shard_map.179 = (bf16[1,224,1024]{2,1,0:T(8,128)(2,1)S(1)}, bf16[1,224,1024]{2,1,0:T(8,128)(2,1)S(1)}, bf16[1,224,1024]{2,1,0:T(8,128)(2,1)S(1)}, bf16[1,224,1024]{2,1,0:T(8,128)(2,1)S(1)}) custom-call(f32[16,96,2048]{2,1,0:T(8,128)} %bitcast.15, f32[16,32,512]{2,1,0:T(8,128)} %bitcast.18), custom_call_target="tpu_custom_call" | custom-call | flops 1000 | bytes 1000 | tf_op jit(solution)/shard_map/pallas_call | solution.py:146
  3.1 1.5 %collective-permute-start.13 = (bf16[1,224,1024]{2,1,0:T(8,128)(2,1)S(1)}, bf16[1,224,1024]{2,1,0:T(8,128)(2,1)S(1)}, u32[]{:S(2)}, u32[]{:S(2)}) collective-permute-start(bf16[1,224,1024]{2,1,0:T(8,128)(2,1)S(1)} %get-tuple-element.39.refs_0_), channel_id=1, source_target_pairs={{0,8},{8,0},{16,24},{24,16},{32,40},{40,32},{48,56},{56,48},{64,72... | collective-permute-start | bytes 1376264 | tf_op jit(solution)/shard_map/ppermute | solution.py:49
  4.7 2.4 %shard_map.180 = (bf16[1,224,1024]{2,1,0:T(8,128)(2,1)S(1)}, bf16[1,224,1024]{2,1,0:T(8,128)(2,1)S(1)}, bf16[1,224,1024]{2,1,0:T(8,128)(2,1)S(1)}, bf16[1,224,1024]{2,1,0:T(8,128)(2,1)S(1)}) custom-call(f32[16,96,2048]{2,1,0:T(8,128)} %bitcast.16, f32[16,32,512]{2,1,0:T(8,128)} %bitcast.19, bf16[1,224,1024]{2,1,0:T(8,128)(2,1)S(1)} %get-tuple-element.39.refs_0_), custom_call_target="tpu_custom_call" | custom-call | flops 1000 | bytes 1000 | tf_op jit(solution)/shard_map/pallas_call | solution.py:146
  7.1 0.5 collective-permute-start.12
  7.6 0.2 add_convert_fusion.1
  7.8 2.9 %collective-permute-start.14 = (bf16[1,224,1024]{2,1,0:T(8,128)(2,1)S(1)}, bf16[1,224,1024]{2,1,0:T(8,128)(2,1)S(1)}, u32[]{:S(2)}, u32[]{:S(2)}) collective-permute-start(bf16[1,224,1024]{2,1,0:T(8,128)(2,1)S(1)} %add_convert_fusion.1), channel_id=1, source_target_pairs={{0,16},{8,56},{16,32},{24,8},{32,48},{40,24},{48,0},{56,40},{64,80... | collective-permute-start | bytes 1376264 | tf_op jit(solution)/shard_map/ppermute | solution.py:59
  10.7 0.2 add_convert_fusion.2
  10.9 0.5 collective-permute-start.10
  11.5 3.5 %shard_map.181 = (bf16[1,192,1024]{2,1,0:T(8,128)(2,1)S(1)}, bf16[1,192,1024]{2,1,0:T(8,128)(2,1)S(1)}, bf16[1,192,1024]{2,1,0:T(8,128)(2,1)S(1)}, bf16[1,192,10...) custom-call(f32[16,96,2048]{2,1,0:T(8,128)} %bitcast.17, ...), custom_call_target="tpu_custom_call" | custom-call | flops 1000 | bytes 1000 | tf_op jit(solution)/shard_map/pallas_call | solution.py:146
  15.1 0.5 collective-permute-start.8
  15.7 0.4 collective-permute-done.14
  16.1 1.5 %collective-permute-start.1 = (bf16[1,192,1024]{2,1,0:T(8,128)(2,1)S(1)}, bf16[1,192,1024]{2,1,0:T(8,128)(2,1)S(1)}, u32[]{:S(2)}, u32[]{:S(2)}) collective-permute-start(bf16[1,192,1024]{2,1,0:T(8,128)(2,1)S(1)} %get-tuple-element.44), channel_id=1, source_target_pairs={{0,8},{8,0},{16,24},{24,16},{32,40},{40,32},{48,56},{56,48},{64,72... | collective-permute-start | bytes 1179656 | tf_op jit(solution)/shard_map/ppermute | solution.py:49
  17.7 0.2 add_convert_fusion
  17.9 1.7 %collective-permute-start.15 = (bf16[1,224,1024]{2,1,0:T(8,128)(2,1)S(1)}, bf16[1,224,1024]{2,1,0:T(8,128)(2,1)S(1)}, u32[]{:S(2)}, u32[]{:S(2)}) collective-permute-start(bf16[1,224,1024]{2,1,0:T(8,128)(2,1)S(1)} %add_convert_fusion), channel_id=1, source_target_pairs={{0,16},{8,56},{16,32},{24,8},{32,48},{40,24},{48,0},{56,40},{64,80... | collective-permute-start | bytes 1376264 | tf_op jit(solution)/shard_map/ppermute | solution.py:59
  19.6 1.4 %collective-permute-done.10 = bf16[1,224,1024]{2,1,0:T(8,128)(2,1)S(1)} collective-permute-done((bf16[1,224,1024]{2,1,0:T(8,128)(2,1)S(1)}, bf16[1,224,1024]{2,1,0:T(8,128)(2,1)S(1)}, u32[]{:S(2)}, u32[]{:S(2)}) %collective-permute-start.10) | collective-permute-done | bytes 458784 | tf_op jit(solution)/shard_map/ppermute | solution.py:59
  21.1 1.5 %collective-permute-start.11 = (bf16[1,224,1024]{2,1,0:T(8,128)(2,1)S(1)}, bf16[1,224,1024]{2,1,0:T(8,128)(2,1)S(1)}, u32[]{:S(2)}, u32[]{:S(2)}) collective-permute-start(bf16[1,224,1024]{2,1,0:T(8,128)(2,1)S(1)} %collective-permute-done.10), channel_id=1, source_target_pairs={{0,8},{8,0},{16,24},{24,16},{32,40},{40,32},{48,56},{56,48},{64,72... | collective-permute-start | bytes 1376264 | tf_op jit(solution)/shard_map/ppermute | solution.py:49
  22.6 0.1 add_convert_fusion.4
  22.7 1.7 %collective-permute-start.6 = (bf16[1,192,1024]{2,1,0:T(8,128)(2,1)S(1)}, bf16[1,192,1024]{2,1,0:T(8,128)(2,1)S(1)}, u32[]{:S(2)}, u32[]{:S(2)}) collective-permute-start(bf16[1,192,1024]{2,1,0:T(8,128)(2,1)S(1)} %add_convert_fusion.4), channel_id=1, source_target_pairs={{0,16},{8,56},{16,32},{24,8},{32,48},{40,24},{48,0},{56,40},{64,80... | collective-permute-start | bytes 1179656 | tf_op jit(solution)/shard_map/ppermute | solution.py:59
  24.4 0.1 add_convert_fusion.5
  24.7 1.3 %collective-permute-done.15 = bf16[1,224,1024]{2,1,0:T(8,128)(2,1)S(1)} collective-permute-done((bf16[1,224,1024]{2,1,0:T(8,128)(2,1)S(1)}, bf16[1,224,1024]{2,1,0:T(8,128)(2,1)S(1)}, u32[]{:S(2)}, u32[]{:S(2)}) %collective-permute-start.15) | collective-permute-done | bytes 458784 | tf_op jit(solution)/shard_map/ppermute | solution.py:59
  26.0 3.1 %collective-permute-start.2 = (bf16[1,192,1024]{2,1,0:T(8,128)(2,1)S(1)}, bf16[1,192,1024]{2,1,0:T(8,128)(2,1)S(1)}, u32[]{:S(2)}, u32[]{:S(2)}) collective-permute-start(bf16[1,192,1024]{2,1,0:T(8,128)(2,1)S(1)} %add_convert_fusion.5), channel_id=1, source_target_pairs={{0,16},{8,56},{16,32},{24,8},{32,48},{40,24},{48,0},{56,40},{64,80... | collective-permute-start | bytes 1179656 | tf_op jit(solution)/shard_map/ppermute | solution.py:59
  29.1 0.3 convert_add_fusion.own
  29.4 2.8 %collective-permute-start.16 = (bf16[1,208,1024]{2,1,0:T(8,128)(2,1)S(1)}, bf16[1,208,1024]{2,1,0:T(8,128)(2,1)S(1)}, u32[]{:S(2)}, u32[]{:S(2)}) collective-permute-start(bf16[1,208,1024]{2,1,0:T(8,128)(2,1)S(1)} %slice.7), channel_id=1, source_target_pairs={{0,64},{8,72},{16,80},{24,88},{32,96},{40,104},{48,112},{56,120},{... | collective-permute-start | bytes 1277960 | tf_op jit(solution)/shard_map/ppermute | solution.py:49
  32.3 0.2 add_convert_fusion.3
  32.5 1.1 %collective-permute-start.7 = (bf16[1,192,1024]{2,1,0:T(8,128)(2,1)S(1)}, bf16[1,192,1024]{2,1,0:T(8,128)(2,1)S(1)}, u32[]{:S(2)}, u32[]{:S(2)}) collective-permute-start(bf16[1,192,1024]{2,1,0:T(8,128)(2,1)S(1)} %add_convert_fusion.3), channel_id=1, source_target_pairs={{0,16},{8,56},{16,32},{24,8},{32,48},{40,24},{48,0},{56,40},{64,80... | collective-permute-start | bytes 1179656 | tf_op jit(solution)/shard_map/ppermute | solution.py:59
  33.7 0.7 %collective-permute-done.2 = bf16[1,192,1024]{2,1,0:T(8,128)(2,1)S(1)} collective-permute-done((bf16[1,192,1024]{2,1,0:T(8,128)(2,1)S(1)}, bf16[1,192,1024]{2,1,0:T(8,128)(2,1)S(1)}, u32[]{:S(2)}, u32[]{:S(2)}) %collective-permute-start.2) | collective-permute-done | bytes 393248 | tf_op jit(solution)/shard_map/ppermute | solution.py:59
  34.4 2.3 %collective-permute-start.3 = (bf16[1,192,1024]{2,1,0:T(8,128)(2,1)S(1)}, bf16[1,192,1024]{2,1,0:T(8,128)(2,1)S(1)}, u32[]{:S(2)}, u32[]{:S(2)}) collective-permute-start(bf16[1,192,1024]{2,1,0:T(8,128)(2,1)S(1)} %collective-permute-done.2), channel_id=1, source_target_pairs={{0,8},{8,0},{16,24},{24,16},{32,40},{40,32},{48,56},{56,48},{64,72... | collective-permute-start | bytes 1179656 | tf_op jit(solution)/shard_map/ppermute | solution.py:49
  36.7 5.2 %collective-permute-done.16.refs_3_.arrived = bf16[1,208,1024]{2,1,0:T(8,128)(2,1)S(1)} collective-permute-done((bf16[1,208,1024]{2,1,0:T(8,128)(2,1)S(1)}, bf16[1,208,1024]{2,1,0:T(8,128)(2,1)S(1)}, u32[]{:S(2)}, u32[]{:S(2)}) %collective-permute-start.16) | collective-permute-done | bytes 426016 | tf_op jit(solution)/shard_map/ppermute | solution.py:49
  41.9 0.1 shard_map.183
  42.1 2.9 %collective-permute-start.17 = (bf16[32,512]{1,0:T(8,128)(2,1)S(1)}, bf16[32,512]{1,0:T(8,128)(2,1)S(1)}, u32[]{:S(2)}, u32[]{:S(2)}) collective-permute-start(bf16[32,512]{1,0:T(8,128)(2,1)S(1)} %get-tuple-element.63), channel_id=1, source_target_pairs={{0,64},{8,72},{16,80},{24,88},{32,96},{40,104},{48,112},{56,120},{... | collective-permute-start | bytes 98312 | tf_op jit(solution)/shard_map/ppermute | solution.py:49
  45.0 1.4 %collective-permute-done.17 = bf16[32,512]{1,0:T(8,128)(2,1)S(1)} collective-permute-done((bf16[32,512]{1,0:T(8,128)(2,1)S(1)}, bf16[32,512]{1,0:T(8,128)(2,1)S(1)}, u32[]{:S(2)}, u32[]{:S(2)}) %collective-permute-start.17) | collective-permute-done | bytes 32800 | tf_op jit(solution)/shard_map/ppermute | solution.py:49
  46.6 1.4 %collective-permute-start.20 = (bf16[2,32,512]{2,1,0:T(8,128)(2,1)S(1)}, bf16[2,32,512]{2,1,0:T(8,128)(2,1)S(1)}, u32[]{:S(2)}, u32[]{:S(2)}) collective-permute-start(bf16[2,32,512]{2,1,0:T(8,128)(2,1)S(1)} %pad_maximum_fusion.2), channel_id=1, source_target_pairs={{0,16},{8,24},{16,32},{24,40},{32,48},{40,56},{48,0},{56,8},{64,80... | collective-permute-start | bytes 196616 | tf_op jit(solution)/shard_map/ppermute | solution.py:49
  48.0 0.1 add_convert_fusion.6.refs_0_
  48.2 1.6 %shard_map.182 = (f32[1,96,2048]{2,1,0:T(8,128)S(1)}, f32[1,96,2048]{2,1,0:T(8,128)S(1)}, f32[1,96,2048]{2,1,0:T(8,128)S(1)}, bf16[8,96,256]{2,1,0:T(8,128)(2,1)}) custom-call(bf16[1,192,1024]{2,1,0:T(8,128)(2,1)S(1)} %add_convert_fusion.6.refs_0_, bf16[1,192,1024]{2,1,0:T(8,128)(2,1)S(1)} %collective-permute-done.3.refs_1_, ...), custom_call_target="tpu_custom_call" | custom-call | flops 1000 | bytes 1000 | tf_op jit(solution)/shard_map/pallas_call | solution.py:212
  49.8 6.0 %all-to-all-start = ((bf16[8,96,256]{2,1,0:T(8,128)(2,1)}), bf16[8,96,256]{2,1,0:T(8,128)(2,1)S(1)}, u32[]{:S(2)}, u32[]{:S(2)}) async-start(bf16[8,96,256]{2,1,0:T(8,128)(2,1)} %get-tuple-element.61), calls=%async_computation | async-start | bytes 786432 | tf_op jit(solution)/shard_map/all_to_all | solution.py:269
  55.8 0.6 copy-done.8
  56.4 0.9 %fusion.29 = (bf16[1,4,2,32,512]{4,3,2,1,0:T(8,128)(2,1)S(1)}, bf16[4,2,32,512]{3,2,1,0:T(8,128)(2,1)S(1)}) fusion(bf16[1,2,32,512]{3,2,1,0:T(8,128)(2,1)} %bitcast.26, bf16[1,2,32,512]{3,2,1,0:T(8,128)(2,1)} %bitcast.25, bf16[1,2,32,512]{3,2,1,0:T(8,128)(2,1)} %bitcast.24, bf16[1,2,32,512]{3,2,1,0:T(8,128)(2,1)S(1)} %bitcast.23), kind=kLoop, calls=%fused_computation.80 | loop fusion | flops 393216 | bytes 786432 | tf_op jit(solution)/shard_map/stack | solution.py:285
  57.4 2.6 %collective-permute-start.21 = (bf16[4,2,32,512]{3,2,1,0:T(8,128)(2,1)S(1)}, bf16[4,2,32,512]{3,2,1,0:T(8,128)(2,1)}, u32[]{:S(2)}, u32[]{:S(2)}) collective-permute-start(bf16[4,2,32,512]{3,2,1,0:T(8,128)(2,1)S(1)} %get-tuple-element.69), channel_id=1, source_target_pairs={{0,8},{8,0},{16,24},{24,16},{32,40},{40,32},{48,56},{56,48},{64,72... | collective-permute-start | bytes 786440 | tf_op jit(solution)/shard_map/ppermute | solution.py:49
  60.0 0.2 select_reduce_fusion
  60.3 0.6 copy.26
  60.9 0.6 copy.27
  61.6 0.6 copy.28
  62.2 0.9 %copy.23 = f32[1,96,2048]{2,1,0:T(8,128)} copy(f32[1,96,2048]{2,1,0:T(8,128)S(1)} %get-tuple-element.70) | data formatting | bytes 1572864
  63.1 0.9 %copy.24 = f32[1,96,2048]{2,1,0:T(8,128)} copy(f32[1,96,2048]{2,1,0:T(8,128)S(1)} %get-tuple-element.71) | data formatting | bytes 1572864
  63.9 0.9 %copy.25 = f32[1,96,2048]{2,1,0:T(8,128)} copy(f32[1,96,2048]{2,1,0:T(8,128)S(1)} %get-tuple-element.72) | data formatting | bytes 1572864
  64.9 0.9 %scatter_fusion = bf16[8,96,256]{2,1,0:T(8,128)(2,1)S(1)} fusion(bf16[8,96,256]{2,1,0:T(8,128)(2,1)S(1)} %broadcast_in_dim.38, s32[8]{0:T(128)S(1)} %compare_select_fusion, bf16[8,96,256]{2,1,0:T(8,128)(2,1)S(1)} %all-to-all-done), kind=kCustom, calls=%fused_computation | custom fusion | bytes 1179680 | tf_op jit(solution)/shard_map/scatter | solution.py:270
  65.8 1.1 %pad_maximum_fusion = bf16[2,4,2,32,512]{4,3,2,1,0:T(8,128)(2,1)S(1)} fusion(bf16[1,4,2,32,512]{4,3,2,1,0:T(8,128)(2,1)} %bitcast.10, bf16[1,4,2,32,512]{4,3,2,1,0:T(8,128)(2,1)S(1)} %get-tuple-element.68), kind=kLoop, calls=%fused_computation.12 | loop fusion | flops 262144 | bytes 1048576 | tf_op jit(solution)/shard_map/stack | solution.py:285
  67.0 1.3 %convolution_convert_fusion = bf16[512,512]{1,0:T(8,128)(2,1)} fusion(bf16[512,512]{1,0:T(8,128)(2,1)S(1)} %bitcast.22, s32[512]{0:T(512)S(1)} %fusion.20), kind=kOutput, calls=%fused_computation.1 | convolution fusion | flops 268959744 | bytes 1050624 | tf_op jit(solution)/shard_map/dot_general | solution.py:295
  (58 shorter events, 1.0 us)
Async XLA Ops:
  3.1 4.5 %collective-permute-start.13 = (bf16[1,224,1024]{2,1,0:T(8,128)(2,1)S(1)}, bf16[1,224,1024]{2,1,0:T(8,128)(2,1)S(1)}, u32[]{:S(2)}, u32[]{:S(2)}) collective-permute-start(bf16[1,224,1024]{2,1,0:T(8,128)(2,1)S(1)} %get-tuple-element.39.refs_0_), channel_id=1, source_target_pairs={{0,8},{8,0},{16,24},{24,16},{32,40},{40,32},{48,56},{56,48},{64,72... | collective-permute-start | bytes 1376264 | tf_op jit(solution)/shard_map/ppermute | solution.py:49
  4.6 6.1 %collective-permute-start.9 = (bf16[1,224,1024]{2,1,0:T(8,128)(2,1)S(1)}, bf16[1,224,1024]{2,1,0:T(8,128)(2,1)S(1)}, u32[]{:S(2)}, u32[]{:S(2)}) collective-permute-start(bf16[1,224,1024]{2,1,0:T(8,128)(2,1)S(1)} %get-tuple-element.52), channel_id=1, source_target_pairs={{0,8},{8,0},{16,24},{24,16},{32,40},{40,32},{48,56},{56,48},{64,72... | collective-permute-start | bytes 1376264 | tf_op jit(solution)/shard_map/ppermute | solution.py:49
  7.1 8.5 %collective-permute-start.12 = (bf16[1,224,1024]{2,1,0:T(8,128)(2,1)S(1)}, bf16[1,224,1024]{2,1,0:T(8,128)(2,1)S(1)}, u32[]{:S(2)}, u32[]{:S(2)}) collective-permute-start(bf16[1,224,1024]{2,1,0:T(8,128)(2,1)S(1)} %get-tuple-element.40.refs_0_), channel_id=1, source_target_pairs={{0,8},{8,0},{16,24},{24,16},{32,40},{40,32},{48,56},{56,48},{64,72... | collective-permute-start | bytes 1376264 | tf_op jit(solution)/shard_map/ppermute | solution.py:49
  7.8 25.8 %copy-start.12 = (s32[8]{0:T(128)S(1)}, s32[8]{0:T(128)}, u32[]{:S(2)}) copy-start(s32[8]{0:T(128)} %param.24) | copy-start | bytes 100
  7.8 25.8 %copy-start.13 = (s32[128]{0:T(128)S(1)}, s32[128]{0:T(128)}, u32[]{:S(2)}) copy-start(s32[128]{0:T(128)} %param.23) | copy-start | bytes 1540
  7.8 34.1 %copy-start.3 = (f32[32,512]{1,0:T(8,128)S(1)}, f32[32,512]{1,0:T(8,128)}, u32[]{:S(2)}) copy-start(f32[32,512]{1,0:T(8,128)} %param.25) | copy-start | bytes 196612
  7.8 34.1 %copy-start.4 = (f32[32,512]{1,0:T(8,128)S(1)}, f32[32,512]{1,0:T(8,128)}, u32[]{:S(2)}) copy-start(f32[32,512]{1,0:T(8,128)} %moment.1) | copy-start | bytes 196612
  7.8 34.1 %copy-start.5 = (f32[32,512]{1,0:T(8,128)S(1)}, f32[32,512]{1,0:T(8,128)}, u32[]{:S(2)}) copy-start(f32[32,512]{1,0:T(8,128)} %variance.1) | copy-start | bytes 196612
  7.8 34.1 %copy-start.6 = (f32[4,4]{1,0:T(4,128)S(1)}, f32[4,4]{1,0:T(4,128)}, u32[]{:S(2)}) copy-start(f32[4,4]{1,0:T(4,128)} %scales.1) | copy-start | bytes 196
  7.8 8.3 %collective-permute-start.14 = (bf16[1,224,1024]{2,1,0:T(8,128)(2,1)S(1)}, bf16[1,224,1024]{2,1,0:T(8,128)(2,1)S(1)}, u32[]{:S(2)}, u32[]{:S(2)}) collective-permute-start(bf16[1,224,1024]{2,1,0:T(8,128)(2,1)S(1)} %add_convert_fusion.1), channel_id=1, source_target_pairs={{0,16},{8,56},{16,32},{24,8},{32,48},{40,24},{48,0},{56,40},{64,80... | collective-permute-start | bytes 1376264 | tf_op jit(solution)/shard_map/ppermute | solution.py:59
  10.9 34.1 %copy-start.11 = (f32[8,12,16]{2,0,1:T(8,128)S(1)}, f32[8,12,16]{2,0,1:T(8,128)}, u32[]{:S(2)}) copy-start(f32[8,12,16]{2,0,1:T(8,128)} %param.21) | copy-start | bytes 18436
  10.9 37.2 %copy-start = (f32[1,96,2048]{2,1,0:T(8,128)S(1)}, f32[1,96,2048]{2,1,0:T(8,128)}, u32[]{:S(2)}) copy-start(f32[1,96,2048]{2,1,0:T(8,128)} %refs_4_.1) | copy-start | bytes 2359300
  10.9 37.2 %copy-start.1 = (f32[1,96,2048]{2,1,0:T(8,128)S(1)}, f32[1,96,2048]{2,1,0:T(8,128)}, u32[]{:S(2)}) copy-start(f32[1,96,2048]{2,1,0:T(8,128)} %refs_5_.1) | copy-start | bytes 2359300
  10.9 37.2 %copy-start.2 = (f32[1,96,2048]{2,1,0:T(8,128)S(1)}, f32[1,96,2048]{2,1,0:T(8,128)}, u32[]{:S(2)}) copy-start(f32[1,96,2048]{2,1,0:T(8,128)} %refs_6_.1) | copy-start | bytes 2359300
  10.9 10.1 %collective-permute-start.10 = (bf16[1,224,1024]{2,1,0:T(8,128)(2,1)S(1)}, bf16[1,224,1024]{2,1,0:T(8,128)(2,1)S(1)}, u32[]{:S(2)}, u32[]{:S(2)}) collective-permute-start(bf16[1,224,1024]{2,1,0:T(8,128)(2,1)S(1)} %add_convert_fusion.2), channel_id=1, source_target_pairs={{0,16},{8,56},{16,32},{24,8},{32,48},{40,24},{48,0},{56,40},{64,80... | collective-permute-start | bytes 1376264 | tf_op jit(solution)/shard_map/ppermute | solution.py:59
  15.0 2.9 %collective-permute-start.5 = (bf16[1,192,1024]{2,1,0:T(8,128)(2,1)S(1)}, bf16[1,192,1024]{2,1,0:T(8,128)(2,1)S(1)}, u32[]{:S(2)}, u32[]{:S(2)}) collective-permute-start(bf16[1,192,1024]{2,1,0:T(8,128)(2,1)S(1)} %get-tuple-element.48), channel_id=1, source_target_pairs={{0,8},{8,0},{16,24},{24,16},{32,40},{40,32},{48,56},{56,48},{64,72... | collective-permute-start | bytes 1179656 | tf_op jit(solution)/shard_map/ppermute | solution.py:49
  15.1 9.5 %collective-permute-start.8 = (bf16[1,224,1024]{2,1,0:T(8,128)(2,1)S(1)}, bf16[1,224,1024]{2,1,0:T(8,128)(2,1)S(1)}, u32[]{:S(2)}, u32[]{:S(2)}) collective-permute-start(bf16[1,224,1024]{2,1,0:T(8,128)(2,1)S(1)} %get-tuple-element.50), channel_id=1, source_target_pairs={{0,8},{8,0},{16,24},{24,16},{32,40},{40,32},{48,56},{56,48},{64,72... | collective-permute-start | bytes 1376264 | tf_op jit(solution)/shard_map/ppermute | solution.py:49
  15.6 16.7 %collective-permute-start.4 = (bf16[1,192,1024]{2,1,0:T(8,128)(2,1)S(1)}, bf16[1,192,1024]{2,1,0:T(8,128)(2,1)S(1)}, u32[]{:S(2)}, u32[]{:S(2)}) collective-permute-start(bf16[1,192,1024]{2,1,0:T(8,128)(2,1)S(1)} %get-tuple-element.46), channel_id=1, source_target_pairs={{0,8},{8,0},{16,24},{24,16},{32,40},{40,32},{48,56},{56,48},{64,72... | collective-permute-start | bytes 1179656 | tf_op jit(solution)/shard_map/ppermute | solution.py:49
  16.1 6.6 %collective-permute-start.1 = (bf16[1,192,1024]{2,1,0:T(8,128)(2,1)S(1)}, bf16[1,192,1024]{2,1,0:T(8,128)(2,1)S(1)}, u32[]{:S(2)}, u32[]{:S(2)}) collective-permute-start(bf16[1,192,1024]{2,1,0:T(8,128)(2,1)S(1)} %get-tuple-element.44), channel_id=1, source_target_pairs={{0,8},{8,0},{16,24},{24,16},{32,40},{40,32},{48,56},{56,48},{64,72... | collective-permute-start | bytes 1179656 | tf_op jit(solution)/shard_map/ppermute | solution.py:49
  17.9 8.0 %collective-permute-start.15 = (bf16[1,224,1024]{2,1,0:T(8,128)(2,1)S(1)}, bf16[1,224,1024]{2,1,0:T(8,128)(2,1)S(1)}, u32[]{:S(2)}, u32[]{:S(2)}) collective-permute-start(bf16[1,224,1024]{2,1,0:T(8,128)(2,1)S(1)} %add_convert_fusion), channel_id=1, source_target_pairs={{0,16},{8,56},{16,32},{24,8},{32,48},{40,24},{48,0},{56,40},{64,80... | collective-permute-start | bytes 1376264 | tf_op jit(solution)/shard_map/ppermute | solution.py:59
  21.1 8.0 %collective-permute-start.11 = (bf16[1,224,1024]{2,1,0:T(8,128)(2,1)S(1)}, bf16[1,224,1024]{2,1,0:T(8,128)(2,1)S(1)}, u32[]{:S(2)}, u32[]{:S(2)}) collective-permute-start(bf16[1,224,1024]{2,1,0:T(8,128)(2,1)S(1)} %collective-permute-done.10), channel_id=1, source_target_pairs={{0,8},{8,0},{16,24},{24,16},{32,40},{40,32},{48,56},{56,48},{64,72... | collective-permute-start | bytes 1376264 | tf_op jit(solution)/shard_map/ppermute | solution.py:49
  22.7 9.6 %collective-permute-start.6 = (bf16[1,192,1024]{2,1,0:T(8,128)(2,1)S(1)}, bf16[1,192,1024]{2,1,0:T(8,128)(2,1)S(1)}, u32[]{:S(2)}, u32[]{:S(2)}) collective-permute-start(bf16[1,192,1024]{2,1,0:T(8,128)(2,1)S(1)} %add_convert_fusion.4), channel_id=1, source_target_pairs={{0,16},{8,56},{16,32},{24,8},{32,48},{40,24},{48,0},{56,40},{64,80... | collective-permute-start | bytes 1179656 | tf_op jit(solution)/shard_map/ppermute | solution.py:59
  24.6 23.4 %collective-permute-start = (bf16[1,192,1024]{2,1,0:T(8,128)(2,1)S(1)}, bf16[1,192,1024]{2,1,0:T(8,128)(2,1)S(1)}, u32[]{:S(2)}, u32[]{:S(2)}) collective-permute-start(bf16[1,192,1024]{2,1,0:T(8,128)(2,1)S(1)} %get-tuple-element.42), channel_id=1, source_target_pairs={{0,8},{8,0},{16,24},{24,16},{32,40},{40,32},{48,56},{56,48},{64,72... | collective-permute-start | bytes 1179656 | tf_op jit(solution)/shard_map/ppermute | solution.py:49
  26.0 8.4 %collective-permute-start.2 = (bf16[1,192,1024]{2,1,0:T(8,128)(2,1)S(1)}, bf16[1,192,1024]{2,1,0:T(8,128)(2,1)S(1)}, u32[]{:S(2)}, u32[]{:S(2)}) collective-permute-start(bf16[1,192,1024]{2,1,0:T(8,128)(2,1)S(1)} %add_convert_fusion.5), channel_id=1, source_target_pairs={{0,16},{8,56},{16,32},{24,8},{32,48},{40,24},{48,0},{56,40},{64,80... | collective-permute-start | bytes 1179656 | tf_op jit(solution)/shard_map/ppermute | solution.py:59
  29.4 12.5 %collective-permute-start.16 = (bf16[1,208,1024]{2,1,0:T(8,128)(2,1)S(1)}, bf16[1,208,1024]{2,1,0:T(8,128)(2,1)S(1)}, u32[]{:S(2)}, u32[]{:S(2)}) collective-permute-start(bf16[1,208,1024]{2,1,0:T(8,128)(2,1)S(1)} %slice.7), channel_id=1, source_target_pairs={{0,64},{8,72},{16,80},{24,88},{32,96},{40,104},{48,112},{56,120},{... | collective-permute-start | bytes 1277960 | tf_op jit(solution)/shard_map/ppermute | solution.py:49
  32.5 13.9 %collective-permute-start.7 = (bf16[1,192,1024]{2,1,0:T(8,128)(2,1)S(1)}, bf16[1,192,1024]{2,1,0:T(8,128)(2,1)S(1)}, u32[]{:S(2)}, u32[]{:S(2)}) collective-permute-start(bf16[1,192,1024]{2,1,0:T(8,128)(2,1)S(1)} %add_convert_fusion.3), channel_id=1, source_target_pairs={{0,16},{8,56},{16,32},{24,8},{32,48},{40,24},{48,0},{56,40},{64,80... | collective-permute-start | bytes 1179656 | tf_op jit(solution)/shard_map/ppermute | solution.py:59
  34.4 13.7 %collective-permute-start.3 = (bf16[1,192,1024]{2,1,0:T(8,128)(2,1)S(1)}, bf16[1,192,1024]{2,1,0:T(8,128)(2,1)S(1)}, u32[]{:S(2)}, u32[]{:S(2)}) collective-permute-start(bf16[1,192,1024]{2,1,0:T(8,128)(2,1)S(1)} %collective-permute-done.2), channel_id=1, source_target_pairs={{0,8},{8,0},{16,24},{24,16},{32,40},{40,32},{48,56},{56,48},{64,72... | collective-permute-start | bytes 1179656 | tf_op jit(solution)/shard_map/ppermute | solution.py:49
  42.1 4.3 %collective-permute-start.17 = (bf16[32,512]{1,0:T(8,128)(2,1)S(1)}, bf16[32,512]{1,0:T(8,128)(2,1)S(1)}, u32[]{:S(2)}, u32[]{:S(2)}) collective-permute-start(bf16[32,512]{1,0:T(8,128)(2,1)S(1)} %get-tuple-element.63), channel_id=1, source_target_pairs={{0,64},{8,72},{16,80},{24,88},{32,96},{40,104},{48,112},{56,120},{... | collective-permute-start | bytes 98312 | tf_op jit(solution)/shard_map/ppermute | solution.py:49
  46.4 9.3 %collective-permute-start.18 = (bf16[2,32,512]{2,1,0:T(8,128)(2,1)S(1)}, bf16[2,32,512]{2,1,0:T(8,128)(2,1)S(1)}, u32[]{:S(2)}, u32[]{:S(2)}) collective-permute-start(bf16[2,32,512]{2,1,0:T(8,128)(2,1)S(1)} %pad_maximum_fusion.2), channel_id=1, source_target_pairs={{0,48},{8,56},{16,0},{24,8},{32,16},{40,24},{48,32},{56,40},{64,11... | collective-permute-start | bytes 196616 | tf_op jit(solution)/shard_map/ppermute | solution.py:49
  46.5 9.3 %collective-permute-start.19 = (bf16[2,32,512]{2,1,0:T(8,128)(2,1)S(1)}, bf16[2,32,512]{2,1,0:T(8,128)(2,1)S(1)}, u32[]{:S(2)}, u32[]{:S(2)}) collective-permute-start(bf16[2,32,512]{2,1,0:T(8,128)(2,1)S(1)} %pad_maximum_fusion.2), channel_id=1, source_target_pairs={{0,32},{8,40},{16,48},{24,56},{32,0},{40,8},{48,16},{56,24},{64,96... | collective-permute-start | bytes 196616 | tf_op jit(solution)/shard_map/ppermute | solution.py:49
  46.6 9.2 %collective-permute-start.20 = (bf16[2,32,512]{2,1,0:T(8,128)(2,1)S(1)}, bf16[2,32,512]{2,1,0:T(8,128)(2,1)S(1)}, u32[]{:S(2)}, u32[]{:S(2)}) collective-permute-start(bf16[2,32,512]{2,1,0:T(8,128)(2,1)S(1)} %pad_maximum_fusion.2), channel_id=1, source_target_pairs={{0,16},{8,24},{16,32},{24,40},{32,48},{40,56},{48,0},{56,8},{64,80... | collective-permute-start | bytes 196616 | tf_op jit(solution)/shard_map/ppermute | solution.py:49
  49.8 15.0 %all-to-all-start = ((bf16[8,96,256]{2,1,0:T(8,128)(2,1)}), bf16[8,96,256]{2,1,0:T(8,128)(2,1)S(1)}, u32[]{:S(2)}, u32[]{:S(2)}) async-start(bf16[8,96,256]{2,1,0:T(8,128)(2,1)} %get-tuple-element.61), calls=%async_computation | async-start | bytes 786432 | tf_op jit(solution)/shard_map/all_to_all | solution.py:269
  55.8 0.6 copy-start.8
  55.8 0.6 copy-start.9
  55.8 0.6 copy-start.10
  57.4 8.4 %collective-permute-start.21 = (bf16[4,2,32,512]{3,2,1,0:T(8,128)(2,1)S(1)}, bf16[4,2,32,512]{3,2,1,0:T(8,128)(2,1)}, u32[]{:S(2)}, u32[]{:S(2)}) collective-permute-start(bf16[4,2,32,512]{3,2,1,0:T(8,128)(2,1)S(1)} %get-tuple-element.69), channel_id=1, source_target_pairs={{0,8},{8,0},{16,24},{24,16},{32,40},{40,32},{48,56},{56,48},{64,72... | collective-permute-start | bytes 786440 | tf_op jit(solution)/shard_map/ppermute | solution.py:49
  65.8 2.5 %copy-start.7 = (bf16[8,96,256]{2,1,0:T(8,128)(2,1)}, bf16[8,96,256]{2,1,0:T(8,128)(2,1)S(1)}, u32[]{:S(2)}) copy-start(bf16[8,96,256]{2,1,0:T(8,128)(2,1)S(1)} %scatter_fusion) | copy-start | bytes 1179652

commit v4 on v3

--- a/solution.py
+++ b/solution.py
@@ -57,10 +57,6 @@
         for c in range(2)
     ]
     return lax.ppermute(value, "dp", pairs)
-
-
-def after(value, *earlier):
-    return lax.optimization_barrier((value, *earlier))[0]
 
 
 def adam_update(param, moment, second, grad):
@@ -211,7 +207,7 @@
     near = lambda v: pltpu.with_memory_space_constraint(v, pltpu.VMEM)
     return pl.pallas_call(
         kernel,
-        out_shape=[pltpu.VMEM(param.shape, F32)] * 3 + [jax.ShapeDtypeStruct(grid_shape, BF)],
+        out_shape=[jax.ShapeDtypeStruct(param.shape, F32)] * 3 + [jax.ShapeDtypeStruct(grid_shape, BF)],
         in_specs=[vmem] * (len(terms) + 4),
         out_specs=[vmem] * 4,
         compiler_params=pltpu.CompilerParams(vmem_limit_bytes=VMEM_BYTES),
@@ -257,6 +253,16 @@
     near_c = ring(plus(keeps_c[2], got_c[2], far_c).astype(BF))
     cross_c = send(plain_c, 0, 0, 1)
     stayed = plus(keeps_c[3], got_c[3]).astype(BF)
+    new_kp, new_km, new_ks, key_grid = update(
+        key_kernel,
+        (turned, x_last),
+        key_param,
+        key_moment,
+        key_second,
+        key_scales,
+        (KROWS, KCOLS),
+    )
+    chip_x = send(key_grid, 1, 0, 0)
     new_ep, new_em, new_es, blocks = update(
         update_kernel,
         (stayed, cross_c, near_c, x_last),
@@ -266,22 +272,12 @@
         expert_scales,
         (8, ROWS, 256),
     )
+    column = jnp.stack([key_grid, chip_x])
+    column, blocks = lax.optimization_barrier((column, blocks))
     arrived = lax.all_to_all(blocks, "expert", split_axis=0, concat_axis=0, tiled=True)
-    placed = jnp.zeros_like(arrived).at[expert_slot].set(arrived)
-    server_expert = jnp.transpose(placed, (0, 2, 1))
-
-    new_kp, new_km, new_ks, key_grid = update(
-        key_kernel,
-        (turned, x_last),
-        key_param,
-        key_moment,
-        key_second,
-        key_scales,
-        (KROWS, KCOLS),
-    )
-    chip_x = send(after(key_grid, far_c), 1, 0, 0)
-    column = after(jnp.stack([key_grid, chip_x]), near_c)
-    all_y = jnp.stack([column, send(column, 0, -1, 0), send(column, 0, -2, 0), send(column, 0, -3, 0)])
+    all_y = [column] + [send(column, 0, -step, 0) for step in (1, 2, 3)]
+    all_y, arrived = lax.optimization_barrier((all_y, arrived))
+    all_y = jnp.stack(all_y)
     everything = jnp.stack([all_y, send(all_y, 0, 0, 1)]).reshape(16 * KROWS, KCOLS)
     order = jnp.arange(16 * KROWS, dtype=jnp.int32)
     piece, row = order // KROWS, order % KROWS
@@ -295,6 +291,8 @@
     server_key = lax.dot_general(
         everything, pick, (((0,), (0,)), ((), ())), preferred_element_type=F32
     ).astype(BF)
+    placed = jnp.zeros_like(arrived).at[expert_slot].set(arrived)
+    server_expert = jnp.transpose(placed, (0, 2, 1))
     return (new_ep, new_em, new_es, new_kp, new_km, new_ks, server_expert, server_key)
 
 

time: 69.6 us -> 65.4 us (0.940); the launches traced: 68.3 us -> 65.2 us
  local copies, waits for them, and re-layouts: 6.25 us -> 1.1 us
  starting transfers between devices: 35 us -> 38.7 us
  other arithmetic: 3.94 us -> 1.95 us
  Pallas kernels: 10.1 us -> 11.4 us
  waiting for transfers between devices: 10.6 us -> 9.61 us
    ppermute x16, starting transfers between devices: 18.1 us -> 24.2 us  [send(): return lax.ppermute(value, 'dp', dp_perm(dx, dy, dc))]
    unnamed x35 -> x23, local copies, waits for them, and re-layouts: 5.24 us -> 0.08 us
    another operation x2, other arithmetic: 2.09 us -> 0.1 us  [on_device(): jnp.stack([all_y, send(all_y, 0, 0, 1)]).reshape(16 * KROWS, KCOLS)]
    ppermute x6, starting transfers between devices: 11 us -> 9.42 us  [ring(): return lax.ppermute(value, 'dp', pairs)]
    pallas_call x2, Pallas kernels: 1.77 us -> 3.12 us  [update(): pl.pallas_call(kernel, out_shape=[jax.ShapeDtypeStruct(param.shape, F32)]...]
    all_to_all x1, starting transfers between devices: 5.96 us -> 5.07 us  [on_device(): lax.all_to_all(blocks, 'expert', split_axis=0, concat_axis=0, tiled=True)]
  transfers between devices with their start and end apart: 23 -> 23, of which waited for: 6 -> 8; matrix products, arithmetic and copies ran while one was open for 12% -> 4% of each run, Pallas kernels for 11% -> 14%
where the time goes in v4:
time: 65.4 us; the launch traced here: 65.2 us
  starting transfers between devices  38.7 us (59%)
  Pallas kernels  11.4 us (17%)
  waiting for transfers between devices  9.61 us (15%)
  other arithmetic  1.95 us (3%)
  matrix products  1.35 us (2%)
  local copies, waits for them, and re-layouts  1.1 us (2%)
  between operations  1.02 us (2%)
    ppermute x16, starting transfers between devices, send(): return lax.ppermute(value, 'dp', dp_perm(dx, dy, dc))  24.2 us
    ppermute x6, starting transfers between devices, ring(): return lax.ppermute(value, 'dp', pairs)  9.42 us
    pallas_call x3, Pallas kernels, load(): pl.pallas_call(functools.partial(load_kernel, batch, roles, len(late)), o...  8.32 us
    ppermute x16, waiting for transfers between devices, send(): return lax.ppermute(value, 'dp', dp_perm(dx, dy, dc))  6.02 us
    all_to_all x1, starting transfers between devices, on_device(): lax.all_to_all(blocks, 'expert', split_axis=0, concat_axis=0, tiled=True)  5.07 us
    ppermute x6, waiting for transfers between devices, ring(): return lax.ppermute(value, 'dp', pairs)  3.58 us
    pallas_call x2, Pallas kernels, update(): pl.pallas_call(kernel, out_shape=[jax.ShapeDtypeStruct(param.shape, F32)]...  3.12 us
    dot_general x1, matrix products, on_device(): lax.dot_general(everything, pick, (((0,), (0,)), ((), ())), preferred_ele...  1.35 us
  transfers between devices with their start and end apart: 23, of which 8 were waited for; matrix products, arithmetic and copies ran while one was open for 4% of the time, Pallas kernels for 14%

profile of v4, /device:TPU:1, one launch (start us, length us, event | category | flops | bytes accessed | tf_op | source)
XLA Modules:
  0.0 65.2 jit_solution(17841321187650562542)
XLA Ops:
  0.7 2.4 %shard_map.179 = (bf16[1,224,1024]{2,1,0:T(8,128)(2,1)S(1)}, bf16[1,224,1024]{2,1,0:T(8,128)(2,1)S(1)}, bf16[1,224,1024]{2,1,0:T(8,128)(2,1)S(1)}, bf16[1,224,1024]{2,1,0:T(8,128)(2,1)S(1)}) custom-call(f32[16,96,2048]{2,1,0:T(8,128)} %bitcast.15, f32[16,32,512]{2,1,0:T(8,128)} %bitcast.18), custom_call_target="tpu_custom_call" | custom-call | flops 1000 | bytes 1000 | tf_op jit(solution)/shard_map/pallas_call | solution.py:142
  3.1 1.5 %collective-permute-start.13 = (bf16[1,224,1024]{2,1,0:T(8,128)(2,1)S(1)}, bf16[1,224,1024]{2,1,0:T(8,128)(2,1)S(1)}, u32[]{:S(2)}, u32[]{:S(2)}) collective-permute-start(bf16[1,224,1024]{2,1,0:T(8,128)(2,1)S(1)} %get-tuple-element.44.refs_0_), channel_id=1, source_target_pairs={{0,8},{8,0},{16,24},{24,16},{32,40},{40,32},{48,56},{56,48},{64,72... | collective-permute-start | bytes 1376264 | tf_op jit(solution)/shard_map/ppermute | solution.py:49
  4.6 0.1 collective-permute-start.9
  4.7 2.4 %shard_map.180 = (bf16[1,224,1024]{2,1,0:T(8,128)(2,1)S(1)}, bf16[1,224,1024]{2,1,0:T(8,128)(2,1)S(1)}, bf16[1,224,1024]{2,1,0:T(8,128)(2,1)S(1)}, bf16[1,224,1024]{2,1,0:T(8,128)(2,1)S(1)}) custom-call(f32[16,96,2048]{2,1,0:T(8,128)} %bitcast.16, f32[16,32,512]{2,1,0:T(8,128)} %bitcast.19, bf16[1,224,1024]{2,1,0:T(8,128)(2,1)S(1)} %get-tuple-element.44.refs_0_), custom_call_target="tpu_custom_call" | custom-call | flops 1000 | bytes 1000 | tf_op jit(solution)/shard_map/pallas_call | solution.py:142
  7.1 0.5 collective-permute-start.12
  7.6 0.2 add_convert_fusion.1
  7.8 2.9 %collective-permute-start.14 = (bf16[1,224,1024]{2,1,0:T(8,128)(2,1)S(1)}, bf16[1,224,1024]{2,1,0:T(8,128)(2,1)S(1)}, u32[]{:S(2)}, u32[]{:S(2)}) collective-permute-start(bf16[1,224,1024]{2,1,0:T(8,128)(2,1)S(1)} %add_convert_fusion.1), channel_id=1, source_target_pairs={{0,16},{8,56},{16,32},{24,8},{32,48},{40,24},{48,0},{56,40},{64,80... | collective-permute-start | bytes 1376264 | tf_op jit(solution)/shard_map/ppermute | solution.py:59
  10.7 0.2 add_convert_fusion.2
  10.9 0.5 collective-permute-start.10
  11.5 3.5 %shard_map.181 = (bf16[1,192,1024]{2,1,0:T(8,128)(2,1)S(1)}, bf16[1,192,1024]{2,1,0:T(8,128)(2,1)S(1)}, bf16[1,192,1024]{2,1,0:T(8,128)(2,1)S(1)}, bf16[1,192,10...) custom-call(f32[16,96,2048]{2,1,0:T(8,128)} %bitcast.17, ...), custom_call_target="tpu_custom_call" | custom-call | flops 1000 | bytes 1000 | tf_op jit(solution)/shard_map/pallas_call | solution.py:142
  15.0 0.1 collective-permute-start.5
  15.1 0.5 collective-permute-start.8
  15.6 0.1 collective-permute-start.4
  15.7 0.4 collective-permute-done.14
  16.1 1.5 %collective-permute-start.1 = (bf16[1,192,1024]{2,1,0:T(8,128)(2,1)S(1)}, bf16[1,192,1024]{2,1,0:T(8,128)(2,1)S(1)}, u32[]{:S(2)}, u32[]{:S(2)}) collective-permute-start(bf16[1,192,1024]{2,1,0:T(8,128)(2,1)S(1)} %get-tuple-element.49), channel_id=1, source_target_pairs={{0,8},{8,0},{16,24},{24,16},{32,40},{40,32},{48,56},{56,48},{64,72... | collective-permute-start | bytes 1179656 | tf_op jit(solution)/shard_map/ppermute | solution.py:49
  17.7 0.2 add_convert_fusion
  17.9 1.7 %collective-permute-start.15 = (bf16[1,224,1024]{2,1,0:T(8,128)(2,1)S(1)}, bf16[1,224,1024]{2,1,0:T(8,128)(2,1)S(1)}, u32[]{:S(2)}, u32[]{:S(2)}) collective-permute-start(bf16[1,224,1024]{2,1,0:T(8,128)(2,1)S(1)} %add_convert_fusion), channel_id=1, source_target_pairs={{0,16},{8,56},{16,32},{24,8},{32,48},{40,24},{48,0},{56,40},{64,80... | collective-permute-start | bytes 1376264 | tf_op jit(solution)/shard_map/ppermute | solution.py:59
  19.6 1.4 %collective-permute-done.10 = bf16[1,224,1024]{2,1,0:T(8,128)(2,1)S(1)} collective-permute-done((bf16[1,224,1024]{2,1,0:T(8,128)(2,1)S(1)}, bf16[1,224,1024]{2,1,0:T(8,128)(2,1)S(1)}, u32[]{:S(2)}, u32[]{:S(2)}) %collective-permute-start.10) | collective-permute-done | bytes 458784 | tf_op jit(solution)/shard_map/ppermute | solution.py:59
  21.0 1.5 %collective-permute-start.11 = (bf16[1,224,1024]{2,1,0:T(8,128)(2,1)S(1)}, bf16[1,224,1024]{2,1,0:T(8,128)(2,1)S(1)}, u32[]{:S(2)}, u32[]{:S(2)}) collective-permute-start(bf16[1,224,1024]{2,1,0:T(8,128)(2,1)S(1)} %collective-permute-done.10), channel_id=1, source_target_pairs={{0,8},{8,0},{16,24},{24,16},{32,40},{40,32},{48,56},{56,48},{64,72... | collective-permute-start | bytes 1376264 | tf_op jit(solution)/shard_map/ppermute | solution.py:49
  22.6 0.1 add_convert_fusion.4
  22.7 1.7 %collective-permute-start.6 = (bf16[1,192,1024]{2,1,0:T(8,128)(2,1)S(1)}, bf16[1,192,1024]{2,1,0:T(8,128)(2,1)S(1)}, u32[]{:S(2)}, u32[]{:S(2)}) collective-permute-start(bf16[1,192,1024]{2,1,0:T(8,128)(2,1)S(1)} %add_convert_fusion.4), channel_id=1, source_target_pairs={{0,16},{8,56},{16,32},{24,8},{32,48},{40,24},{48,0},{56,40},{64,80... | collective-permute-start | bytes 1179656 | tf_op jit(solution)/shard_map/ppermute | solution.py:59
  24.4 0.1 add_convert_fusion.5
  24.6 0.5 collective-permute-start.2
  25.1 0.9 %collective-permute-done.15 = bf16[1,224,1024]{2,1,0:T(8,128)(2,1)S(1)} collective-permute-done((bf16[1,224,1024]{2,1,0:T(8,128)(2,1)S(1)}, bf16[1,224,1024]{2,1,0:T(8,128)(2,1)S(1)}, u32[]{:S(2)}, u32[]{:S(2)}) %collective-permute-start.15) | collective-permute-done | bytes 458784 | tf_op jit(solution)/shard_map/ppermute | solution.py:59
  26.0 0.3 convert_add_fusion.own
  26.3 0.1 slice.7
  26.3 2.8 %collective-permute-start.16 = (bf16[1,208,1024]{2,1,0:T(8,128)(2,1)S(1)}, bf16[1,208,1024]{2,1,0:T(8,128)(2,1)S(1)}, u32[]{:S(2)}, u32[]{:S(2)}) collective-permute-start(bf16[1,208,1024]{2,1,0:T(8,128)(2,1)S(1)} %slice.7), channel_id=1, source_target_pairs={{0,64},{8,72},{16,80},{24,88},{32,96},{40,104},{48,112},{56,120},{... | collective-permute-start | bytes 1277960 | tf_op jit(solution)/shard_map/ppermute | solution.py:49
  29.2 2.1 %collective-permute-start = (bf16[1,192,1024]{2,1,0:T(8,128)(2,1)S(1)}, bf16[1,192,1024]{2,1,0:T(8,128)(2,1)S(1)}, u32[]{:S(2)}, u32[]{:S(2)}) collective-permute-start(bf16[1,192,1024]{2,1,0:T(8,128)(2,1)S(1)} %get-tuple-element.47), channel_id=1, source_target_pairs={{0,8},{8,0},{16,24},{24,16},{32,40},{40,32},{48,56},{56,48},{64,72... | collective-permute-start | bytes 1179656 | tf_op jit(solution)/shard_map/ppermute | solution.py:49
  31.2 0.2 add_convert_fusion.3
  31.4 2.1 %collective-permute-start.7 = (bf16[1,192,1024]{2,1,0:T(8,128)(2,1)S(1)}, bf16[1,192,1024]{2,1,0:T(8,128)(2,1)S(1)}, u32[]{:S(2)}, u32[]{:S(2)}) collective-permute-start(bf16[1,192,1024]{2,1,0:T(8,128)(2,1)S(1)} %add_convert_fusion.3), channel_id=1, source_target_pairs={{0,16},{8,56},{16,32},{24,8},{32,48},{40,24},{48,0},{56,40},{64,80... | collective-permute-start | bytes 1179656 | tf_op jit(solution)/shard_map/ppermute | solution.py:59
  33.6 0.8 %collective-permute-done.2 = bf16[1,192,1024]{2,1,0:T(8,128)(2,1)S(1)} collective-permute-done((bf16[1,192,1024]{2,1,0:T(8,128)(2,1)S(1)}, bf16[1,192,1024]{2,1,0:T(8,128)(2,1)S(1)}, u32[]{:S(2)}, u32[]{:S(2)}) %collective-permute-start.2) | collective-permute-done | bytes 393248 | tf_op jit(solution)/shard_map/ppermute | solution.py:59
  34.4 1.7 %collective-permute-start.3 = (bf16[1,192,1024]{2,1,0:T(8,128)(2,1)S(1)}, bf16[1,192,1024]{2,1,0:T(8,128)(2,1)S(1)}, u32[]{:S(2)}, u32[]{:S(2)}) collective-permute-start(bf16[1,192,1024]{2,1,0:T(8,128)(2,1)S(1)} %collective-permute-done.2), channel_id=1, source_target_pairs={{0,8},{8,0},{16,24},{24,16},{32,40},{40,32},{48,56},{56,48},{64,72... | collective-permute-start | bytes 1179656 | tf_op jit(solution)/shard_map/ppermute | solution.py:49
  36.1 1.4 %collective-permute-done.16.refs_3_.arrived = bf16[1,208,1024]{2,1,0:T(8,128)(2,1)S(1)} collective-permute-done((bf16[1,208,1024]{2,1,0:T(8,128)(2,1)S(1)}, bf16[1,208,1024]{2,1,0:T(8,128)(2,1)S(1)}, u32[]{:S(2)}, u32[]{:S(2)}) %collective-permute-start.16) | collective-permute-done | bytes 426016 | tf_op jit(solution)/shard_map/ppermute | solution.py:49
  37.5 0.7 %shard_map.183 = (f32[32,512]{1,0:T(8,128)}, f32[32,512]{1,0:T(8,128)}, f32[32,512]{1,0:T(8,128)}, bf16[32,512]{1,0:T(8,128)(2,1)S(1)}) custom-call(f32[1,224,1024]{2,1,0:T(8,128)S(1)} %convert_add_fusion.own, bf16[1,208,1024]{2,1,0:T(8,128)(2,1)S(1)} %collective-permute-done.16.refs_3_.arrived, f32[32,512]{1,0:T(8,128)S(1)} %copy-done.3, ...), custom_call_target="tpu_custom_call" | custom-call | flops 1000 | bytes 1000 | tf_op jit(solution)/shard_map/pallas_call | solution.py:208
  38.3 2.7 %collective-permute-start.17 = (bf16[32,512]{1,0:T(8,128)(2,1)S(1)}, bf16[32,512]{1,0:T(8,128)(2,1)S(1)}, u32[]{:S(2)}, u32[]{:S(2)}) collective-permute-start(bf16[32,512]{1,0:T(8,128)(2,1)S(1)} %get-tuple-element.66), channel_id=1, source_target_pairs={{0,64},{8,72},{16,80},{24,88},{32,96},{40,104},{48,112},{56,120},{... | collective-permute-start | bytes 98312 | tf_op jit(solution)/shard_map/ppermute | solution.py:49
  41.0 0.1 add_convert_fusion.6.refs_0_
  41.1 2.4 %shard_map.182 = (f32[1,96,2048]{2,1,0:T(8,128)}, f32[1,96,2048]{2,1,0:T(8,128)}, f32[1,96,2048]{2,1,0:T(8,128)}, bf16[8,96,256]{2,1,0:T(8,128)(2,1)}) custom-call(bf16[1,192,1024]{2,1,0:T(8,128)(2,1)S(1)} %add_convert_fusion.6.refs_0_, bf16[1,192,1024]{2,1,0:T(8,128)(2,1)S(1)} %collective-permute-done.3.refs_1_, ...), custom_call_target="tpu_custom_call" | custom-call | flops 1000 | bytes 1000 | tf_op jit(solution)/shard_map/pallas_call | solution.py:208
  43.5 5.1 %all-to-all-start = ((bf16[8,96,256]{2,1,0:T(8,128)(2,1)}), bf16[8,96,256]{2,1,0:T(8,128)(2,1)S(1)}, u32[]{:S(2)}, u32[]{:S(2)}) async-start(bf16[8,96,256]{2,1,0:T(8,128)(2,1)} %get-tuple-element.69), calls=%async_computation | async-start | bytes 786432 | tf_op jit(solution)/shard_map/all_to_all | solution.py:277
  48.6 0.1 select_reduce_fusion.1
  48.7 5.1 %collective-permute-start.18 = (bf16[2,32,512]{2,1,0:T(8,128)(2,1)S(1)}, bf16[2,32,512]{2,1,0:T(8,128)(2,1)S(1)}, u32[]{:S(2)}, u32[]{:S(2)}) collective-permute-start(bf16[2,32,512]{2,1,0:T(8,128)(2,1)S(1)} %pad_maximum_fusion.2), channel_id=1, source_target_pairs={{0,48},{8,56},{16,0},{24,8},{32,16},{40,24},{48,32},{56,40},{64,11... | collective-permute-start | bytes 196616 | tf_op jit(solution)/shard_map/ppermute | solution.py:49
  53.8 0.7 %collective-permute-start.20 = (bf16[2,32,512]{2,1,0:T(8,128)(2,1)S(1)}, bf16[2,32,512]{2,1,0:T(8,128)(2,1)S(1)}, u32[]{:S(2)}, u32[]{:S(2)}) collective-permute-start(bf16[2,32,512]{2,1,0:T(8,128)(2,1)S(1)} %pad_maximum_fusion.2), channel_id=1, source_target_pairs={{0,16},{8,24},{16,32},{24,40},{32,48},{40,56},{48,0},{56,8},{64,80... | collective-permute-start | bytes 196616 | tf_op jit(solution)/shard_map/ppermute | solution.py:49
  54.5 0.9 %collective-permute-done.18 = bf16[2,32,512]{2,1,0:T(8,128)(2,1)S(1)} collective-permute-done((bf16[2,32,512]{2,1,0:T(8,128)(2,1)S(1)}, bf16[2,32,512]{2,1,0:T(8,128)(2,1)S(1)}, u32[]{:S(2)}, u32[]{:S(2)}) %collective-permute-start.18) | collective-permute-done | bytes 65568 | tf_op jit(solution)/shard_map/ppermute | solution.py:49
  55.4 3.1 %collective-permute-done.19 = bf16[2,32,512]{2,1,0:T(8,128)(2,1)S(1)} collective-permute-done((bf16[2,32,512]{2,1,0:T(8,128)(2,1)S(1)}, bf16[2,32,512]{2,1,0:T(8,128)(2,1)S(1)}, u32[]{:S(2)}, u32[]{:S(2)}) %collective-permute-start.19) | collective-permute-done | bytes 65568 | tf_op jit(solution)/shard_map/ppermute | solution.py:49
  58.5 0.6 collective-permute-done.20
  59.2 3.3 %collective-permute-start.21 = (bf16[4,2,32,512]{3,2,1,0:T(8,128)(2,1)S(1)}, bf16[4,2,32,512]{3,2,1,0:T(8,128)(2,1)S(1)}, u32[]{:S(2)}, u32[]{:S(2)}) collective-permute-start(bf16[4,2,32,512]{3,2,1,0:T(8,128)(2,1)S(1)} %get-tuple-element.79), channel_id=1, source_target_pairs={{0,8},{8,0},{16,24},{24,16},{32,40},{40,32},{48,56},{56,48},{64,72... | collective-permute-start | bytes 786440 | tf_op jit(solution)/shard_map/ppermute | solution.py:49
  62.5 0.2 select_reduce_fusion
  62.8 0.9 %scatter_fusion = bf16[8,96,256]{2,1,0:T(8,128)(2,1)S(1)} fusion(bf16[8,96,256]{2,1,0:T(8,128)(2,1)S(1)} %broadcast_in_dim.38, s32[8]{0:T(128)S(1)} %compare_select_fusion, bf16[8,96,256]{2,1,0:T(8,128)(2,1)S(1)} %all-to-all-done), kind=kCustom, calls=%fused_computation | custom fusion | bytes 1179680 | tf_op jit(solution)/shard_map/scatter | solution.py:294
  63.8 1.3 %convolution_convert_fusion = bf16[512,512]{1,0:T(8,128)(2,1)} fusion(bf16[512,512]{1,0:T(8,128)(2,1)S(1)} %bitcast.22, s32[512]{0:T(512)S(1)} %fusion.20), kind=kOutput, calls=%fused_computation.1 | convolution fusion | flops 268959744 | bytes 1050624 | tf_op jit(solution)/shard_map/dot_general | solution.py:291
  (46 shorter events, 0.3 us)
Async XLA Ops:
  3.1 4.5 %collective-permute-start.13 = (bf16[1,224,1024]{2,1,0:T(8,128)(2,1)S(1)}, bf16[1,224,1024]{2,1,0:T(8,128)(2,1)S(1)}, u32[]{:S(2)}, u32[]{:S(2)}) collective-permute-start(bf16[1,224,1024]{2,1,0:T(8,128)(2,1)S(1)} %get-tuple-element.44.refs_0_), channel_id=1, source_target_pairs={{0,8},{8,0},{16,24},{24,16},{32,40},{40,32},{48,56},{56,48},{64,72... | collective-permute-start | bytes 1376264 | tf_op jit(solution)/shard_map/ppermute | solution.py:49
  4.6 6.1 %collective-permute-start.9 = (bf16[1,224,1024]{2,1,0:T(8,128)(2,1)S(1)}, bf16[1,224,1024]{2,1,0:T(8,128)(2,1)S(1)}, u32[]{:S(2)}, u32[]{:S(2)}) collective-permute-start(bf16[1,224,1024]{2,1,0:T(8,128)(2,1)S(1)} %get-tuple-element.57), channel_id=1, source_target_pairs={{0,8},{8,0},{16,24},{24,16},{32,40},{40,32},{48,56},{56,48},{64,72... | collective-permute-start | bytes 1376264 | tf_op jit(solution)/shard_map/ppermute | solution.py:49
  7.1 8.5 %collective-permute-start.12 = (bf16[1,224,1024]{2,1,0:T(8,128)(2,1)S(1)}, bf16[1,224,1024]{2,1,0:T(8,128)(2,1)S(1)}, u32[]{:S(2)}, u32[]{:S(2)}) collective-permute-start(bf16[1,224,1024]{2,1,0:T(8,128)(2,1)S(1)} %get-tuple-element.45.refs_0_), channel_id=1, source_target_pairs={{0,8},{8,0},{16,24},{24,16},{32,40},{40,32},{48,56},{56,48},{64,72... | collective-permute-start | bytes 1376264 | tf_op jit(solution)/shard_map/ppermute | solution.py:49
  7.8 28.4 %copy-start.8 = (f32[8,12,16]{2,0,1:T(8,128)S(1)}, f32[8,12,16]{2,0,1:T(8,128)}, u32[]{:S(2)}) copy-start(f32[8,12,16]{2,0,1:T(8,128)} %param.21) | copy-start | bytes 18436
  7.8 29.7 %copy-start.3 = (f32[32,512]{1,0:T(8,128)S(1)}, f32[32,512]{1,0:T(8,128)}, u32[]{:S(2)}) copy-start(f32[32,512]{1,0:T(8,128)} %param.25) | copy-start | bytes 196612
  7.8 29.7 %copy-start.4 = (f32[32,512]{1,0:T(8,128)S(1)}, f32[32,512]{1,0:T(8,128)}, u32[]{:S(2)}) copy-start(f32[32,512]{1,0:T(8,128)} %moment.1) | copy-start | bytes 196612
  7.8 29.7 %copy-start.5 = (f32[32,512]{1,0:T(8,128)S(1)}, f32[32,512]{1,0:T(8,128)}, u32[]{:S(2)}) copy-start(f32[32,512]{1,0:T(8,128)} %variance.1) | copy-start | bytes 196612
  7.8 29.7 %copy-start.6 = (f32[4,4]{1,0:T(4,128)S(1)}, f32[4,4]{1,0:T(4,128)}, u32[]{:S(2)}) copy-start(f32[4,4]{1,0:T(4,128)} %scales.1) | copy-start | bytes 196
  7.8 8.3 %collective-permute-start.14 = (bf16[1,224,1024]{2,1,0:T(8,128)(2,1)S(1)}, bf16[1,224,1024]{2,1,0:T(8,128)(2,1)S(1)}, u32[]{:S(2)}, u32[]{:S(2)}) collective-permute-start(bf16[1,224,1024]{2,1,0:T(8,128)(2,1)S(1)} %add_convert_fusion.1), channel_id=1, source_target_pairs={{0,16},{8,56},{16,32},{24,8},{32,48},{40,24},{48,0},{56,40},{64,80... | collective-permute-start | bytes 1376264 | tf_op jit(solution)/shard_map/ppermute | solution.py:59
  10.9 30.2 %copy-start = (f32[1,96,2048]{2,1,0:T(8,128)S(1)}, f32[1,96,2048]{2,1,0:T(8,128)}, u32[]{:S(2)}) copy-start(f32[1,96,2048]{2,1,0:T(8,128)} %refs_4_.1) | copy-start | bytes 2359300
  10.9 30.2 %copy-start.1 = (f32[1,96,2048]{2,1,0:T(8,128)S(1)}, f32[1,96,2048]{2,1,0:T(8,128)}, u32[]{:S(2)}) copy-start(f32[1,96,2048]{2,1,0:T(8,128)} %refs_5_.1) | copy-start | bytes 2359300
  10.9 30.2 %copy-start.2 = (f32[1,96,2048]{2,1,0:T(8,128)S(1)}, f32[1,96,2048]{2,1,0:T(8,128)}, u32[]{:S(2)}) copy-start(f32[1,96,2048]{2,1,0:T(8,128)} %refs_6_.1) | copy-start | bytes 2359300
  10.9 37.7 %copy-start.9 = (s32[128]{0:T(128)S(1)}, s32[128]{0:T(128)}, u32[]{:S(2)}) copy-start(s32[128]{0:T(128)} %param.23) | copy-start | bytes 1540
  10.9 37.8 %copy-start.10 = (s32[8]{0:T(128)S(1)}, s32[8]{0:T(128)}, u32[]{:S(2)}) copy-start(s32[8]{0:T(128)} %param.24) | copy-start | bytes 100
  10.9 10.1 %collective-permute-start.10 = (bf16[1,224,1024]{2,1,0:T(8,128)(2,1)S(1)}, bf16[1,224,1024]{2,1,0:T(8,128)(2,1)S(1)}, u32[]{:S(2)}, u32[]{:S(2)}) collective-permute-start(bf16[1,224,1024]{2,1,0:T(8,128)(2,1)S(1)} %add_convert_fusion.2), channel_id=1, source_target_pairs={{0,16},{8,56},{16,32},{24,8},{32,48},{40,24},{48,0},{56,40},{64,80... | collective-permute-start | bytes 1376264 | tf_op jit(solution)/shard_map/ppermute | solution.py:59
  15.0 2.9 %collective-permute-start.5 = (bf16[1,192,1024]{2,1,0:T(8,128)(2,1)S(1)}, bf16[1,192,1024]{2,1,0:T(8,128)(2,1)S(1)}, u32[]{:S(2)}, u32[]{:S(2)}) collective-permute-start(bf16[1,192,1024]{2,1,0:T(8,128)(2,1)S(1)} %get-tuple-element.53), channel_id=1, source_target_pairs={{0,8},{8,0},{16,24},{24,16},{32,40},{40,32},{48,56},{56,48},{64,72... | collective-permute-start | bytes 1179656 | tf_op jit(solution)/shard_map/ppermute | solution.py:49
  15.1 9.5 %collective-permute-start.8 = (bf16[1,224,1024]{2,1,0:T(8,128)(2,1)S(1)}, bf16[1,224,1024]{2,1,0:T(8,128)(2,1)S(1)}, u32[]{:S(2)}, u32[]{:S(2)}) collective-permute-start(bf16[1,224,1024]{2,1,0:T(8,128)(2,1)S(1)} %get-tuple-element.55), channel_id=1, source_target_pairs={{0,8},{8,0},{16,24},{24,16},{32,40},{40,32},{48,56},{56,48},{64,72... | collective-permute-start | bytes 1376264 | tf_op jit(solution)/shard_map/ppermute | solution.py:49
  15.6 15.6 %collective-permute-start.4 = (bf16[1,192,1024]{2,1,0:T(8,128)(2,1)S(1)}, bf16[1,192,1024]{2,1,0:T(8,128)(2,1)S(1)}, u32[]{:S(2)}, u32[]{:S(2)}) collective-permute-start(bf16[1,192,1024]{2,1,0:T(8,128)(2,1)S(1)} %get-tuple-element.51), channel_id=1, source_target_pairs={{0,8},{8,0},{16,24},{24,16},{32,40},{40,32},{48,56},{56,48},{64,72... | collective-permute-start | bytes 1179656 | tf_op jit(solution)/shard_map/ppermute | solution.py:49
  16.1 6.6 %collective-permute-start.1 = (bf16[1,192,1024]{2,1,0:T(8,128)(2,1)S(1)}, bf16[1,192,1024]{2,1,0:T(8,128)(2,1)S(1)}, u32[]{:S(2)}, u32[]{:S(2)}) collective-permute-start(bf16[1,192,1024]{2,1,0:T(8,128)(2,1)S(1)} %get-tuple-element.49), channel_id=1, source_target_pairs={{0,8},{8,0},{16,24},{24,16},{32,40},{40,32},{48,56},{56,48},{64,72... | collective-permute-start | bytes 1179656 | tf_op jit(solution)/shard_map/ppermute | solution.py:49
  17.9 8.0 %collective-permute-start.15 = (bf16[1,224,1024]{2,1,0:T(8,128)(2,1)S(1)}, bf16[1,224,1024]{2,1,0:T(8,128)(2,1)S(1)}, u32[]{:S(2)}, u32[]{:S(2)}) collective-permute-start(bf16[1,224,1024]{2,1,0:T(8,128)(2,1)S(1)} %add_convert_fusion), channel_id=1, source_target_pairs={{0,16},{8,56},{16,32},{24,8},{32,48},{40,24},{48,0},{56,40},{64,80... | collective-permute-start | bytes 1376264 | tf_op jit(solution)/shard_map/ppermute | solution.py:59
  21.0 4.9 %collective-permute-start.11 = (bf16[1,224,1024]{2,1,0:T(8,128)(2,1)S(1)}, bf16[1,224,1024]{2,1,0:T(8,128)(2,1)S(1)}, u32[]{:S(2)}, u32[]{:S(2)}) collective-permute-start(bf16[1,224,1024]{2,1,0:T(8,128)(2,1)S(1)} %collective-permute-done.10), channel_id=1, source_target_pairs={{0,8},{8,0},{16,24},{24,16},{32,40},{40,32},{48,56},{56,48},{64,72... | collective-permute-start | bytes 1376264 | tf_op jit(solution)/shard_map/ppermute | solution.py:49
  22.7 8.5 %collective-permute-start.6 = (bf16[1,192,1024]{2,1,0:T(8,128)(2,1)S(1)}, bf16[1,192,1024]{2,1,0:T(8,128)(2,1)S(1)}, u32[]{:S(2)}, u32[]{:S(2)}) collective-permute-start(bf16[1,192,1024]{2,1,0:T(8,128)(2,1)S(1)} %add_convert_fusion.4), channel_id=1, source_target_pairs={{0,16},{8,56},{16,32},{24,8},{32,48},{40,24},{48,0},{56,40},{64,80... | collective-permute-start | bytes 1179656 | tf_op jit(solution)/shard_map/ppermute | solution.py:59
  24.6 9.8 %collective-permute-start.2 = (bf16[1,192,1024]{2,1,0:T(8,128)(2,1)S(1)}, bf16[1,192,1024]{2,1,0:T(8,128)(2,1)S(1)}, u32[]{:S(2)}, u32[]{:S(2)}) collective-permute-start(bf16[1,192,1024]{2,1,0:T(8,128)(2,1)S(1)} %add_convert_fusion.5), channel_id=1, source_target_pairs={{0,16},{8,56},{16,32},{24,8},{32,48},{40,24},{48,0},{56,40},{64,80... | collective-permute-start | bytes 1179656 | tf_op jit(solution)/shard_map/ppermute | solution.py:59
  26.3 11.2 %collective-permute-start.16 = (bf16[1,208,1024]{2,1,0:T(8,128)(2,1)S(1)}, bf16[1,208,1024]{2,1,0:T(8,128)(2,1)S(1)}, u32[]{:S(2)}, u32[]{:S(2)}) collective-permute-start(bf16[1,208,1024]{2,1,0:T(8,128)(2,1)S(1)} %slice.7), channel_id=1, source_target_pairs={{0,64},{8,72},{16,80},{24,88},{32,96},{40,104},{48,112},{56,120},{... | collective-permute-start | bytes 1277960 | tf_op jit(solution)/shard_map/ppermute | solution.py:49
  29.2 11.8 %collective-permute-start = (bf16[1,192,1024]{2,1,0:T(8,128)(2,1)S(1)}, bf16[1,192,1024]{2,1,0:T(8,128)(2,1)S(1)}, u32[]{:S(2)}, u32[]{:S(2)}) collective-permute-start(bf16[1,192,1024]{2,1,0:T(8,128)(2,1)S(1)} %get-tuple-element.47), channel_id=1, source_target_pairs={{0,8},{8,0},{16,24},{24,16},{32,40},{40,32},{48,56},{56,48},{64,72... | collective-permute-start | bytes 1179656 | tf_op jit(solution)/shard_map/ppermute | solution.py:49
  31.4 9.7 %collective-permute-start.7 = (bf16[1,192,1024]{2,1,0:T(8,128)(2,1)S(1)}, bf16[1,192,1024]{2,1,0:T(8,128)(2,1)S(1)}, u32[]{:S(2)}, u32[]{:S(2)}) collective-permute-start(bf16[1,192,1024]{2,1,0:T(8,128)(2,1)S(1)} %add_convert_fusion.3), channel_id=1, source_target_pairs={{0,16},{8,56},{16,32},{24,8},{32,48},{40,24},{48,0},{56,40},{64,80... | collective-permute-start | bytes 1179656 | tf_op jit(solution)/shard_map/ppermute | solution.py:59
  34.4 6.7 %collective-permute-start.3 = (bf16[1,192,1024]{2,1,0:T(8,128)(2,1)S(1)}, bf16[1,192,1024]{2,1,0:T(8,128)(2,1)S(1)}, u32[]{:S(2)}, u32[]{:S(2)}) collective-permute-start(bf16[1,192,1024]{2,1,0:T(8,128)(2,1)S(1)} %collective-permute-done.2), channel_id=1, source_target_pairs={{0,8},{8,0},{16,24},{24,16},{32,40},{40,32},{48,56},{56,48},{64,72... | collective-permute-start | bytes 1179656 | tf_op jit(solution)/shard_map/ppermute | solution.py:49
  38.3 5.3 %collective-permute-start.17 = (bf16[32,512]{1,0:T(8,128)(2,1)S(1)}, bf16[32,512]{1,0:T(8,128)(2,1)S(1)}, u32[]{:S(2)}, u32[]{:S(2)}) collective-permute-start(bf16[32,512]{1,0:T(8,128)(2,1)S(1)} %get-tuple-element.66), channel_id=1, source_target_pairs={{0,64},{8,72},{16,80},{24,88},{32,96},{40,104},{48,112},{56,120},{... | collective-permute-start | bytes 98312 | tf_op jit(solution)/shard_map/ppermute | solution.py:49
  43.5 15.6 %all-to-all-start = ((bf16[8,96,256]{2,1,0:T(8,128)(2,1)}), bf16[8,96,256]{2,1,0:T(8,128)(2,1)S(1)}, u32[]{:S(2)}, u32[]{:S(2)}) async-start(bf16[8,96,256]{2,1,0:T(8,128)(2,1)} %get-tuple-element.69), calls=%async_computation | async-start | bytes 786432 | tf_op jit(solution)/shard_map/all_to_all | solution.py:277
  48.7 6.7 %collective-permute-start.18 = (bf16[2,32,512]{2,1,0:T(8,128)(2,1)S(1)}, bf16[2,32,512]{2,1,0:T(8,128)(2,1)S(1)}, u32[]{:S(2)}, u32[]{:S(2)}) collective-permute-start(bf16[2,32,512]{2,1,0:T(8,128)(2,1)S(1)} %pad_maximum_fusion.2), channel_id=1, source_target_pairs={{0,48},{8,56},{16,0},{24,8},{32,16},{40,24},{48,32},{56,40},{64,11... | collective-permute-start | bytes 196616 | tf_op jit(solution)/shard_map/ppermute | solution.py:49
  53.8 4.7 %collective-permute-start.19 = (bf16[2,32,512]{2,1,0:T(8,128)(2,1)S(1)}, bf16[2,32,512]{2,1,0:T(8,128)(2,1)S(1)}, u32[]{:S(2)}, u32[]{:S(2)}) collective-permute-start(bf16[2,32,512]{2,1,0:T(8,128)(2,1)S(1)} %pad_maximum_fusion.2), channel_id=1, source_target_pairs={{0,32},{8,40},{16,48},{24,56},{32,0},{40,8},{48,16},{56,24},{64,96... | collective-permute-start | bytes 196616 | tf_op jit(solution)/shard_map/ppermute | solution.py:49
  53.8 5.3 %collective-permute-start.20 = (bf16[2,32,512]{2,1,0:T(8,128)(2,1)S(1)}, bf16[2,32,512]{2,1,0:T(8,128)(2,1)S(1)}, u32[]{:S(2)}, u32[]{:S(2)}) collective-permute-start(bf16[2,32,512]{2,1,0:T(8,128)(2,1)S(1)} %pad_maximum_fusion.2), channel_id=1, source_target_pairs={{0,16},{8,24},{16,32},{24,40},{32,48},{40,56},{48,0},{56,8},{64,80... | collective-permute-start | bytes 196616 | tf_op jit(solution)/shard_map/ppermute | solution.py:49
  59.2 4.6 %collective-permute-start.21 = (bf16[4,2,32,512]{3,2,1,0:T(8,128)(2,1)S(1)}, bf16[4,2,32,512]{3,2,1,0:T(8,128)(2,1)S(1)}, u32[]{:S(2)}, u32[]{:S(2)}) collective-permute-start(bf16[4,2,32,512]{3,2,1,0:T(8,128)(2,1)S(1)} %get-tuple-element.79), channel_id=1, source_target_pairs={{0,8},{8,0},{16,24},{24,16},{32,40},{40,32},{48,56},{56,48},{64,72... | collective-permute-start | bytes 786440 | tf_op jit(solution)/shard_map/ppermute | solution.py:49
  63.7 1.4 %copy-start.7 = (bf16[8,96,256]{2,1,0:T(8,128)(2,1)}, bf16[8,96,256]{2,1,0:T(8,128)(2,1)S(1)}, u32[]{:S(2)}) copy-start(bf16[8,96,256]{2,1,0:T(8,128)(2,1)S(1)} %scatter_fusion) | copy-start | bytes 1179652

commit v5 on v4

--- a/solution.py
+++ b/solution.py
@@ -162,7 +162,7 @@
 
 
 def update_kernel(*refs):
-    terms, (param, moment, variance, scales), results, grid = refs[:4], refs[4:8], refs[8:11], refs[11]
+    terms, (param, moment, variance, scales), results, grid = refs[:5], refs[5:9], refs[9:12], refs[12]
     start = lax.axis_index("dp") * ROWS
     low = start // BLOCK
     expert = lax.axis_index("expert")
@@ -179,8 +179,9 @@
             held = pl.ds(k % 8 * BLOCK, BLOCK)
             rows = pl.ds(k // 8 * ROWS, ROWS)
             grad = terms[0][0, rows, held].astype(F32)
-            for term in terms[1:]:
+            for term in terms[1:3]:
                 grad = grad + term[0, rows, held].astype(F32)
+            grad = grad + terms[3 + k // 8][0, :ROWS, held].astype(F32)
             new = adam_update(param[0, :, columns], moment[0, :, columns], variance[0, :, columns], grad)
             for result, value in zip(results, new):
                 result[0, :, columns] = value
@@ -195,7 +196,7 @@
         for k in range(KCOLS // BLOCK):
             columns = pl.ds(k * BLOCK, BLOCK)
             held = pl.ds(part * KCOLS + k * BLOCK, BLOCK)
-            grad = own[0, FOLD + KFOLD :, held] + arrived[0, FOLD:, held].astype(F32)
+            grad = own[0, FOLD + KFOLD :, held] + arrived[0, ROWS:, held].astype(F32)
             new = adam_update(param[rows, columns], moment[rows, columns], variance[rows, columns], grad)
             for result, value in zip(results, new):
                 result[rows, columns] = value
@@ -249,7 +250,8 @@
     far_c = ring(plus(keeps_c[0], got_c[0]).astype(BF))
     plain_c = ring(plus(keeps_c[1], got_c[1]).astype(BF))
     turned = plus(keeps_b[1], got_b[1], cross, near)
-    x_last = send(turned[:, : FOLD + KFOLD].astype(BF), 1, 0, 0)
+    x_late = send(turned[:, :ROWS].astype(BF), 1, 0, 0)
+    x_last = send(turned[:, ROWS : FOLD + KFOLD].astype(BF), 1, 0, 0)
     near_c = ring(plus(keeps_c[2], got_c[2], far_c).astype(BF))
     cross_c = send(plain_c, 0, 0, 1)
     stayed = plus(keeps_c[3], got_c[3]).astype(BF)
@@ -262,10 +264,11 @@
         key_scales,
         (KROWS, KCOLS),
     )
+    key_grid, x_late = lax.optimization_barrier((key_grid, x_late))
     chip_x = send(key_grid, 1, 0, 0)
     new_ep, new_em, new_es, blocks = update(
         update_kernel,
-        (stayed, cross_c, near_c, x_last),
+        (stayed, cross_c, near_c, x_late, x_last),
         expert_param,
         expert_moment,
         expert_second,

time: 65.4 us -> 65 us (level)
  starting transfers between devices: 38.7 us -> 33.7 us
  waiting for transfers between devices: 9.61 us -> 14.2 us
    ppermute x16 -> x17, starting transfers between devices: 24.2 us -> 17.9 us  [send(): return lax.ppermute(value, 'dp', dp_perm(dx, dy, dc))]
    ppermute x16 -> x17, waiting for transfers between devices: 6.02 us -> 8.79 us  [send(): return lax.ppermute(value, 'dp', dp_perm(dx, dy, dc))]
    all_to_all x1, waiting for transfers between devices: 0.01 us -> 1.41 us  [on_device(): lax.all_to_all(blocks, 'expert', split_axis=0, concat_axis=0, tiled=True)]
    ppermute x6, starting transfers between devices: 9.42 us -> 10.7 us  [ring(): return lax.ppermute(value, 'dp', pairs)]
  transfers between devices with their start and end apart: 23 -> 24, of which waited for: 8 -> 10; matrix products, arithmetic and copies ran while one was open for 4% -> 4% of each run, Pallas kernels for 14% -> 14%
where the time goes in v5:
time: 65 us; the launch traced here: 64.7 us
  starting transfers between devices  33.7 us (52%)
  waiting for transfers between devices  14.2 us (22%)
  Pallas kernels  11.5 us (18%)
  other arithmetic  1.97 us (3%)
  matrix products  1.35 us (2%)
  local copies, waits for them, and re-layouts  1.06 us (2%)
  between operations  1.03 us (2%)
    ppermute x17, starting transfers between devices, send(): return lax.ppermute(value, 'dp', dp_perm(dx, dy, dc))  17.9 us
    ppermute x6, starting transfers between devices, ring(): return lax.ppermute(value, 'dp', pairs)  10.7 us
    ppermute x17, waiting for transfers between devices, send(): return lax.ppermute(value, 'dp', dp_perm(dx, dy, dc))  8.79 us
    pallas_call x3, Pallas kernels, load(): pl.pallas_call(functools.partial(load_kernel, batch, roles, len(late)), o...  8.32 us
    all_to_all x1, starting transfers between devices, on_device(): lax.all_to_all(blocks, 'expert', split_axis=0, concat_axis=0, tiled=True)  5.07 us
    ppermute x6, waiting for transfers between devices, ring(): return lax.ppermute(value, 'dp', pairs)  3.99 us
    pallas_call x2, Pallas kernels, update(): pl.pallas_call(kernel, out_shape=[jax.ShapeDtypeStruct(param.shape, F32)]...  3.14 us
    all_to_all x1, waiting for transfers between devices, on_device(): lax.all_to_all(blocks, 'expert', split_axis=0, concat_axis=0, tiled=True)  1.41 us
  transfers between devices with their start and end apart: 24, of which 10 were waited for; matrix products, arithmetic and copies ran while one was open for 4% of the time, Pallas kernels for 14%

profile of v5, /device:TPU:1, one launch (start us, length us, event | category | flops | bytes accessed | tf_op | source)
XLA Modules:
  0.0 64.7 jit_solution(9145758861946998813)
XLA Ops:
  0.7 2.4 %shard_map.179 = (bf16[1,224,1024]{2,1,0:T(8,128)(2,1)S(1)}, bf16[1,224,1024]{2,1,0:T(8,128)(2,1)S(1)}, bf16[1,224,1024]{2,1,0:T(8,128)(2,1)S(1)}, bf16[1,224,1024]{2,1,0:T(8,128)(2,1)S(1)}) custom-call(f32[16,96,2048]{2,1,0:T(8,128)} %bitcast.15, f32[16,32,512]{2,1,0:T(8,128)} %bitcast.18), custom_call_target="tpu_custom_call" | custom-call | flops 1000 | bytes 1000 | tf_op jit(solution)/shard_map/pallas_call | solution.py:142
  3.1 1.5 %collective-permute-start.13 = (bf16[1,224,1024]{2,1,0:T(8,128)(2,1)S(1)}, bf16[1,224,1024]{2,1,0:T(8,128)(2,1)S(1)}, u32[]{:S(2)}, u32[]{:S(2)}) collective-permute-start(bf16[1,224,1024]{2,1,0:T(8,128)(2,1)S(1)} %get-tuple-element.46.refs_0_), channel_id=1, source_target_pairs={{0,8},{8,0},{16,24},{24,16},{32,40},{40,32},{48,56},{56,48},{64,72... | collective-permute-start | bytes 1376264 | tf_op jit(solution)/shard_map/ppermute | solution.py:49
  4.6 0.1 collective-permute-start.9
  4.7 2.4 %shard_map.180 = (bf16[1,224,1024]{2,1,0:T(8,128)(2,1)S(1)}, bf16[1,224,1024]{2,1,0:T(8,128)(2,1)S(1)}, bf16[1,224,1024]{2,1,0:T(8,128)(2,1)S(1)}, bf16[1,224,1024]{2,1,0:T(8,128)(2,1)S(1)}) custom-call(f32[16,96,2048]{2,1,0:T(8,128)} %bitcast.16, f32[16,32,512]{2,1,0:T(8,128)} %bitcast.19, bf16[1,224,1024]{2,1,0:T(8,128)(2,1)S(1)} %get-tuple-element.46.refs_0_), custom_call_target="tpu_custom_call" | custom-call | flops 1000 | bytes 1000 | tf_op jit(solution)/shard_map/pallas_call | solution.py:142
  7.1 0.5 collective-permute-start.12
  7.6 0.2 add_convert_fusion.1
  7.7 2.9 %collective-permute-start.14 = (bf16[1,224,1024]{2,1,0:T(8,128)(2,1)S(1)}, bf16[1,224,1024]{2,1,0:T(8,128)(2,1)S(1)}, u32[]{:S(2)}, u32[]{:S(2)}) collective-permute-start(bf16[1,224,1024]{2,1,0:T(8,128)(2,1)S(1)} %add_convert_fusion.1), channel_id=1, source_target_pairs={{0,16},{8,56},{16,32},{24,8},{32,48},{40,24},{48,0},{56,40},{64,80... | collective-permute-start | bytes 1376264 | tf_op jit(solution)/shard_map/ppermute | solution.py:59
  10.7 0.2 add_convert_fusion.2
  10.9 0.5 collective-permute-start.10
  11.4 3.5 %shard_map.181 = (bf16[1,192,1024]{2,1,0:T(8,128)(2,1)S(1)}, bf16[1,192,1024]{2,1,0:T(8,128)(2,1)S(1)}, bf16[1,192,1024]{2,1,0:T(8,128)(2,1)S(1)}, bf16[1,192,10...) custom-call(f32[16,96,2048]{2,1,0:T(8,128)} %bitcast.17, ...), custom_call_target="tpu_custom_call" | custom-call | flops 1000 | bytes 1000 | tf_op jit(solution)/shard_map/pallas_call | solution.py:142
  15.1 0.5 collective-permute-start.8
  15.6 0.1 collective-permute-start.4
  15.7 0.4 collective-permute-done.14
  16.1 1.5 %collective-permute-start.1 = (bf16[1,192,1024]{2,1,0:T(8,128)(2,1)S(1)}, bf16[1,192,1024]{2,1,0:T(8,128)(2,1)S(1)}, u32[]{:S(2)}, u32[]{:S(2)}) collective-permute-start(bf16[1,192,1024]{2,1,0:T(8,128)(2,1)S(1)} %get-tuple-element.51), channel_id=1, source_target_pairs={{0,8},{8,0},{16,24},{24,16},{32,40},{40,32},{48,56},{56,48},{64,72... | collective-permute-start | bytes 1179656 | tf_op jit(solution)/shard_map/ppermute | solution.py:49
  17.6 0.2 add_convert_fusion
  17.9 1.7 %collective-permute-start.15 = (bf16[1,224,1024]{2,1,0:T(8,128)(2,1)S(1)}, bf16[1,224,1024]{2,1,0:T(8,128)(2,1)S(1)}, u32[]{:S(2)}, u32[]{:S(2)}) collective-permute-start(bf16[1,224,1024]{2,1,0:T(8,128)(2,1)S(1)} %add_convert_fusion), channel_id=1, source_target_pairs={{0,16},{8,56},{16,32},{24,8},{32,48},{40,24},{48,0},{56,40},{64,80... | collective-permute-start | bytes 1376264 | tf_op jit(solution)/shard_map/ppermute | solution.py:59
  19.5 1.4 %collective-permute-done.10 = bf16[1,224,1024]{2,1,0:T(8,128)(2,1)S(1)} collective-permute-done((bf16[1,224,1024]{2,1,0:T(8,128)(2,1)S(1)}, bf16[1,224,1024]{2,1,0:T(8,128)(2,1)S(1)}, u32[]{:S(2)}, u32[]{:S(2)}) %collective-permute-start.10) | collective-permute-done | bytes 458784 | tf_op jit(solution)/shard_map/ppermute | solution.py:59
  21.0 1.5 %collective-permute-start.11 = (bf16[1,224,1024]{2,1,0:T(8,128)(2,1)S(1)}, bf16[1,224,1024]{2,1,0:T(8,128)(2,1)S(1)}, u32[]{:S(2)}, u32[]{:S(2)}) collective-permute-start(bf16[1,224,1024]{2,1,0:T(8,128)(2,1)S(1)} %collective-permute-done.10), channel_id=1, source_target_pairs={{0,8},{8,0},{16,24},{24,16},{32,40},{40,32},{48,56},{56,48},{64,72... | collective-permute-start | bytes 1376264 | tf_op jit(solution)/shard_map/ppermute | solution.py:49
  22.5 0.1 add_convert_fusion.4
  22.7 1.7 %collective-permute-start.6 = (bf16[1,192,1024]{2,1,0:T(8,128)(2,1)S(1)}, bf16[1,192,1024]{2,1,0:T(8,128)(2,1)S(1)}, u32[]{:S(2)}, u32[]{:S(2)}) collective-permute-start(bf16[1,192,1024]{2,1,0:T(8,128)(2,1)S(1)} %add_convert_fusion.4), channel_id=1, source_target_pairs={{0,16},{8,56},{16,32},{24,8},{32,48},{40,24},{48,0},{56,40},{64,80... | collective-permute-start | bytes 1179656 | tf_op jit(solution)/shard_map/ppermute | solution.py:59
  24.3 0.1 add_convert_fusion.5
  24.5 0.1 collective-permute-start
  24.6 1.3 %collective-permute-done.15 = bf16[1,224,1024]{2,1,0:T(8,128)(2,1)S(1)} collective-permute-done((bf16[1,224,1024]{2,1,0:T(8,128)(2,1)S(1)}, bf16[1,224,1024]{2,1,0:T(8,128)(2,1)S(1)}, u32[]{:S(2)}, u32[]{:S(2)}) %collective-permute-start.15) | collective-permute-done | bytes 458784 | tf_op jit(solution)/shard_map/ppermute | solution.py:59
  25.9 3.1 %collective-permute-start.2 = (bf16[1,192,1024]{2,1,0:T(8,128)(2,1)S(1)}, bf16[1,192,1024]{2,1,0:T(8,128)(2,1)S(1)}, u32[]{:S(2)}, u32[]{:S(2)}) collective-permute-start(bf16[1,192,1024]{2,1,0:T(8,128)(2,1)S(1)} %add_convert_fusion.5), channel_id=1, source_target_pairs={{0,16},{8,56},{16,32},{24,8},{32,48},{40,24},{48,0},{56,40},{64,80... | collective-permute-start | bytes 1179656 | tf_op jit(solution)/shard_map/ppermute | solution.py:59
  29.0 0.3 fusion.30
  29.4 2.8 %collective-permute-start.16 = (bf16[1,112,1024]{2,1,0:T(8,128)(2,1)S(1)}, bf16[1,112,1024]{2,1,0:T(8,128)(2,1)S(1)}, u32[]{:S(2)}, u32[]{:S(2)}) collective-permute-start(bf16[1,112,1024]{2,1,0:T(8,128)(2,1)S(1)} %slice.10), channel_id=1, source_target_pairs={{0,64},{8,72},{16,80},{24,88},{32,96},{40,104},{48,112},{56,120},{... | collective-permute-start | bytes 688136 | tf_op jit(solution)/shard_map/ppermute | solution.py:49
  32.2 0.2 collective-permute-start.17
  32.4 0.2 add_convert_fusion.3
  32.6 0.8 %collective-permute-start.7 = (bf16[1,192,1024]{2,1,0:T(8,128)(2,1)S(1)}, bf16[1,192,1024]{2,1,0:T(8,128)(2,1)S(1)}, u32[]{:S(2)}, u32[]{:S(2)}) collective-permute-start(bf16[1,192,1024]{2,1,0:T(8,128)(2,1)S(1)} %add_convert_fusion.3), channel_id=1, source_target_pairs={{0,16},{8,56},{16,32},{24,8},{32,48},{40,24},{48,0},{56,40},{64,80... | collective-permute-start | bytes 1179656 | tf_op jit(solution)/shard_map/ppermute | solution.py:59
  33.5 0.8 %collective-permute-done.2 = bf16[1,192,1024]{2,1,0:T(8,128)(2,1)S(1)} collective-permute-done((bf16[1,192,1024]{2,1,0:T(8,128)(2,1)S(1)}, bf16[1,192,1024]{2,1,0:T(8,128)(2,1)S(1)}, u32[]{:S(2)}, u32[]{:S(2)}) %collective-permute-start.2) | collective-permute-done | bytes 393248 | tf_op jit(solution)/shard_map/ppermute | solution.py:59
  34.3 2.3 %collective-permute-start.3 = (bf16[1,192,1024]{2,1,0:T(8,128)(2,1)S(1)}, bf16[1,192,1024]{2,1,0:T(8,128)(2,1)S(1)}, u32[]{:S(2)}, u32[]{:S(2)}) collective-permute-start(bf16[1,192,1024]{2,1,0:T(8,128)(2,1)S(1)} %collective-permute-done.2), channel_id=1, source_target_pairs={{0,8},{8,0},{16,24},{24,16},{32,40},{40,32},{48,56},{56,48},{64,72... | collective-permute-start | bytes 1179656 | tf_op jit(solution)/shard_map/ppermute | solution.py:49
  36.6 1.9 %collective-permute-done.16.arrived.refs_4_ = bf16[1,112,1024]{2,1,0:T(8,128)(2,1)S(1)} collective-permute-done((bf16[1,112,1024]{2,1,0:T(8,128)(2,1)S(1)}, bf16[1,112,1024]{2,1,0:T(8,128)(2,1)S(1)}, u32[]{:S(2)}, u32[]{:S(2)}) %collective-permute-start.16) | collective-permute-done | bytes 229408 | tf_op jit(solution)/shard_map/ppermute | solution.py:49
  38.6 0.7 %shard_map.182 = (f32[32,512]{1,0:T(8,128)}, f32[32,512]{1,0:T(8,128)}, f32[32,512]{1,0:T(8,128)}, bf16[32,512]{1,0:T(8,128)(2,1)S(1)}) custom-call(f32[1,224,1024]{2,1,0:T(8,128)S(1)} %get-tuple-element.83.own, bf16[1,112,1024]{2,1,0:T(8,128)(2,1)S(1)} %collective-permute-done.16.arrived.refs_4_, f32[32,512]{1,0:T(8,128)S(1)} %copy-done.3, ...), custom_call_target="tpu_custom_call" | custom-call | flops 1000 | bytes 1000 | tf_op jit(solution)/shard_map/pallas_call | solution.py:209
  39.3 2.5 %collective-permute-done.17.refs_3_ = bf16[1,96,1024]{2,1,0:T(8,128)(2,1)S(1)} collective-permute-done((bf16[1,96,1024]{2,1,0:T(8,128)(2,1)S(1)}, bf16[1,96,1024]{2,1,0:T(8,128)(2,1)S(1)}, u32[]{:S(2)}, u32[]{:S(2)}) %collective-permute-start.17) | collective-permute-done | bytes 196640 | tf_op jit(solution)/shard_map/ppermute | solution.py:49
  41.8 2.8 %collective-permute-start.18 = (bf16[32,512]{1,0:T(8,128)(2,1)S(1)}, bf16[32,512]{1,0:T(8,128)(2,1)S(1)}, u32[]{:S(2)}, u32[]{:S(2)}) collective-permute-start(bf16[32,512]{1,0:T(8,128)(2,1)S(1)} %get-tuple-element.70), channel_id=1, source_target_pairs={{0,64},{8,72},{16,80},{24,88},{32,96},{40,104},{48,112},{56,120},{... | collective-permute-start | bytes 98312 | tf_op jit(solution)/shard_map/ppermute | solution.py:49
  44.6 0.1 add_convert_fusion.6.refs_0_
  44.8 2.4 %shard_map.183 = (f32[1,96,2048]{2,1,0:T(8,128)}, f32[1,96,2048]{2,1,0:T(8,128)}, f32[1,96,2048]{2,1,0:T(8,128)}, bf16[8,96,256]{2,1,0:T(8,128)(2,1)}) custom-call(bf16[1,192,1024]{2,1,0:T(8,128)(2,1)S(1)} %add_convert_fusion.6.refs_0_, bf16[1,192,1024]{2,1,0:T(8,128)(2,1)S(1)} %collective-permute-done.3.refs_1_, ...), custom_call_target="tpu_custom_call" | custom-call | flops 1000 | bytes 1000 | tf_op jit(solution)/shard_map/pallas_call | solution.py:209
  47.2 5.1 %all-to-all-start = ((bf16[8,96,256]{2,1,0:T(8,128)(2,1)}), bf16[8,96,256]{2,1,0:T(8,128)(2,1)S(1)}, u32[]{:S(2)}, u32[]{:S(2)}) async-start(bf16[8,96,256]{2,1,0:T(8,128)(2,1)} %get-tuple-element.73), calls=%async_computation | async-start | bytes 786432 | tf_op jit(solution)/shard_map/all_to_all | solution.py:280
  52.3 0.1 select_reduce_fusion.1
  52.6 1.4 %collective-permute-start.21 = (bf16[2,32,512]{2,1,0:T(8,128)(2,1)S(1)}, bf16[2,32,512]{2,1,0:T(8,128)(2,1)S(1)}, u32[]{:S(2)}, u32[]{:S(2)}) collective-permute-start(bf16[2,32,512]{2,1,0:T(8,128)(2,1)S(1)} %pad_maximum_fusion.2), channel_id=1, source_target_pairs={{0,16},{8,24},{16,32},{24,40},{32,48},{40,56},{48,0},{56,8},{64,80... | collective-permute-start | bytes 196616 | tf_op jit(solution)/shard_map/ppermute | solution.py:49
  54.0 1.6 %collective-permute-done.19 = bf16[2,32,512]{2,1,0:T(8,128)(2,1)S(1)} collective-permute-done((bf16[2,32,512]{2,1,0:T(8,128)(2,1)S(1)}, bf16[2,32,512]{2,1,0:T(8,128)(2,1)S(1)}, u32[]{:S(2)}, u32[]{:S(2)}) %collective-permute-start.19) | collective-permute-done | bytes 65568 | tf_op jit(solution)/shard_map/ppermute | solution.py:49
  55.6 1.6 %collective-permute-done.20 = bf16[2,32,512]{2,1,0:T(8,128)(2,1)S(1)} collective-permute-done((bf16[2,32,512]{2,1,0:T(8,128)(2,1)S(1)}, bf16[2,32,512]{2,1,0:T(8,128)(2,1)S(1)}, u32[]{:S(2)}, u32[]{:S(2)}) %collective-permute-start.20) | collective-permute-done | bytes 65568 | tf_op jit(solution)/shard_map/ppermute | solution.py:49
  57.2 1.1 %collective-permute-done.21 = bf16[2,32,512]{2,1,0:T(8,128)(2,1)S(1)} collective-permute-done((bf16[2,32,512]{2,1,0:T(8,128)(2,1)S(1)}, bf16[2,32,512]{2,1,0:T(8,128)(2,1)S(1)}, u32[]{:S(2)}, u32[]{:S(2)}) %collective-permute-start.21) | collective-permute-done | bytes 65568 | tf_op jit(solution)/shard_map/ppermute | solution.py:49
  58.3 1.4 %all-to-all-done = bf16[8,96,256]{2,1,0:T(8,128)(2,1)S(1)} async-done(((bf16[8,96,256]{2,1,0:T(8,128)(2,1)}), bf16[8,96,256]{2,1,0:T(8,128)(2,1)S(1)}, u32[]{:S(2)}, u32[]{:S(2)}) %all-to-all-start) | async-done | bytes 393248 | tf_op jit(solution)/shard_map/all_to_all | solution.py:280
  59.8 2.3 %collective-permute-start.22 = (bf16[4,2,32,512]{3,2,1,0:T(8,128)(2,1)S(1)}, bf16[4,2,32,512]{3,2,1,0:T(8,128)(2,1)S(1)}, u32[]{:S(2)}, u32[]{:S(2)}) collective-permute-start(bf16[4,2,32,512]{3,2,1,0:T(8,128)(2,1)S(1)} %get-tuple-element.85), channel_id=1, source_target_pairs={{0,8},{8,0},{16,24},{24,16},{32,40},{40,32},{48,56},{56,48},{64,72... | collective-permute-start | bytes 786440 | tf_op jit(solution)/shard_map/ppermute | solution.py:49
  62.1 0.2 select_reduce_fusion
  62.4 0.9 %scatter_fusion = bf16[8,96,256]{2,1,0:T(8,128)(2,1)S(1)} fusion(bf16[8,96,256]{2,1,0:T(8,128)(2,1)S(1)} %broadcast_in_dim.38, s32[8]{0:T(128)S(1)} %compare_select_fusion, bf16[8,96,256]{2,1,0:T(8,128)(2,1)S(1)} %all-to-all-done), kind=kCustom, calls=%fused_computation | custom fusion | bytes 1179680 | tf_op jit(solution)/shard_map/scatter | solution.py:297
  63.4 1.3 %convolution_convert_fusion = bf16[512,512]{1,0:T(8,128)(2,1)} fusion(bf16[512,512]{1,0:T(8,128)(2,1)S(1)} %bitcast.22, s32[512]{0:T(512)S(1)} %fusion.20), kind=kOutput, calls=%fused_computation.1 | convolution fusion | flops 268959744 | bytes 1050624 | tf_op jit(solution)/shard_map/dot_general | solution.py:294
  (49 shorter events, 0.6 us)
Async XLA Ops:
  3.1 4.5 %collective-permute-start.13 = (bf16[1,224,1024]{2,1,0:T(8,128)(2,1)S(1)}, bf16[1,224,1024]{2,1,0:T(8,128)(2,1)S(1)}, u32[]{:S(2)}, u32[]{:S(2)}) collective-permute-start(bf16[1,224,1024]{2,1,0:T(8,128)(2,1)S(1)} %get-tuple-element.46.refs_0_), channel_id=1, source_target_pairs={{0,8},{8,0},{16,24},{24,16},{32,40},{40,32},{48,56},{56,48},{64,72... | collective-permute-start | bytes 1376264 | tf_op jit(solution)/shard_map/ppermute | solution.py:49
  4.6 6.0 %collective-permute-start.9 = (bf16[1,224,1024]{2,1,0:T(8,128)(2,1)S(1)}, bf16[1,224,1024]{2,1,0:T(8,128)(2,1)S(1)}, u32[]{:S(2)}, u32[]{:S(2)}) collective-permute-start(bf16[1,224,1024]{2,1,0:T(8,128)(2,1)S(1)} %get-tuple-element.59), channel_id=1, source_target_pairs={{0,8},{8,0},{16,24},{24,16},{32,40},{40,32},{48,56},{56,48},{64,72... | collective-permute-start | bytes 1376264 | tf_op jit(solution)/shard_map/ppermute | solution.py:49
  7.1 8.5 %collective-permute-start.12 = (bf16[1,224,1024]{2,1,0:T(8,128)(2,1)S(1)}, bf16[1,224,1024]{2,1,0:T(8,128)(2,1)S(1)}, u32[]{:S(2)}, u32[]{:S(2)}) collective-permute-start(bf16[1,224,1024]{2,1,0:T(8,128)(2,1)S(1)} %get-tuple-element.47.refs_0_), channel_id=1, source_target_pairs={{0,8},{8,0},{16,24},{24,16},{32,40},{40,32},{48,56},{56,48},{64,72... | collective-permute-start | bytes 1376264 | tf_op jit(solution)/shard_map/ppermute | solution.py:49
  7.7 8.3 %collective-permute-start.14 = (bf16[1,224,1024]{2,1,0:T(8,128)(2,1)S(1)}, bf16[1,224,1024]{2,1,0:T(8,128)(2,1)S(1)}, u32[]{:S(2)}, u32[]{:S(2)}) collective-permute-start(bf16[1,224,1024]{2,1,0:T(8,128)(2,1)S(1)} %add_convert_fusion.1), channel_id=1, source_target_pairs={{0,16},{8,56},{16,32},{24,8},{32,48},{40,24},{48,0},{56,40},{64,80... | collective-permute-start | bytes 1376264 | tf_op jit(solution)/shard_map/ppermute | solution.py:59
  10.6 26.0 %copy-start.8 = (f32[8,12,16]{2,0,1:T(8,128)S(1)}, f32[8,12,16]{2,0,1:T(8,128)}, u32[]{:S(2)}) copy-start(f32[8,12,16]{2,0,1:T(8,128)} %param.21) | copy-start | bytes 18436
  10.6 27.9 %copy-start.3 = (f32[32,512]{1,0:T(8,128)S(1)}, f32[32,512]{1,0:T(8,128)}, u32[]{:S(2)}) copy-start(f32[32,512]{1,0:T(8,128)} %param.25) | copy-start | bytes 196612
  10.6 27.9 %copy-start.4 = (f32[32,512]{1,0:T(8,128)S(1)}, f32[32,512]{1,0:T(8,128)}, u32[]{:S(2)}) copy-start(f32[32,512]{1,0:T(8,128)} %moment.1) | copy-start | bytes 196612
  10.7 27.9 %copy-start.5 = (f32[32,512]{1,0:T(8,128)S(1)}, f32[32,512]{1,0:T(8,128)}, u32[]{:S(2)}) copy-start(f32[32,512]{1,0:T(8,128)} %variance.1) | copy-start | bytes 196612
  10.7 27.9 %copy-start.6 = (f32[4,4]{1,0:T(4,128)S(1)}, f32[4,4]{1,0:T(4,128)}, u32[]{:S(2)}) copy-start(f32[4,4]{1,0:T(4,128)} %scales.1) | copy-start | bytes 196
  10.8 34.0 %copy-start = (f32[1,96,2048]{2,1,0:T(8,128)S(1)}, f32[1,96,2048]{2,1,0:T(8,128)}, u32[]{:S(2)}) copy-start(f32[1,96,2048]{2,1,0:T(8,128)} %refs_5_.1) | copy-start | bytes 2359300
  10.9 34.0 %copy-start.1 = (f32[1,96,2048]{2,1,0:T(8,128)S(1)}, f32[1,96,2048]{2,1,0:T(8,128)}, u32[]{:S(2)}) copy-start(f32[1,96,2048]{2,1,0:T(8,128)} %refs_6_.1) | copy-start | bytes 2359300
  10.9 33.9 %copy-start.2 = (f32[1,96,2048]{2,1,0:T(8,128)S(1)}, f32[1,96,2048]{2,1,0:T(8,128)}, u32[]{:S(2)}) copy-start(f32[1,96,2048]{2,1,0:T(8,128)} %refs_7_.1) | copy-start | bytes 2359300
  10.9 41.4 %copy-start.9 = (s32[128]{0:T(128)S(1)}, s32[128]{0:T(128)}, u32[]{:S(2)}) copy-start(s32[128]{0:T(128)} %param.23) | copy-start | bytes 1540
  10.9 41.5 %copy-start.10 = (s32[8]{0:T(128)S(1)}, s32[8]{0:T(128)}, u32[]{:S(2)}) copy-start(s32[8]{0:T(128)} %param.24) | copy-start | bytes 100
  10.9 10.1 %collective-permute-start.10 = (bf16[1,224,1024]{2,1,0:T(8,128)(2,1)S(1)}, bf16[1,224,1024]{2,1,0:T(8,128)(2,1)S(1)}, u32[]{:S(2)}, u32[]{:S(2)}) collective-permute-start(bf16[1,224,1024]{2,1,0:T(8,128)(2,1)S(1)} %add_convert_fusion.2), channel_id=1, source_target_pairs={{0,16},{8,56},{16,32},{24,8},{32,48},{40,24},{48,0},{56,40},{64,80... | collective-permute-start | bytes 1376264 | tf_op jit(solution)/shard_map/ppermute | solution.py:59
  15.0 2.9 %collective-permute-start.5 = (bf16[1,192,1024]{2,1,0:T(8,128)(2,1)S(1)}, bf16[1,192,1024]{2,1,0:T(8,128)(2,1)S(1)}, u32[]{:S(2)}, u32[]{:S(2)}) collective-permute-start(bf16[1,192,1024]{2,1,0:T(8,128)(2,1)S(1)} %get-tuple-element.55), channel_id=1, source_target_pairs={{0,8},{8,0},{16,24},{24,16},{32,40},{40,32},{48,56},{56,48},{64,72... | collective-permute-start | bytes 1179656 | tf_op jit(solution)/shard_map/ppermute | solution.py:49
  15.1 9.4 %collective-permute-start.8 = (bf16[1,224,1024]{2,1,0:T(8,128)(2,1)S(1)}, bf16[1,224,1024]{2,1,0:T(8,128)(2,1)S(1)}, u32[]{:S(2)}, u32[]{:S(2)}) collective-permute-start(bf16[1,224,1024]{2,1,0:T(8,128)(2,1)S(1)} %get-tuple-element.57), channel_id=1, source_target_pairs={{0,8},{8,0},{16,24},{24,16},{32,40},{40,32},{48,56},{56,48},{64,72... | collective-permute-start | bytes 1376264 | tf_op jit(solution)/shard_map/ppermute | solution.py:49
  15.6 16.7 %collective-permute-start.4 = (bf16[1,192,1024]{2,1,0:T(8,128)(2,1)S(1)}, bf16[1,192,1024]{2,1,0:T(8,128)(2,1)S(1)}, u32[]{:S(2)}, u32[]{:S(2)}) collective-permute-start(bf16[1,192,1024]{2,1,0:T(8,128)(2,1)S(1)} %get-tuple-element.53), channel_id=1, source_target_pairs={{0,8},{8,0},{16,24},{24,16},{32,40},{40,32},{48,56},{56,48},{64,72... | collective-permute-start | bytes 1179656 | tf_op jit(solution)/shard_map/ppermute | solution.py:49
  16.1 6.6 %collective-permute-start.1 = (bf16[1,192,1024]{2,1,0:T(8,128)(2,1)S(1)}, bf16[1,192,1024]{2,1,0:T(8,128)(2,1)S(1)}, u32[]{:S(2)}, u32[]{:S(2)}) collective-permute-start(bf16[1,192,1024]{2,1,0:T(8,128)(2,1)S(1)} %get-tuple-element.51), channel_id=1, source_target_pairs={{0,8},{8,0},{16,24},{24,16},{32,40},{40,32},{48,56},{56,48},{64,72... | collective-permute-start | bytes 1179656 | tf_op jit(solution)/shard_map/ppermute | solution.py:49
  17.9 8.0 %collective-permute-start.15 = (bf16[1,224,1024]{2,1,0:T(8,128)(2,1)S(1)}, bf16[1,224,1024]{2,1,0:T(8,128)(2,1)S(1)}, u32[]{:S(2)}, u32[]{:S(2)}) collective-permute-start(bf16[1,224,1024]{2,1,0:T(8,128)(2,1)S(1)} %add_convert_fusion), channel_id=1, source_target_pairs={{0,16},{8,56},{16,32},{24,8},{32,48},{40,24},{48,0},{56,40},{64,80... | collective-permute-start | bytes 1376264 | tf_op jit(solution)/shard_map/ppermute | solution.py:59
  21.0 8.0 %collective-permute-start.11 = (bf16[1,224,1024]{2,1,0:T(8,128)(2,1)S(1)}, bf16[1,224,1024]{2,1,0:T(8,128)(2,1)S(1)}, u32[]{:S(2)}, u32[]{:S(2)}) collective-permute-start(bf16[1,224,1024]{2,1,0:T(8,128)(2,1)S(1)} %collective-permute-done.10), channel_id=1, source_target_pairs={{0,8},{8,0},{16,24},{24,16},{32,40},{40,32},{48,56},{56,48},{64,72... | collective-permute-start | bytes 1376264 | tf_op jit(solution)/shard_map/ppermute | solution.py:49
  22.7 9.8 %collective-permute-start.6 = (bf16[1,192,1024]{2,1,0:T(8,128)(2,1)S(1)}, bf16[1,192,1024]{2,1,0:T(8,128)(2,1)S(1)}, u32[]{:S(2)}, u32[]{:S(2)}) collective-permute-start(bf16[1,192,1024]{2,1,0:T(8,128)(2,1)S(1)} %add_convert_fusion.4), channel_id=1, source_target_pairs={{0,16},{8,56},{16,32},{24,8},{32,48},{40,24},{48,0},{56,40},{64,80... | collective-permute-start | bytes 1179656 | tf_op jit(solution)/shard_map/ppermute | solution.py:59
  24.5 20.1 %collective-permute-start = (bf16[1,192,1024]{2,1,0:T(8,128)(2,1)S(1)}, bf16[1,192,1024]{2,1,0:T(8,128)(2,1)S(1)}, u32[]{:S(2)}, u32[]{:S(2)}) collective-permute-start(bf16[1,192,1024]{2,1,0:T(8,128)(2,1)S(1)} %get-tuple-element.49), channel_id=1, source_target_pairs={{0,8},{8,0},{16,24},{24,16},{32,40},{40,32},{48,56},{56,48},{64,72... | collective-permute-start | bytes 1179656 | tf_op jit(solution)/shard_map/ppermute | solution.py:49
  25.9 8.4 %collective-permute-start.2 = (bf16[1,192,1024]{2,1,0:T(8,128)(2,1)S(1)}, bf16[1,192,1024]{2,1,0:T(8,128)(2,1)S(1)}, u32[]{:S(2)}, u32[]{:S(2)}) collective-permute-start(bf16[1,192,1024]{2,1,0:T(8,128)(2,1)S(1)} %add_convert_fusion.5), channel_id=1, source_target_pairs={{0,16},{8,56},{16,32},{24,8},{32,48},{40,24},{48,0},{56,40},{64,80... | collective-permute-start | bytes 1179656 | tf_op jit(solution)/shard_map/ppermute | solution.py:59
  29.4 9.2 %collective-permute-start.16 = (bf16[1,112,1024]{2,1,0:T(8,128)(2,1)S(1)}, bf16[1,112,1024]{2,1,0:T(8,128)(2,1)S(1)}, u32[]{:S(2)}, u32[]{:S(2)}) collective-permute-start(bf16[1,112,1024]{2,1,0:T(8,128)(2,1)S(1)} %slice.10), channel_id=1, source_target_pairs={{0,64},{8,72},{16,80},{24,88},{32,96},{40,104},{48,112},{56,120},{... | collective-permute-start | bytes 688136 | tf_op jit(solution)/shard_map/ppermute | solution.py:49
  32.2 9.6 %collective-permute-start.17 = (bf16[1,96,1024]{2,1,0:T(8,128)(2,1)S(1)}, bf16[1,96,1024]{2,1,0:T(8,128)(2,1)S(1)}, u32[]{:S(2)}, u32[]{:S(2)}) collective-permute-start(bf16[1,96,1024]{2,1,0:T(8,128)(2,1)S(1)} %slice.11), channel_id=1, source_target_pairs={{0,64},{8,72},{16,80},{24,88},{32,96},{40,104},{48,112},{56,120},{... | collective-permute-start | bytes 589832 | tf_op jit(solution)/shard_map/ppermute | solution.py:49
  32.6 12.1 %collective-permute-start.7 = (bf16[1,192,1024]{2,1,0:T(8,128)(2,1)S(1)}, bf16[1,192,1024]{2,1,0:T(8,128)(2,1)S(1)}, u32[]{:S(2)}, u32[]{:S(2)}) collective-permute-start(bf16[1,192,1024]{2,1,0:T(8,128)(2,1)S(1)} %add_convert_fusion.3), channel_id=1, source_target_pairs={{0,16},{8,56},{16,32},{24,8},{32,48},{40,24},{48,0},{56,40},{64,80... | collective-permute-start | bytes 1179656 | tf_op jit(solution)/shard_map/ppermute | solution.py:59
  34.3 10.5 %collective-permute-start.3 = (bf16[1,192,1024]{2,1,0:T(8,128)(2,1)S(1)}, bf16[1,192,1024]{2,1,0:T(8,128)(2,1)S(1)}, u32[]{:S(2)}, u32[]{:S(2)}) collective-permute-start(bf16[1,192,1024]{2,1,0:T(8,128)(2,1)S(1)} %collective-permute-done.2), channel_id=1, source_target_pairs={{0,8},{8,0},{16,24},{24,16},{32,40},{40,32},{48,56},{56,48},{64,72... | collective-permute-start | bytes 1179656 | tf_op jit(solution)/shard_map/ppermute | solution.py:49
  41.8 5.4 %collective-permute-start.18 = (bf16[32,512]{1,0:T(8,128)(2,1)S(1)}, bf16[32,512]{1,0:T(8,128)(2,1)S(1)}, u32[]{:S(2)}, u32[]{:S(2)}) collective-permute-start(bf16[32,512]{1,0:T(8,128)(2,1)S(1)} %get-tuple-element.70), channel_id=1, source_target_pairs={{0,64},{8,72},{16,80},{24,88},{32,96},{40,104},{48,112},{56,120},{... | collective-permute-start | bytes 98312 | tf_op jit(solution)/shard_map/ppermute | solution.py:49
  47.2 12.5 %all-to-all-start = ((bf16[8,96,256]{2,1,0:T(8,128)(2,1)}), bf16[8,96,256]{2,1,0:T(8,128)(2,1)S(1)}, u32[]{:S(2)}, u32[]{:S(2)}) async-start(bf16[8,96,256]{2,1,0:T(8,128)(2,1)} %get-tuple-element.73), calls=%async_computation | async-start | bytes 786432 | tf_op jit(solution)/shard_map/all_to_all | solution.py:280
  52.4 3.2 %collective-permute-start.19 = (bf16[2,32,512]{2,1,0:T(8,128)(2,1)S(1)}, bf16[2,32,512]{2,1,0:T(8,128)(2,1)S(1)}, u32[]{:S(2)}, u32[]{:S(2)}) collective-permute-start(bf16[2,32,512]{2,1,0:T(8,128)(2,1)S(1)} %pad_maximum_fusion.2), channel_id=1, source_target_pairs={{0,48},{8,56},{16,0},{24,8},{32,16},{40,24},{48,32},{56,40},{64,11... | collective-permute-start | bytes 196616 | tf_op jit(solution)/shard_map/ppermute | solution.py:49
  52.5 4.7 %collective-permute-start.20 = (bf16[2,32,512]{2,1,0:T(8,128)(2,1)S(1)}, bf16[2,32,512]{2,1,0:T(8,128)(2,1)S(1)}, u32[]{:S(2)}, u32[]{:S(2)}) collective-permute-start(bf16[2,32,512]{2,1,0:T(8,128)(2,1)S(1)} %pad_maximum_fusion.2), channel_id=1, source_target_pairs={{0,32},{8,40},{16,48},{24,56},{32,0},{40,8},{48,16},{56,24},{64,96... | collective-permute-start | bytes 196616 | tf_op jit(solution)/shard_map/ppermute | solution.py:49
  52.6 5.7 %collective-permute-start.21 = (bf16[2,32,512]{2,1,0:T(8,128)(2,1)S(1)}, bf16[2,32,512]{2,1,0:T(8,128)(2,1)S(1)}, u32[]{:S(2)}, u32[]{:S(2)}) collective-permute-start(bf16[2,32,512]{2,1,0:T(8,128)(2,1)S(1)} %pad_maximum_fusion.2), channel_id=1, source_target_pairs={{0,16},{8,24},{16,32},{24,40},{32,48},{40,56},{48,0},{56,8},{64,80... | collective-permute-start | bytes 196616 | tf_op jit(solution)/shard_map/ppermute | solution.py:49
  59.8 3.6 %collective-permute-start.22 = (bf16[4,2,32,512]{3,2,1,0:T(8,128)(2,1)S(1)}, bf16[4,2,32,512]{3,2,1,0:T(8,128)(2,1)S(1)}, u32[]{:S(2)}, u32[]{:S(2)}) collective-permute-start(bf16[4,2,32,512]{3,2,1,0:T(8,128)(2,1)S(1)} %get-tuple-element.85), channel_id=1, source_target_pairs={{0,8},{8,0},{16,24},{24,16},{32,40},{40,32},{48,56},{56,48},{64,72... | collective-permute-start | bytes 786440 | tf_op jit(solution)/shard_map/ppermute | solution.py:49
  63.3 1.4 %copy-start.7 = (bf16[8,96,256]{2,1,0:T(8,128)(2,1)}, bf16[8,96,256]{2,1,0:T(8,128)(2,1)S(1)}, u32[]{:S(2)}) copy-start(bf16[8,96,256]{2,1,0:T(8,128)(2,1)S(1)} %scatter_fusion) | copy-start | bytes 1179652

commit v6 on v5

--- a/solution.py
+++ b/solution.py
@@ -237,19 +237,19 @@
     kp = pltpu.with_memory_space_constraint(key_partials.reshape(16, KROWS, KCOLS), pltpu.HBM)
 
     across = lambda values: [send(value, 0, 0, 1) for value in values]
-    casts, keeps = load(ep, kp, "turn", ["far", "plain"])
+    casts, keeps = load(ep, kp, "turn", ["far", "plain", "near"])
     got = across(casts)
-    casts_b, keeps_b = load(ep, kp, "turn", ["near", "own"], late=(casts[0],))
+    casts_b, keeps_b = load(ep, kp, "turn", ["own"], late=(casts[0],))
     got_b = across(casts_b)
     casts_c, keeps_c = load(ep, kp, "stay", ["far", "plain", "near", "own"], late=(casts_b[0],))
     got_c = across(casts_c)
     far = ring(plus(keeps[0], got[0]).astype(BF))
     plain = ring(plus(keeps[1], got[1]).astype(BF))
-    near = ring(plus(keeps_b[0], got_b[0], far).astype(BF))
+    near = ring(plus(keeps[2], got[2], far).astype(BF))
     cross = send(plain, 0, 0, 1)
     far_c = ring(plus(keeps_c[0], got_c[0]).astype(BF))
     plain_c = ring(plus(keeps_c[1], got_c[1]).astype(BF))
-    turned = plus(keeps_b[1], got_b[1], cross, near)
+    turned = plus(keeps_b[0], got_b[0], cross, near)
     x_late = send(turned[:, :ROWS].astype(BF), 1, 0, 0)
     x_last = send(turned[:, ROWS : FOLD + KFOLD].astype(BF), 1, 0, 0)
     near_c = ring(plus(keeps_c[2], got_c[2], far_c).astype(BF))

time: 65 us -> 65 us (level)
    ppermute x6, starting transfers between devices: 10.7 us -> 9.53 us  [ring(): return lax.ppermute(value, 'dp', pairs)]
    ppermute x17, starting transfers between devices: 17.9 us -> 18.8 us  [send(): return lax.ppermute(value, 'dp', dp_perm(dx, dy, dc))]
where the time goes in v6:
time: 65 us; the launch traced here: 64.8 us
  starting transfers between devices  33.4 us (51%)
  waiting for transfers between devices  13.9 us (21%)
  Pallas kernels  12.1 us (19%)
  other arithmetic  1.96 us (3%)
  matrix products  1.35 us (2%)
  local copies, waits for them, and re-layouts  1.07 us (2%)
  between operations  1.06 us (2%)
    ppermute x17, starting transfers between devices, send(): return lax.ppermute(value, 'dp', dp_perm(dx, dy, dc))  18.8 us
    ppermute x6, starting transfers between devices, ring(): return lax.ppermute(value, 'dp', pairs)  9.53 us
    pallas_call x3, Pallas kernels, load(): pl.pallas_call(functools.partial(load_kernel, batch, roles, len(late)), o...  8.93 us
    ppermute x17, waiting for transfers between devices, send(): return lax.ppermute(value, 'dp', dp_perm(dx, dy, dc))  8.65 us
    all_to_all x1, starting transfers between devices, on_device(): lax.all_to_all(blocks, 'expert', split_axis=0, concat_axis=0, tiled=True)  5.07 us
    ppermute x6, waiting for transfers between devices, ring(): return lax.ppermute(value, 'dp', pairs)  4.1 us
    pallas_call x2, Pallas kernels, update(): pl.pallas_call(kernel, out_shape=[jax.ShapeDtypeStruct(param.shape, F32)]...  3.14 us
    dot_general x1, matrix products, on_device(): lax.dot_general(everything, pick, (((0,), (0,)), ((), ())), preferred_ele...  1.35 us
  transfers between devices with their start and end apart: 24, of which 10 were waited for; matrix products, arithmetic and copies ran while one was open for 4% of the time, Pallas kernels for 14%

profile of v6, /device:TPU:1, one launch (start us, length us, event | category | flops | bytes accessed | tf_op | source)
XLA Modules:
  0.0 64.8 jit_solution(14407340296673911467)
XLA Ops:
  0.7 3.0 %shard_map.179 = (bf16[1,224,1024]{2,1,0:T(8,128)(2,1)S(1)}, bf16[1,224,1024]{2,1,0:T(8,128)(2,1)S(1)}, bf16[1,224,1024]{2,1,0:T(8,128)(2,1)S(1)}, bf16[1,224,10...) custom-call(f32[16,96,2048]{2,1,0:T(8,128)} %bitcast.15, ...), custom_call_target="tpu_custom_call" | custom-call | flops 1000 | bytes 1000 | tf_op jit(solution)/shard_map/pallas_call | solution.py:142
  3.7 1.5 %collective-permute-start.13 = (bf16[1,224,1024]{2,1,0:T(8,128)(2,1)S(1)}, bf16[1,224,1024]{2,1,0:T(8,128)(2,1)S(1)}, u32[]{:S(2)}, u32[]{:S(2)}) collective-permute-start(bf16[1,224,1024]{2,1,0:T(8,128)(2,1)S(1)} %get-tuple-element.46.refs_0_), channel_id=1, source_target_pairs={{0,8},{8,0},{16,24},{24,16},{32,40},{40,32},{48,56},{56,48},{64,72... | collective-permute-start | bytes 1376264 | tf_op jit(solution)/shard_map/ppermute | solution.py:49
  5.2 0.1 collective-permute-start.9
  5.2 0.4 collective-permute-start.12
  5.7 0.9 %collective-permute-done.13 = bf16[1,224,1024]{2,1,0:T(8,128)(2,1)S(1)} collective-permute-done((bf16[1,224,1024]{2,1,0:T(8,128)(2,1)S(1)}, bf16[1,224,1024]{2,1,0:T(8,128)(2,1)S(1)}, u32[]{:S(2)}, u32[]{:S(2)}) %collective-permute-start.13) | collective-permute-done | bytes 458784 | tf_op jit(solution)/shard_map/ppermute | solution.py:49
  6.6 0.2 add_convert_fusion.1
  6.8 2.9 %collective-permute-start.14 = (bf16[1,224,1024]{2,1,0:T(8,128)(2,1)S(1)}, bf16[1,224,1024]{2,1,0:T(8,128)(2,1)S(1)}, u32[]{:S(2)}, u32[]{:S(2)}) collective-permute-start(bf16[1,224,1024]{2,1,0:T(8,128)(2,1)S(1)} %add_convert_fusion.1), channel_id=1, source_target_pairs={{0,16},{8,56},{16,32},{24,8},{32,48},{40,24},{48,0},{56,40},{64,80... | collective-permute-start | bytes 1376264 | tf_op jit(solution)/shard_map/ppermute | solution.py:59
  9.7 0.2 add_convert_fusion.2
  9.8 0.5 collective-permute-start.10
  10.4 1.8 %shard_map.180 = (bf16[1,224,1024]{2,1,0:T(8,128)(2,1)S(1)}, bf16[1,224,1024]{2,1,0:T(8,128)(2,1)S(1)}) custom-call(f32[16,96,2048]{2,1,0:T(8,128)} %bitcast.16, f32[16,32,512]{2,1,0:T(8,128)} %bitcast.19, bf16[1,224,1024]{2,1,0:T(8,128)(2,1)S(1)} %get-tuple-element.46.refs_0_), custom_call_target="tpu_custom_call" | custom-call | flops 1000 | bytes 1000 | tf_op jit(solution)/shard_map/pallas_call | solution.py:142
  12.3 4.1 %shard_map.181 = (bf16[1,192,1024]{2,1,0:T(8,128)(2,1)S(1)}, bf16[1,192,1024]{2,1,0:T(8,128)(2,1)S(1)}, bf16[1,192,1024]{2,1,0:T(8,128)(2,1)S(1)}, bf16[1,192,10...) custom-call(f32[16,96,2048]{2,1,0:T(8,128)} %bitcast.17, ...), custom_call_target="tpu_custom_call" | custom-call | flops 1000 | bytes 1000 | tf_op jit(solution)/shard_map/pallas_call | solution.py:142
  16.4 0.4 collective-permute-start.5
  16.9 0.2 collective-permute-start.8
  17.0 0.3 collective-permute-start.4
  17.4 0.2 collective-permute-start.1
  17.6 0.2 add_convert_fusion
  17.8 0.5 collective-permute-done.5
  18.3 1.3 %collective-permute-start.15 = (bf16[1,224,1024]{2,1,0:T(8,128)(2,1)S(1)}, bf16[1,224,1024]{2,1,0:T(8,128)(2,1)S(1)}, u32[]{:S(2)}, u32[]{:S(2)}) collective-permute-start(bf16[1,224,1024]{2,1,0:T(8,128)(2,1)S(1)} %add_convert_fusion), channel_id=1, source_target_pairs={{0,16},{8,56},{16,32},{24,8},{32,48},{40,24},{48,0},{56,40},{64,80... | collective-permute-start | bytes 1376264 | tf_op jit(solution)/shard_map/ppermute | solution.py:59
  19.6 0.4 collective-permute-done.10
  20.0 1.8 %collective-permute-start.11 = (bf16[1,224,1024]{2,1,0:T(8,128)(2,1)S(1)}, bf16[1,224,1024]{2,1,0:T(8,128)(2,1)S(1)}, u32[]{:S(2)}, u32[]{:S(2)}) collective-permute-start(bf16[1,224,1024]{2,1,0:T(8,128)(2,1)S(1)} %collective-permute-done.10), channel_id=1, source_target_pairs={{0,8},{8,0},{16,24},{24,16},{32,40},{40,32},{48,56},{56,48},{64,72... | collective-permute-start | bytes 1376264 | tf_op jit(solution)/shard_map/ppermute | solution.py:49
  21.8 0.1 add_convert_fusion.4
  22.0 1.7 %collective-permute-start.6 = (bf16[1,192,1024]{2,1,0:T(8,128)(2,1)S(1)}, bf16[1,192,1024]{2,1,0:T(8,128)(2,1)S(1)}, u32[]{:S(2)}, u32[]{:S(2)}) collective-permute-start(bf16[1,192,1024]{2,1,0:T(8,128)(2,1)S(1)} %add_convert_fusion.4), channel_id=1, source_target_pairs={{0,16},{8,56},{16,32},{24,8},{32,48},{40,24},{48,0},{56,40},{64,80... | collective-permute-start | bytes 1179656 | tf_op jit(solution)/shard_map/ppermute | solution.py:59
  23.6 0.1 add_convert_fusion.5
  23.9 2.0 %collective-permute-done.15 = bf16[1,224,1024]{2,1,0:T(8,128)(2,1)S(1)} collective-permute-done((bf16[1,224,1024]{2,1,0:T(8,128)(2,1)S(1)}, bf16[1,224,1024]{2,1,0:T(8,128)(2,1)S(1)}, u32[]{:S(2)}, u32[]{:S(2)}) %collective-permute-start.15) | collective-permute-done | bytes 458784 | tf_op jit(solution)/shard_map/ppermute | solution.py:59
  25.9 2.3 %collective-permute-start.2 = (bf16[1,192,1024]{2,1,0:T(8,128)(2,1)S(1)}, bf16[1,192,1024]{2,1,0:T(8,128)(2,1)S(1)}, u32[]{:S(2)}, u32[]{:S(2)}) collective-permute-start(bf16[1,192,1024]{2,1,0:T(8,128)(2,1)S(1)} %add_convert_fusion.5), channel_id=1, source_target_pairs={{0,16},{8,56},{16,32},{24,8},{32,48},{40,24},{48,0},{56,40},{64,80... | collective-permute-start | bytes 1179656 | tf_op jit(solution)/shard_map/ppermute | solution.py:59
  28.1 0.3 fusion.30
  28.5 2.8 %collective-permute-start.16 = (bf16[1,112,1024]{2,1,0:T(8,128)(2,1)S(1)}, bf16[1,112,1024]{2,1,0:T(8,128)(2,1)S(1)}, u32[]{:S(2)}, u32[]{:S(2)}) collective-permute-start(bf16[1,112,1024]{2,1,0:T(8,128)(2,1)S(1)} %slice.10), channel_id=1, source_target_pairs={{0,64},{8,72},{16,80},{24,88},{32,96},{40,104},{48,112},{56,120},{... | collective-permute-start | bytes 688136 | tf_op jit(solution)/shard_map/ppermute | solution.py:49
  31.3 0.2 collective-permute-start.17
  31.6 0.2 add_convert_fusion.3
  31.8 0.8 %collective-permute-start.7 = (bf16[1,192,1024]{2,1,0:T(8,128)(2,1)S(1)}, bf16[1,192,1024]{2,1,0:T(8,128)(2,1)S(1)}, u32[]{:S(2)}, u32[]{:S(2)}) collective-permute-start(bf16[1,192,1024]{2,1,0:T(8,128)(2,1)S(1)} %add_convert_fusion.3), channel_id=1, source_target_pairs={{0,16},{8,56},{16,32},{24,8},{32,48},{40,24},{48,0},{56,40},{64,80... | collective-permute-start | bytes 1179656 | tf_op jit(solution)/shard_map/ppermute | solution.py:59
  32.6 1.7 %collective-permute-done.2 = bf16[1,192,1024]{2,1,0:T(8,128)(2,1)S(1)} collective-permute-done((bf16[1,192,1024]{2,1,0:T(8,128)(2,1)S(1)}, bf16[1,192,1024]{2,1,0:T(8,128)(2,1)S(1)}, u32[]{:S(2)}, u32[]{:S(2)}) %collective-permute-start.2) | collective-permute-done | bytes 393248 | tf_op jit(solution)/shard_map/ppermute | solution.py:59
  34.3 3.0 %collective-permute-start.3 = (bf16[1,192,1024]{2,1,0:T(8,128)(2,1)S(1)}, bf16[1,192,1024]{2,1,0:T(8,128)(2,1)S(1)}, u32[]{:S(2)}, u32[]{:S(2)}) collective-permute-start(bf16[1,192,1024]{2,1,0:T(8,128)(2,1)S(1)} %collective-permute-done.2), channel_id=1, source_target_pairs={{0,8},{8,0},{16,24},{24,16},{32,40},{40,32},{48,56},{56,48},{64,72... | collective-permute-start | bytes 1179656 | tf_op jit(solution)/shard_map/ppermute | solution.py:49
  37.3 0.7 %shard_map.182 = (f32[32,512]{1,0:T(8,128)}, f32[32,512]{1,0:T(8,128)}, f32[32,512]{1,0:T(8,128)}, bf16[32,512]{1,0:T(8,128)(2,1)S(1)}) custom-call(f32[1,224,1024]{2,1,0:T(8,128)S(1)} %get-tuple-element.83.own, bf16[1,112,1024]{2,1,0:T(8,128)(2,1)S(1)} %collective-permute-done.16.arrived.refs_4_, f32[32,512]{1,0:T(8,128)S(1)} %copy-done.3, ...), custom_call_target="tpu_custom_call" | custom-call | flops 1000 | bytes 1000 | tf_op jit(solution)/shard_map/pallas_call | solution.py:209
  38.1 3.2 %collective-permute-done.17.refs_3_ = bf16[1,96,1024]{2,1,0:T(8,128)(2,1)S(1)} collective-permute-done((bf16[1,96,1024]{2,1,0:T(8,128)(2,1)S(1)}, bf16[1,96,1024]{2,1,0:T(8,128)(2,1)S(1)}, u32[]{:S(2)}, u32[]{:S(2)}) %collective-permute-start.17) | collective-permute-done | bytes 196640 | tf_op jit(solution)/shard_map/ppermute | solution.py:49
  41.3 2.7 %collective-permute-start.18 = (bf16[32,512]{1,0:T(8,128)(2,1)S(1)}, bf16[32,512]{1,0:T(8,128)(2,1)S(1)}, u32[]{:S(2)}, u32[]{:S(2)}) collective-permute-start(bf16[32,512]{1,0:T(8,128)(2,1)S(1)} %get-tuple-element.70), channel_id=1, source_target_pairs={{0,64},{8,72},{16,80},{24,88},{32,96},{40,104},{48,112},{56,120},{... | collective-permute-start | bytes 98312 | tf_op jit(solution)/shard_map/ppermute | solution.py:49
  44.0 0.1 add_convert_fusion.6.refs_0_
  44.2 2.4 %shard_map.183 = (f32[1,96,2048]{2,1,0:T(8,128)}, f32[1,96,2048]{2,1,0:T(8,128)}, f32[1,96,2048]{2,1,0:T(8,128)}, bf16[8,96,256]{2,1,0:T(8,128)(2,1)}) custom-call(bf16[1,192,1024]{2,1,0:T(8,128)(2,1)S(1)} %add_convert_fusion.6.refs_0_, bf16[1,192,1024]{2,1,0:T(8,128)(2,1)S(1)} %collective-permute-done.3.refs_1_, ...), custom_call_target="tpu_custom_call" | custom-call | flops 1000 | bytes 1000 | tf_op jit(solution)/shard_map/pallas_call | solution.py:209
  46.6 5.1 %all-to-all-start = ((bf16[8,96,256]{2,1,0:T(8,128)(2,1)}), bf16[8,96,256]{2,1,0:T(8,128)(2,1)S(1)}, u32[]{:S(2)}, u32[]{:S(2)}) async-start(bf16[8,96,256]{2,1,0:T(8,128)(2,1)} %get-tuple-element.73), calls=%async_computation | async-start | bytes 786432 | tf_op jit(solution)/shard_map/all_to_all | solution.py:280
  51.7 0.1 select_reduce_fusion.1
  52.0 1.4 %collective-permute-start.21 = (bf16[2,32,512]{2,1,0:T(8,128)(2,1)S(1)}, bf16[2,32,512]{2,1,0:T(8,128)(2,1)S(1)}, u32[]{:S(2)}, u32[]{:S(2)}) collective-permute-start(bf16[2,32,512]{2,1,0:T(8,128)(2,1)S(1)} %pad_maximum_fusion.2), channel_id=1, source_target_pairs={{0,16},{8,24},{16,32},{24,40},{32,48},{40,56},{48,0},{56,8},{64,80... | collective-permute-start | bytes 196616 | tf_op jit(solution)/shard_map/ppermute | solution.py:49
  53.4 1.6 %collective-permute-done.19 = bf16[2,32,512]{2,1,0:T(8,128)(2,1)S(1)} collective-permute-done((bf16[2,32,512]{2,1,0:T(8,128)(2,1)S(1)}, bf16[2,32,512]{2,1,0:T(8,128)(2,1)S(1)}, u32[]{:S(2)}, u32[]{:S(2)}) %collective-permute-start.19) | collective-permute-done | bytes 65568 | tf_op jit(solution)/shard_map/ppermute | solution.py:49
  55.0 1.6 %collective-permute-done.20 = bf16[2,32,512]{2,1,0:T(8,128)(2,1)S(1)} collective-permute-done((bf16[2,32,512]{2,1,0:T(8,128)(2,1)S(1)}, bf16[2,32,512]{2,1,0:T(8,128)(2,1)S(1)}, u32[]{:S(2)}, u32[]{:S(2)}) %collective-permute-start.20) | collective-permute-done | bytes 65568 | tf_op jit(solution)/shard_map/ppermute | solution.py:49
  56.6 0.8 %collective-permute-done.21 = bf16[2,32,512]{2,1,0:T(8,128)(2,1)S(1)} collective-permute-done((bf16[2,32,512]{2,1,0:T(8,128)(2,1)S(1)}, bf16[2,32,512]{2,1,0:T(8,128)(2,1)S(1)}, u32[]{:S(2)}, u32[]{:S(2)}) %collective-permute-start.21) | collective-permute-done | bytes 65568 | tf_op jit(solution)/shard_map/ppermute | solution.py:49
  57.4 1.2 %all-to-all-done = bf16[8,96,256]{2,1,0:T(8,128)(2,1)S(1)} async-done(((bf16[8,96,256]{2,1,0:T(8,128)(2,1)}), bf16[8,96,256]{2,1,0:T(8,128)(2,1)S(1)}, u32[]{:S(2)}, u32[]{:S(2)}) %all-to-all-start) | async-done | bytes 393248 | tf_op jit(solution)/shard_map/all_to_all | solution.py:280
  58.6 3.5 %collective-permute-start.22 = (bf16[4,2,32,512]{3,2,1,0:T(8,128)(2,1)S(1)}, bf16[4,2,32,512]{3,2,1,0:T(8,128)(2,1)S(1)}, u32[]{:S(2)}, u32[]{:S(2)}) collective-permute-start(bf16[4,2,32,512]{3,2,1,0:T(8,128)(2,1)S(1)} %get-tuple-element.85), channel_id=1, source_target_pairs={{0,8},{8,0},{16,24},{24,16},{32,40},{40,32},{48,56},{56,48},{64,72... | collective-permute-start | bytes 786440 | tf_op jit(solution)/shard_map/ppermute | solution.py:49
  62.1 0.2 select_reduce_fusion
  62.4 0.9 %scatter_fusion = bf16[8,96,256]{2,1,0:T(8,128)(2,1)S(1)} fusion(bf16[8,96,256]{2,1,0:T(8,128)(2,1)S(1)} %broadcast_in_dim.38, s32[8]{0:T(128)S(1)} %compare_select_fusion, bf16[8,96,256]{2,1,0:T(8,128)(2,1)S(1)} %all-to-all-done), kind=kCustom, calls=%fused_computation | custom fusion | bytes 1179680 | tf_op jit(solution)/shard_map/scatter | solution.py:297
  63.4 1.3 %convolution_convert_fusion = bf16[512,512]{1,0:T(8,128)(2,1)} fusion(bf16[512,512]{1,0:T(8,128)(2,1)S(1)} %bitcast.22, s32[512]{0:T(512)S(1)} %fusion.20), kind=kOutput, calls=%fused_computation.1 | convolution fusion | flops 268959744 | bytes 1050624 | tf_op jit(solution)/shard_map/dot_general | solution.py:294
  (49 shorter events, 0.6 us)
Async XLA Ops:
  3.7 2.9 %collective-permute-start.13 = (bf16[1,224,1024]{2,1,0:T(8,128)(2,1)S(1)}, bf16[1,224,1024]{2,1,0:T(8,128)(2,1)S(1)}, u32[]{:S(2)}, u32[]{:S(2)}) collective-permute-start(bf16[1,224,1024]{2,1,0:T(8,128)(2,1)S(1)} %get-tuple-element.46.refs_0_), channel_id=1, source_target_pairs={{0,8},{8,0},{16,24},{24,16},{32,40},{40,32},{48,56},{56,48},{64,72... | collective-permute-start | bytes 1376264 | tf_op jit(solution)/shard_map/ppermute | solution.py:49
  5.2 4.5 %collective-permute-start.9 = (bf16[1,224,1024]{2,1,0:T(8,128)(2,1)S(1)}, bf16[1,224,1024]{2,1,0:T(8,128)(2,1)S(1)}, u32[]{:S(2)}, u32[]{:S(2)}) collective-permute-start(bf16[1,224,1024]{2,1,0:T(8,128)(2,1)S(1)} %get-tuple-element.58), channel_id=1, source_target_pairs={{0,8},{8,0},{16,24},{24,16},{32,40},{40,32},{48,56},{56,48},{64,72... | collective-permute-start | bytes 1376264 | tf_op jit(solution)/shard_map/ppermute | solution.py:49
  5.2 11.8 %collective-permute-start.12 = (bf16[1,224,1024]{2,1,0:T(8,128)(2,1)S(1)}, bf16[1,224,1024]{2,1,0:T(8,128)(2,1)S(1)}, u32[]{:S(2)}, u32[]{:S(2)}) collective-permute-start(bf16[1,224,1024]{2,1,0:T(8,128)(2,1)S(1)} %get-tuple-element.60), channel_id=1, source_target_pairs={{0,8},{8,0},{16,24},{24,16},{32,40},{40,32},{48,56},{56,48},{64,72... | collective-permute-start | bytes 1376264 | tf_op jit(solution)/shard_map/ppermute | solution.py:49
  6.8 10.6 %collective-permute-start.14 = (bf16[1,224,1024]{2,1,0:T(8,128)(2,1)S(1)}, bf16[1,224,1024]{2,1,0:T(8,128)(2,1)S(1)}, u32[]{:S(2)}, u32[]{:S(2)}) collective-permute-start(bf16[1,224,1024]{2,1,0:T(8,128)(2,1)S(1)} %add_convert_fusion.1), channel_id=1, source_target_pairs={{0,16},{8,56},{16,32},{24,8},{32,48},{40,24},{48,0},{56,40},{64,80... | collective-permute-start | bytes 1376264 | tf_op jit(solution)/shard_map/ppermute | solution.py:59
  9.8 10.2 %collective-permute-start.10 = (bf16[1,224,1024]{2,1,0:T(8,128)(2,1)S(1)}, bf16[1,224,1024]{2,1,0:T(8,128)(2,1)S(1)}, u32[]{:S(2)}, u32[]{:S(2)}) collective-permute-start(bf16[1,224,1024]{2,1,0:T(8,128)(2,1)S(1)} %add_convert_fusion.2), channel_id=1, source_target_pairs={{0,16},{8,56},{16,32},{24,8},{32,48},{40,24},{48,0},{56,40},{64,80... | collective-permute-start | bytes 1376264 | tf_op jit(solution)/shard_map/ppermute | solution.py:59
  12.2 25.1 %copy-start.8 = (f32[8,12,16]{2,0,1:T(8,128)S(1)}, f32[8,12,16]{2,0,1:T(8,128)}, u32[]{:S(2)}) copy-start(f32[8,12,16]{2,0,1:T(8,128)} %param.21) | copy-start | bytes 18436
  12.2 25.1 %copy-start.3 = (f32[32,512]{1,0:T(8,128)S(1)}, f32[32,512]{1,0:T(8,128)}, u32[]{:S(2)}) copy-start(f32[32,512]{1,0:T(8,128)} %param.25) | copy-start | bytes 196612
  12.2 25.1 %copy-start.4 = (f32[32,512]{1,0:T(8,128)S(1)}, f32[32,512]{1,0:T(8,128)}, u32[]{:S(2)}) copy-start(f32[32,512]{1,0:T(8,128)} %moment.1) | copy-start | bytes 196612
  12.2 25.1 %copy-start.5 = (f32[32,512]{1,0:T(8,128)S(1)}, f32[32,512]{1,0:T(8,128)}, u32[]{:S(2)}) copy-start(f32[32,512]{1,0:T(8,128)} %variance.1) | copy-start | bytes 196612
  12.2 25.1 %copy-start.6 = (f32[4,4]{1,0:T(4,128)S(1)}, f32[4,4]{1,0:T(4,128)}, u32[]{:S(2)}) copy-start(f32[4,4]{1,0:T(4,128)} %scales.1) | copy-start | bytes 196
  12.3 32.0 %copy-start = (f32[1,96,2048]{2,1,0:T(8,128)S(1)}, f32[1,96,2048]{2,1,0:T(8,128)}, u32[]{:S(2)}) copy-start(f32[1,96,2048]{2,1,0:T(8,128)} %refs_5_.1) | copy-start | bytes 2359300
  12.3 32.0 %copy-start.1 = (f32[1,96,2048]{2,1,0:T(8,128)S(1)}, f32[1,96,2048]{2,1,0:T(8,128)}, u32[]{:S(2)}) copy-start(f32[1,96,2048]{2,1,0:T(8,128)} %refs_6_.1) | copy-start | bytes 2359300
  12.3 32.0 %copy-start.2 = (f32[1,96,2048]{2,1,0:T(8,128)S(1)}, f32[1,96,2048]{2,1,0:T(8,128)}, u32[]{:S(2)}) copy-start(f32[1,96,2048]{2,1,0:T(8,128)} %refs_7_.1) | copy-start | bytes 2359300
  12.3 39.4 %copy-start.9 = (s32[128]{0:T(128)S(1)}, s32[128]{0:T(128)}, u32[]{:S(2)}) copy-start(s32[128]{0:T(128)} %param.23) | copy-start | bytes 1540
  12.3 39.5 %copy-start.10 = (s32[8]{0:T(128)S(1)}, s32[8]{0:T(128)}, u32[]{:S(2)}) copy-start(s32[8]{0:T(128)} %param.24) | copy-start | bytes 100
  16.4 1.8 %collective-permute-start.5 = (bf16[1,192,1024]{2,1,0:T(8,128)(2,1)S(1)}, bf16[1,192,1024]{2,1,0:T(8,128)(2,1)S(1)}, u32[]{:S(2)}, u32[]{:S(2)}) collective-permute-start(bf16[1,192,1024]{2,1,0:T(8,128)(2,1)S(1)} %get-tuple-element.55), channel_id=1, source_target_pairs={{0,8},{8,0},{16,24},{24,16},{32,40},{40,32},{48,56},{56,48},{64,72... | collective-permute-start | bytes 1179656 | tf_op jit(solution)/shard_map/ppermute | solution.py:49
  16.9 6.9 %collective-permute-start.8 = (bf16[1,224,1024]{2,1,0:T(8,128)(2,1)S(1)}, bf16[1,224,1024]{2,1,0:T(8,128)(2,1)S(1)}, u32[]{:S(2)}, u32[]{:S(2)}) collective-permute-start(bf16[1,224,1024]{2,1,0:T(8,128)(2,1)S(1)} %get-tuple-element.47.refs_0_), channel_id=1, source_target_pairs={{0,8},{8,0},{16,24},{24,16},{32,40},{40,32},{48,56},{56,48},{64,72... | collective-permute-start | bytes 1376264 | tf_op jit(solution)/shard_map/ppermute | solution.py:49
  17.0 14.3 %collective-permute-start.4 = (bf16[1,192,1024]{2,1,0:T(8,128)(2,1)S(1)}, bf16[1,192,1024]{2,1,0:T(8,128)(2,1)S(1)}, u32[]{:S(2)}, u32[]{:S(2)}) collective-permute-start(bf16[1,192,1024]{2,1,0:T(8,128)(2,1)S(1)} %get-tuple-element.53), channel_id=1, source_target_pairs={{0,8},{8,0},{16,24},{24,16},{32,40},{40,32},{48,56},{56,48},{64,72... | collective-permute-start | bytes 1179656 | tf_op jit(solution)/shard_map/ppermute | solution.py:49
  17.4 4.6 %collective-permute-start.1 = (bf16[1,192,1024]{2,1,0:T(8,128)(2,1)S(1)}, bf16[1,192,1024]{2,1,0:T(8,128)(2,1)S(1)}, u32[]{:S(2)}, u32[]{:S(2)}) collective-permute-start(bf16[1,192,1024]{2,1,0:T(8,128)(2,1)S(1)} %get-tuple-element.51), channel_id=1, source_target_pairs={{0,8},{8,0},{16,24},{24,16},{32,40},{40,32},{48,56},{56,48},{64,72... | collective-permute-start | bytes 1179656 | tf_op jit(solution)/shard_map/ppermute | solution.py:49
  18.3 7.6 %collective-permute-start.15 = (bf16[1,224,1024]{2,1,0:T(8,128)(2,1)S(1)}, bf16[1,224,1024]{2,1,0:T(8,128)(2,1)S(1)}, u32[]{:S(2)}, u32[]{:S(2)}) collective-permute-start(bf16[1,224,1024]{2,1,0:T(8,128)(2,1)S(1)} %add_convert_fusion), channel_id=1, source_target_pairs={{0,16},{8,56},{16,32},{24,8},{32,48},{40,24},{48,0},{56,40},{64,80... | collective-permute-start | bytes 1376264 | tf_op jit(solution)/shard_map/ppermute | solution.py:59
  20.0 8.1 %collective-permute-start.11 = (bf16[1,224,1024]{2,1,0:T(8,128)(2,1)S(1)}, bf16[1,224,1024]{2,1,0:T(8,128)(2,1)S(1)}, u32[]{:S(2)}, u32[]{:S(2)}) collective-permute-start(bf16[1,224,1024]{2,1,0:T(8,128)(2,1)S(1)} %collective-permute-done.10), channel_id=1, source_target_pairs={{0,8},{8,0},{16,24},{24,16},{32,40},{40,32},{48,56},{56,48},{64,72... | collective-permute-start | bytes 1376264 | tf_op jit(solution)/shard_map/ppermute | solution.py:49
  22.0 9.6 %collective-permute-start.6 = (bf16[1,192,1024]{2,1,0:T(8,128)(2,1)S(1)}, bf16[1,192,1024]{2,1,0:T(8,128)(2,1)S(1)}, u32[]{:S(2)}, u32[]{:S(2)}) collective-permute-start(bf16[1,192,1024]{2,1,0:T(8,128)(2,1)S(1)} %add_convert_fusion.4), channel_id=1, source_target_pairs={{0,16},{8,56},{16,32},{24,8},{32,48},{40,24},{48,0},{56,40},{64,80... | collective-permute-start | bytes 1179656 | tf_op jit(solution)/shard_map/ppermute | solution.py:59
  23.8 20.3 %collective-permute-start = (bf16[1,192,1024]{2,1,0:T(8,128)(2,1)S(1)}, bf16[1,192,1024]{2,1,0:T(8,128)(2,1)S(1)}, u32[]{:S(2)}, u32[]{:S(2)}) collective-permute-start(bf16[1,192,1024]{2,1,0:T(8,128)(2,1)S(1)} %get-tuple-element.49), channel_id=1, source_target_pairs={{0,8},{8,0},{16,24},{24,16},{32,40},{40,32},{48,56},{56,48},{64,72... | collective-permute-start | bytes 1179656 | tf_op jit(solution)/shard_map/ppermute | solution.py:49
  25.9 8.4 %collective-permute-start.2 = (bf16[1,192,1024]{2,1,0:T(8,128)(2,1)S(1)}, bf16[1,192,1024]{2,1,0:T(8,128)(2,1)S(1)}, u32[]{:S(2)}, u32[]{:S(2)}) collective-permute-start(bf16[1,192,1024]{2,1,0:T(8,128)(2,1)S(1)} %add_convert_fusion.5), channel_id=1, source_target_pairs={{0,16},{8,56},{16,32},{24,8},{32,48},{40,24},{48,0},{56,40},{64,80... | collective-permute-start | bytes 1179656 | tf_op jit(solution)/shard_map/ppermute | solution.py:59
  28.5 8.8 %collective-permute-start.16 = (bf16[1,112,1024]{2,1,0:T(8,128)(2,1)S(1)}, bf16[1,112,1024]{2,1,0:T(8,128)(2,1)S(1)}, u32[]{:S(2)}, u32[]{:S(2)}) collective-permute-start(bf16[1,112,1024]{2,1,0:T(8,128)(2,1)S(1)} %slice.10), channel_id=1, source_target_pairs={{0,64},{8,72},{16,80},{24,88},{32,96},{40,104},{48,112},{56,120},{... | collective-permute-start | bytes 688136 | tf_op jit(solution)/shard_map/ppermute | solution.py:49
  31.3 10.0 %collective-permute-start.17 = (bf16[1,96,1024]{2,1,0:T(8,128)(2,1)S(1)}, bf16[1,96,1024]{2,1,0:T(8,128)(2,1)S(1)}, u32[]{:S(2)}, u32[]{:S(2)}) collective-permute-start(bf16[1,96,1024]{2,1,0:T(8,128)(2,1)S(1)} %slice.11), channel_id=1, source_target_pairs={{0,64},{8,72},{16,80},{24,88},{32,96},{40,104},{48,112},{56,120},{... | collective-permute-start | bytes 589832 | tf_op jit(solution)/shard_map/ppermute | solution.py:49
  31.8 12.4 %collective-permute-start.7 = (bf16[1,192,1024]{2,1,0:T(8,128)(2,1)S(1)}, bf16[1,192,1024]{2,1,0:T(8,128)(2,1)S(1)}, u32[]{:S(2)}, u32[]{:S(2)}) collective-permute-start(bf16[1,192,1024]{2,1,0:T(8,128)(2,1)S(1)} %add_convert_fusion.3), channel_id=1, source_target_pairs={{0,16},{8,56},{16,32},{24,8},{32,48},{40,24},{48,0},{56,40},{64,80... | collective-permute-start | bytes 1179656 | tf_op jit(solution)/shard_map/ppermute | solution.py:59
  34.3 9.9 %collective-permute-start.3 = (bf16[1,192,1024]{2,1,0:T(8,128)(2,1)S(1)}, bf16[1,192,1024]{2,1,0:T(8,128)(2,1)S(1)}, u32[]{:S(2)}, u32[]{:S(2)}) collective-permute-start(bf16[1,192,1024]{2,1,0:T(8,128)(2,1)S(1)} %collective-permute-done.2), channel_id=1, source_target_pairs={{0,8},{8,0},{16,24},{24,16},{32,40},{40,32},{48,56},{56,48},{64,72... | collective-permute-start | bytes 1179656 | tf_op jit(solution)/shard_map/ppermute | solution.py:49
  41.3 5.3 %collective-permute-start.18 = (bf16[32,512]{1,0:T(8,128)(2,1)S(1)}, bf16[32,512]{1,0:T(8,128)(2,1)S(1)}, u32[]{:S(2)}, u32[]{:S(2)}) collective-permute-start(bf16[32,512]{1,0:T(8,128)(2,1)S(1)} %get-tuple-element.70), channel_id=1, source_target_pairs={{0,64},{8,72},{16,80},{24,88},{32,96},{40,104},{48,112},{56,120},{... | collective-permute-start | bytes 98312 | tf_op jit(solution)/shard_map/ppermute | solution.py:49
  46.6 11.9 %all-to-all-start = ((bf16[8,96,256]{2,1,0:T(8,128)(2,1)}), bf16[8,96,256]{2,1,0:T(8,128)(2,1)S(1)}, u32[]{:S(2)}, u32[]{:S(2)}) async-start(bf16[8,96,256]{2,1,0:T(8,128)(2,1)} %get-tuple-element.73), calls=%async_computation | async-start | bytes 786432 | tf_op jit(solution)/shard_map/all_to_all | solution.py:280
  51.8 3.2 %collective-permute-start.19 = (bf16[2,32,512]{2,1,0:T(8,128)(2,1)S(1)}, bf16[2,32,512]{2,1,0:T(8,128)(2,1)S(1)}, u32[]{:S(2)}, u32[]{:S(2)}) collective-permute-start(bf16[2,32,512]{2,1,0:T(8,128)(2,1)S(1)} %pad_maximum_fusion.2), channel_id=1, source_target_pairs={{0,48},{8,56},{16,0},{24,8},{32,16},{40,24},{48,32},{56,40},{64,11... | collective-permute-start | bytes 196616 | tf_op jit(solution)/shard_map/ppermute | solution.py:49
  51.9 4.7 %collective-permute-start.20 = (bf16[2,32,512]{2,1,0:T(8,128)(2,1)S(1)}, bf16[2,32,512]{2,1,0:T(8,128)(2,1)S(1)}, u32[]{:S(2)}, u32[]{:S(2)}) collective-permute-start(bf16[2,32,512]{2,1,0:T(8,128)(2,1)S(1)} %pad_maximum_fusion.2), channel_id=1, source_target_pairs={{0,32},{8,40},{16,48},{24,56},{32,0},{40,8},{48,16},{56,24},{64,96... | collective-permute-start | bytes 196616 | tf_op jit(solution)/shard_map/ppermute | solution.py:49
  52.0 5.4 %collective-permute-start.21 = (bf16[2,32,512]{2,1,0:T(8,128)(2,1)S(1)}, bf16[2,32,512]{2,1,0:T(8,128)(2,1)S(1)}, u32[]{:S(2)}, u32[]{:S(2)}) collective-permute-start(bf16[2,32,512]{2,1,0:T(8,128)(2,1)S(1)} %pad_maximum_fusion.2), channel_id=1, source_target_pairs={{0,16},{8,24},{16,32},{24,40},{32,48},{40,56},{48,0},{56,8},{64,80... | collective-permute-start | bytes 196616 | tf_op jit(solution)/shard_map/ppermute | solution.py:49
  58.6 4.8 %collective-permute-start.22 = (bf16[4,2,32,512]{3,2,1,0:T(8,128)(2,1)S(1)}, bf16[4,2,32,512]{3,2,1,0:T(8,128)(2,1)S(1)}, u32[]{:S(2)}, u32[]{:S(2)}) collective-permute-start(bf16[4,2,32,512]{3,2,1,0:T(8,128)(2,1)S(1)} %get-tuple-element.85), channel_id=1, source_target_pairs={{0,8},{8,0},{16,24},{24,16},{32,40},{40,32},{48,56},{56,48},{64,72... | collective-permute-start | bytes 786440 | tf_op jit(solution)/shard_map/ppermute | solution.py:49
  63.4 1.4 %copy-start.7 = (bf16[8,96,256]{2,1,0:T(8,128)(2,1)}, bf16[8,96,256]{2,1,0:T(8,128)(2,1)S(1)}, u32[]{:S(2)}) copy-start(bf16[8,96,256]{2,1,0:T(8,128)(2,1)S(1)} %scatter_fusion) | copy-start | bytes 1179652
